TPU v7x, 1024 devices: a whole 4x4x32 slice. The times are simulated.
1024 devices in a mesh: expert: 32 (over y, x, core), dp: 32 (over z).
Axes of the slice: x: 4, y: 4, z: 32, core: 2. Of those that a mesh axis runs over, the one named last changes fastest.
Arguments:
- grad_out: bfloat16 [1024, 7168], P('expert', 'dp'), may hold values from -6 to 6
- expert_ids: int32 [1024, 8], P('expert'), may hold values from 0 to 31, all different within a row; in each aligned block of 32 rows (0 to 31, 32 to 63, ...) at most 12 rows name the same one
- gate_weights: float32 [1024, 8], P('expert'), may hold values from 0.05 to 0.5
- layer_inputs: bfloat16 [1024, 7168], P('expert', 'dp'), may hold values from -6 to 6
- shared_pre: bfloat16 [1024, 2048], P('expert'), may hold values from -6 to 6
- routed_inputs: bfloat16 [32, 384, 7168], P('expert', None, 'dp'), may hold values from -6 to 6
- routed_pre: bfloat16 [32, 384, 2048], P('expert'), may hold values from -6 to 6
- w_gate_up: bfloat16 [32, 7168, 2048], P('expert', 'dp'), may hold values from -0.125 to 0.125
- w_down: bfloat16 [32, 1024, 7168], P('expert', None, 'dp'), may hold values from -0.0625 to 0.0625
- shared_gate_up: bfloat16 [7168, 2048], P('dp'), may hold values from -0.125 to 0.125
- shared_down: bfloat16 [1024, 7168], P(None, 'dp'), may hold values from -0.0625 to 0.0625
Outputs:
- grad_in: bfloat16 [1024, 7168], P('expert', 'dp')
- grad_gate_up: bfloat16 [32, 7168, 2048], P('expert', 'dp')
- grad_down: bfloat16 [32, 1024, 7168], P('expert', None, 'dp')
- shared_grad_gate_up: bfloat16 [7168, 2048], P('dp', 'expert')
- shared_grad_down: bfloat16 [1024, 7168], P('expert', 'dp')
Inputs may be any that keep to these rules, and one draw needn't show every extreme that they name: `expert_ids`: among the 32 tokens of one block, each expert is named by at most 12 of them, a bound that some block reaches; a token names 8 different experts.
All inputs are finite; a program needn't handle non-finite values.
Results may differ from a plain program's by a relative error of at most 0.0057.
Values may be sent and summed in bfloat16 or wider, within the bound.
No kernel may reach another device: no remote copies, remote signals or barrier semaphores. Data moves between devices by JAX's collectives and lax.ppermute only.
A program may use at most 32 MiB of HBM per device.

v0:
```python
import jax
import jax.numpy as jnp
from jax import lax
from jax.sharding import PartitionSpec as P


def pre_halves(saved_pre, share_start, share_width):
    half_width = saved_pre.shape[-1] // 2
    last_axis = saved_pre.ndim - 1
    gate_pre = lax.dynamic_slice_in_dim(saved_pre, share_start, share_width, last_axis)
    up_pre = lax.dynamic_slice_in_dim(saved_pre, half_width + share_start, share_width, last_axis)
    return (gate_pre.astype(jnp.float32), up_pre.astype(jnp.float32))


def hidden_grads(saved_pre, grad_hidden, share_start):
    gate_pre, up_pre = pre_halves(saved_pre, share_start, grad_hidden.shape[-1])
    sigmoid_gate = jax.nn.sigmoid(gate_pre)
    activated = gate_pre * sigmoid_gate
    grad_gate = grad_hidden * up_pre * sigmoid_gate * (1.0 + gate_pre * (1.0 - sigmoid_gate))
    return (grad_gate, grad_hidden * activated)


def gated_hidden(saved_pre):
    half_width = saved_pre.shape[-1] // 2
    gate_pre, up_pre = pre_halves(saved_pre, 0, half_width)
    return (gate_pre * jax.nn.sigmoid(gate_pre) * up_pre).astype(jnp.bfloat16)


def on_device(
    grad_out,
    expert_ids,
    gate_weights,
    layer_inputs,
    shared_pre,
    routed_inputs,
    routed_pre,
    w_gate_up,
    w_down,
    shared_gate_up,
    shared_down,
):
    groups = lax.axis_size("expert")
    local_count = w_down.shape[0]
    slot_count = routed_pre.shape[1]
    capacity = slot_count // groups
    token_count, route_count = expert_ids.shape
    features = grad_out.shape[1]
    flat_ids = expert_ids.reshape(token_count * route_count)
    onehot = (
        flat_ids[:, None] == jnp.arange(local_count * groups, dtype=jnp.int32)[None, :]
    ).astype(jnp.int32)
    before = jnp.cumsum(onehot, axis=0) - onehot
    slot_rank = jnp.sum(before * onehot, axis=1)
    position = flat_ids % local_count * slot_count + flat_ids // local_count * capacity + slot_rank
    route_table = (
        position[:, None] == jnp.arange(local_count * slot_count, dtype=jnp.int32)[None, :]
    ).astype(jnp.bfloat16)
    scaled = (gate_weights[:, :, None] * grad_out[:, None, :].astype(jnp.float32)).astype(
        jnp.bfloat16
    )
    outgoing = jnp.einsum(
        "rs,rd->sd",
        route_table,
        scaled.reshape(token_count * route_count, features),
        preferred_element_type=jnp.float32,
    ).astype(jnp.bfloat16)
    arrived = lax.all_to_all(
        outgoing.reshape(local_count, groups, capacity, features),
        "expert",
        split_axis=1,
        concat_axis=1,
        tiled=True,
    )
    arrived = arrived.reshape(local_count, slot_count, features)
    routed_part = jnp.einsum("lsd,lhd->lsh", arrived, w_down, preferred_element_type=jnp.float32)
    shared_part = jnp.einsum("td,hd->th", grad_out, shared_down, preferred_element_type=jnp.float32)
    routed_grad, shared_grad = lax.psum((routed_part, shared_part), "dp")
    routed_gate, routed_up = hidden_grads(routed_pre, routed_grad, 0)
    shared_gate, shared_up = hidden_grads(shared_pre, shared_grad, 0)
    routed_pre_grad = jnp.concatenate([routed_gate, routed_up], axis=2).astype(jnp.bfloat16)
    shared_pre_grad = jnp.concatenate([shared_gate, shared_up], axis=1).astype(jnp.bfloat16)
    hidden = gated_hidden(routed_pre)
    shared_hidden = gated_hidden(shared_pre)
    grad_gate_up = jnp.einsum(
        "lsd,lsk->ldk", routed_inputs, routed_pre_grad, preferred_element_type=jnp.float32
    ).astype(jnp.bfloat16)
    grad_down = jnp.einsum(
        "lsh,lsd->lhd", hidden, arrived, preferred_element_type=jnp.float32
    ).astype(jnp.bfloat16)
    returned = jnp.einsum(
        "lsk,ldk->lsd", routed_pre_grad, w_gate_up, preferred_element_type=jnp.float32
    ).astype(jnp.bfloat16)
    came_back = lax.all_to_all(
        returned.reshape(local_count, groups, capacity, features),
        "expert",
        split_axis=1,
        concat_axis=1,
        tiled=True,
    )
    token_table = jnp.sum(
        route_table.reshape(token_count, route_count, local_count * slot_count), axis=1
    )
    routed_sum = jnp.dot(
        token_table,
        came_back.reshape(local_count * slot_count, features),
        preferred_element_type=jnp.float32,
    )
    shared_back = jnp.einsum(
        "tk,dk->td", shared_pre_grad, shared_gate_up, preferred_element_type=jnp.float32
    )
    grad_in = (shared_back + routed_sum).astype(jnp.bfloat16)
    shared_gu_part = jnp.einsum(
        "td,tk->dk", layer_inputs, shared_pre_grad, preferred_element_type=jnp.float32
    )
    shared_down_part = jnp.einsum(
        "th,td->hd", shared_hidden, grad_out, preferred_element_type=jnp.float32
    )
    shared_gu_sum, shared_down_sum = (
        lax.psum_scatter(shared_gu_part, "expert", scatter_dimension=1, tiled=True),
        lax.psum_scatter(shared_down_part, "expert", scatter_dimension=0, tiled=True),
    )
    return (
        grad_in,
        grad_gate_up,
        grad_down,
        shared_gu_sum.astype(jnp.bfloat16),
        shared_down_sum.astype(jnp.bfloat16),
    )


def solution(mesh):
    in_specs = (
        P("expert", "dp"),
        P("expert", None),
        P("expert", None),
        P("expert", "dp"),
        P("expert", None),
        P("expert", None, "dp"),
        P("expert", None, None),
        P("expert", "dp", None),
        P("expert", None, "dp"),
        P("dp", None),
        P(None, "dp"),
    )
    out_specs = (
        P("expert", "dp"),
        P("expert", "dp", None),
        P("expert", None, "dp"),
        P("dp", "expert"),
        P("expert", "dp"),
    )
    return jax.shard_map(
        on_device, mesh=mesh, in_specs=in_specs, out_specs=out_specs, check_vma=False
    )
```

profile of v0, /device:TPU:1, one launch (start us, length us, event | category | flops | bytes accessed | tf_op | source)
XLA Modules:
  0.0 439.1 jit_solution(4182671655336109137)
XLA Ops:
  8.0 0.9 copy.36
  9.1 0.6 reduce-window.6
  9.7 0.2 slice_reduce_fusion
  10.1 0.7 convert_element_type.85
  10.8 0.8 copy.40
  11.6 0.4 convolution_convert_fusion.3
  12.2 0.8 reshape.108
  12.9 17.7 %all-to-all-start = ((bf16[1,32,12,224]{3,2,0,1:T(8,128)(2,1)}), bf16[1,32,12,224]{3,2,0,1:T(8,128)(2,1)S(1)}, u32[]{:S(2)}, u32[]{:S(2)}) async-start(bf16[1,32,12,224]{3,2,0,1:T(8,128)(2,1)} %bitcast.2), calls=%async_computation | async-start | bytes 524288 | tf_op jit(solution)/shard_map/all_to_all | solution.py:67
  30.7 0.8 fusion.48
  31.5 8.1 %all-to-all-done = bf16[1,32,12,224]{3,2,0,1:T(8,128)(2,1)S(1)} async-done(((bf16[1,32,12,224]{3,2,0,1:T(8,128)(2,1)}), bf16[1,32,12,224]{3,2,0,1:T(8,128)(2,1)S(1)}, u32[]{:S(2)}, u32[]{:S(2)}) %all-to-all-start) | async-done | bytes 172064 | tf_op jit(solution)/shard_map/all_to_all | solution.py:67
  39.7 1.5 convolution_bitcast_fusion.1
  41.4 1.3 fusion.35
  42.8 241.9 %all-reduce.3.cloned.1.call-done = (f32[32,1024]{1,0:T(8,128)}, f32[1,384,1024]{2,1,0:T(8,128)}) async-done(((f32[32,1024]{1,0:T(8,128)}, f32[1,384,1024]{2,1,0:T(8,128)}), (f32[32,1024]{1,0:T(8,128)}, f32[1,384,1024]{2,1,0:T(8,128)})) %all-reduce.3.cloned.1.call-update) | async-done | bytes 1703952 | tf_op jit(solution)/shard_map/psum | solution.py:77
  284.6 1.0 fusion.25
  285.6 0.4 convolution_bitcast_fusion
  286.1 1.8 copy.46
  288.0 0.2 fusion.20
  288.2 1.1 copy-done.1
  289.3 1.5 fusion.9
  290.8 1.4 convert_element_type.100
  292.2 2.2 fusion.15
  294.4 0.9 copy-done.3
  295.3 0.7 convolution_convert_fusion.2
  296.2 0.8 reshape.112
  297.0 27.7 %all-to-all-start.1 = ((bf16[1,32,12,224]{3,2,0,1:T(8,128)(2,1)}), bf16[1,32,12,224]{3,2,0,1:T(8,128)(2,1)S(1)}, u32[]{:S(2)}, u32[]{:S(2)}) async-start(bf16[1,32,12,224]{3,2,0,1:T(8,128)(2,1)} %bitcast.8), calls=%async_computation.1 | async-start | bytes 524288 | tf_op jit(solution)/shard_map/all_to_all | solution.py:93
  324.7 0.4 fusion.34
  325.1 2.7 fusion
  327.8 5.8 %all-to-all-done.1 = bf16[1,32,12,224]{3,2,0,1:T(8,128)(2,1)S(1)} async-done(((bf16[1,32,12,224]{3,2,0,1:T(8,128)(2,1)}), bf16[1,32,12,224]{3,2,0,1:T(8,128)(2,1)S(1)}, u32[]{:S(2)}, u32[]{:S(2)}) %all-to-all-start.1) | async-done | bytes 172064 | tf_op jit(solution)/shard_map/all_to_all | solution.py:93
  333.6 0.8 fusion.10
  334.4 95.6 %reduce-scatter.7.cloned.1.call-done = f32[64,224]{1,0:T(8,128)} async-done(((f32[2048,224]{1,0:T(8,128)}), f32[64,224]{1,0:T(8,128)}) %reduce-scatter.7.cloned.1.call-update) | async-done | bytes 57360
  430.0 0.9 copy.47
  431.0 0.7 copy.45
  (39 shorter events, 1.2 us)
Async XLA Ops:
  8.0 287.3 %copy-start = (bf16[1,224,2048]{2,1,0:T(8,128)(2,1)S(1)}, bf16[1,224,2048]{2,1,0:T(8,128)(2,1)}, u32[]{:S(2)}) copy-start(bf16[1,224,2048]{2,1,0:T(8,128)(2,1)} %param.18) | copy-start | bytes 2752516
  8.0 22.6 %copy-start.7 = (bf16[32,224]{1,0:T(8,128)(2,1)S(1)}, bf16[32,224]{1,0:T(8,128)(2,1)}, u32[]{:S(2)}) copy-start(bf16[32,224]{1,0:T(8,128)(2,1)} %param.11) | copy-start | bytes 43012
  8.0 22.6 %copy-start.4 = (bf16[1024,224]{0,1:T(8,128)(2,1)S(1)}, bf16[1024,224]{0,1:T(8,128)(2,1)}, u32[]{:S(2)}) copy-start(bf16[1024,224]{0,1:T(8,128)(2,1)} %param.21) | copy-start | bytes 1376260
  8.0 31.7 %copy-start.5 = (bf16[1,1024,224]{1,2,0:T(8,128)(2,1)S(1)}, bf16[1,1024,224]{1,2,0:T(8,128)(2,1)}, u32[]{:S(2)}) copy-start(bf16[1,1024,224]{1,2,0:T(8,128)(2,1)} %param.19) | copy-start | bytes 1376260
  12.9 26.7 %all-to-all-start = ((bf16[1,32,12,224]{3,2,0,1:T(8,128)(2,1)}), bf16[1,32,12,224]{3,2,0,1:T(8,128)(2,1)S(1)}, u32[]{:S(2)}, u32[]{:S(2)}) async-start(bf16[1,32,12,224]{3,2,0,1:T(8,128)(2,1)} %bitcast.2), calls=%async_computation | async-start | bytes 524288 | tf_op jit(solution)/shard_map/all_to_all | solution.py:67
  30.6 254.0 %all-reduce.3.cloned.1.call-start = ((), (), s32[]{:S(2)}) async-start(), calls=%async_computation.6 | async-start | bytes 3407872 | tf_op jit(solution)/shard_map/psum | solution.py:77
  39.7 1.6 copy-start.6
  41.3 244.3 %copy-start.8 = (bf16[32,224]{1,0:T(8,128)(2,1)S(1)}, bf16[32,224]{1,0:T(8,128)(2,1)}, u32[]{:S(2)}) copy-start(bf16[32,224]{1,0:T(8,128)(2,1)} %param.14) | copy-start | bytes 43012
  41.3 249.5 %reduce-scatter.5.cloned.1.call-start = ((), (), s32[]{:S(2)}) async-start(), calls=%async_computation.4 | async-start | bytes 1081344 | tf_op jit(solution)/shard_map/reduce_scatter | solution.py:120
  42.7 387.3 %reduce-scatter.7.cloned.1.call-start = ((), (), s32[]{:S(2)}) async-start(), calls=%async_computation.5 | async-start | bytes 2162688
  287.9 1.4 copy-start.1
  294.4 0.9 copy-start.3
  295.3 29.4 %copy-start.2 = (bf16[224,2048]{1,0:T(8,128)(2,1)S(1)}, bf16[224,2048]{1,0:T(8,128)(2,1)}, u32[]{:S(2)}) copy-start(bf16[224,2048]{1,0:T(8,128)(2,1)} %param.20) | copy-start | bytes 2752516
  296.0 29.1 %copy-start.9 = (bf16[1,384,224]{1,2,0:T(8,128)(2,1)S(1)}, bf16[1,384,224]{1,2,0:T(8,128)(2,1)}, u32[]{:S(2)}) copy-start(bf16[1,384,224]{1,2,0:T(8,128)(2,1)} %param.16) | copy-start | bytes 516100
  297.0 36.6 %all-to-all-start.1 = ((bf16[1,32,12,224]{3,2,0,1:T(8,128)(2,1)}), bf16[1,32,12,224]{3,2,0,1:T(8,128)(2,1)S(1)}, u32[]{:S(2)}, u32[]{:S(2)}) async-start(bf16[1,32,12,224]{3,2,0,1:T(8,128)(2,1)} %bitcast.8), calls=%async_computation.1 | async-start | bytes 524288 | tf_op jit(solution)/shard_map/all_to_all | solution.py:93
Sparse Core Ops, SparseCore 0:
  41.4 243.1 all-reduce.2
Sparse Core Ops, SparseCore 1:
  48.2 124.3 reduce-scatter.4
  288.0 142.0 reduce-scatter.6
where the time goes:
time: 441 us; the launch traced here: 439 us
  waiting for transfers between devices  351 us (80%)
  starting transfers between devices  45.5 us (10%)
  between operations  15.7 us (4%)
  matrix products  10.5 us (2%)
  local copies, waits for them, and re-layouts  9.75 us (2%)
  other arithmetic  6.2 us (1%)
    psum x1, waiting for transfers between devices, on_device(): routed_grad, shared_grad = lax.psum((routed_part, shared_part), 'dp')  242 us
    unnamed x4, waiting for transfers between devices  95.7 us
    all_to_all x1, starting transfers between devices, on_device(): lax.all_to_all(returned.reshape(local_count, groups, capacity, features),...  27.7 us
    all_to_all x1, starting transfers between devices, on_device(): lax.all_to_all(outgoing.reshape(local_count, groups, capacity, features),...  17.7 us
  transfers between devices with their start and end apart: 5, of which 4 were waited for; matrix products, arithmetic and copies ran while one was open for 4% of the time, Pallas kernels for 0%

commit v1 on v0

v1 whole, which is shorter than its diff:
```python
import jax
import jax.numpy as jnp
from jax import lax
from jax.experimental import pallas as pl
from jax.experimental.pallas import tpu as pltpu
from jax.sharding import PartitionSpec as P

NEAR = 4


def route_kernel(capacity, ids_ref, gates_ref, grad_ref, sel_ref, out_ref):
    slots, tokens = sel_ref.shape
    slot = lax.broadcasted_iota(jnp.int32, (slots, 1), 0)
    expert = slot // capacity
    place = (slot - expert * capacity).astype(jnp.float32)
    ids = ids_ref[...]
    gates = gates_ref[...]
    hit = jnp.zeros((slots, tokens), jnp.float32)
    weight = jnp.zeros((slots, tokens), jnp.float32)
    for k in range(ids.shape[0]):
        same = ids[k : k + 1, :] == expert
        hit = jnp.where(same, 1.0, hit)
        weight = jnp.where(same, gates[k : k + 1, :], weight)
    row = lax.broadcasted_iota(jnp.int32, (tokens, tokens), 0)
    col = lax.broadcasted_iota(jnp.int32, (tokens, tokens), 1)
    earlier = jnp.where(row < col, 1.0, 0.0).astype(jnp.bfloat16)
    rank = jnp.dot(hit.astype(jnp.bfloat16), earlier, preferred_element_type=jnp.float32)
    taken = (hit > 0.0) & (rank == place)
    sel = jnp.where(taken, 1.0, 0.0).astype(jnp.bfloat16)
    gate = jnp.sum(jnp.where(taken, weight, 0.0), axis=1, keepdims=True)
    rows = jnp.dot(sel, grad_ref[...], preferred_element_type=jnp.float32)
    sel_ref[...] = sel
    out_ref[...] = (gate * rows).astype(jnp.bfloat16)


def swiglu_back(saved_pre, grad_hidden):
    half = saved_pre.shape[-1] // 2
    gate = saved_pre[:, :half].astype(jnp.float32)
    up = saved_pre[:, half:].astype(jnp.float32)
    sig = jax.nn.sigmoid(gate)
    act = gate * sig
    d_gate = grad_hidden * up * sig * (1.0 + gate * (1.0 - sig))
    d_up = grad_hidden * act
    grad_pre = jnp.concatenate([d_gate, d_up], axis=1).astype(jnp.bfloat16)
    return grad_pre, (act * up).astype(jnp.bfloat16)


def dot(a, b, ca, cb):
    return lax.dot_general(a, b, (((ca,), (cb,)), ((), ())), preferred_element_type=jnp.float32)


def total(parts):
    acc = parts[0].astype(jnp.float32)
    for i in range(1, parts.shape[0]):
        acc = acc + parts[i].astype(jnp.float32)
    return acc.astype(jnp.bfloat16)


def on_device(
    grad_out,
    expert_ids,
    gate_weights,
    layer_inputs,
    shared_pre,
    routed_inputs,
    routed_pre,
    w_gate_up,
    w_down,
    shared_gate_up,
    shared_down,
):
    groups = lax.axis_size("expert")
    ring = lax.axis_size("dp")
    far = ring // NEAR
    near_groups = [[NEAR * a + b for b in range(NEAR)] for a in range(far)]
    far_groups = [[NEAR * a + b for a in range(far)] for b in range(NEAR)]
    slots = routed_pre.shape[1]
    capacity = slots // groups
    tokens, width = grad_out.shape
    hidden_width = w_down.shape[1]
    routed_pre, routed_inputs = routed_pre[0], routed_inputs[0]
    w_gate_up, w_down = w_gate_up[0], w_down[0]

    pad = jnp.zeros((tokens, 512 - 2 * width), jnp.bfloat16)
    everyone = lax.all_gather(
        jnp.concatenate([grad_out, layer_inputs, pad], axis=1), "expert", axis=0, tiled=True
    )

    sel, outgoing = pl.pallas_call(
        lambda *refs: route_kernel(capacity, *refs),
        out_shape=(
            jax.ShapeDtypeStruct((slots, tokens), jnp.bfloat16),
            jax.ShapeDtypeStruct((slots, width), jnp.bfloat16),
        ),
        name="route",
    )(expert_ids.T, gate_weights.T, grad_out)
    arrived = lax.all_to_all(
        outgoing.reshape(groups, capacity, width), "expert", split_axis=0, concat_axis=0, tiled=True
    ).reshape(slots, width)

    part = jnp.concatenate(
        [dot(arrived, w_down, 1, 1), dot(grad_out, shared_down, 1, 1)], axis=0
    ).astype(jnp.bfloat16)
    rows = (slots + tokens) // NEAR
    cols = hidden_width // far
    near = lax.all_to_all(
        part.reshape(NEAR, rows, hidden_width),
        "dp",
        split_axis=0,
        concat_axis=0,
        tiled=True,
        axis_index_groups=near_groups,
    )
    near = total(near)
    near = near.reshape(rows, far, cols).transpose(1, 0, 2)
    distant = lax.all_to_all(
        near,
        "dp",
        split_axis=0,
        concat_axis=0,
        tiled=True,
        axis_index_groups=far_groups,
    )
    own = total(distant)
    full = lax.all_gather(own, "dp", axis=0, tiled=False)
    full = full.reshape(far, NEAR, rows, cols).transpose(1, 2, 0, 3)
    full = full.reshape(slots + tokens, hidden_width).astype(jnp.float32)

    routed_grad, hidden = swiglu_back(routed_pre, full[:slots])
    shared_grad, shared_hidden = swiglu_back(shared_pre, full[slots:])

    lanes = 128
    returned = dot(routed_grad, w_gate_up, 1, 1).astype(jnp.bfloat16)
    low = returned[:, :lanes].reshape(groups, capacity, lanes)
    high = jnp.pad(returned[:, lanes:], ((0, 0), (0, 2 * lanes - width)))
    high = high.reshape(groups, capacity, lanes)
    gu_cols = 2 * hidden_width // groups
    down_cols = hidden_width // groups
    shared_cols = jnp.concatenate(
        [
            shared_grad.reshape(tokens, groups, gu_cols).transpose(1, 0, 2),
            shared_hidden.reshape(tokens, groups, down_cols).transpose(1, 0, 2),
            jnp.zeros((groups, tokens, lanes - gu_cols - down_cols), jnp.bfloat16),
        ],
        axis=2,
    )
    back = lax.all_to_all(
        jnp.concatenate([shared_cols, low, high], axis=1),
        "expert",
        split_axis=0,
        concat_axis=0,
        tiled=True,
    )

    grad_down = dot(hidden, arrived, 0, 0).astype(jnp.bfloat16)
    grad_gate_up = dot(routed_inputs, routed_grad, 0, 0).astype(jnp.bfloat16)
    shared_back = dot(shared_grad, shared_gate_up, 1, 1)

    came_low = back[:, tokens : tokens + capacity].reshape(slots, lanes)
    came_high = back[:, tokens + capacity :].reshape(slots, lanes)
    came_back = jnp.concatenate([came_low, came_high[:, : width - lanes]], axis=1)
    grad_in = (shared_back + dot(sel, came_back, 0, 0)).astype(jnp.bfloat16)
    all_shared = back[:, :tokens].reshape(groups * tokens, lanes)
    shared_gu = dot(all_shared[:, :gu_cols], everyone[:, width : 2 * width], 0, 0)
    shared_dn = dot(all_shared[:, gu_cols : gu_cols + down_cols], everyone[:, :width], 0, 0)
    return (
        grad_in,
        grad_gate_up[None],
        grad_down[None],
        shared_gu.astype(jnp.bfloat16).T,
        shared_dn.astype(jnp.bfloat16),
    )


def solution(mesh):
    in_specs = (
        P("expert", "dp"),
        P("expert", None),
        P("expert", None),
        P("expert", "dp"),
        P("expert", None),
        P("expert", None, "dp"),
        P("expert", None, None),
        P("expert", "dp", None),
        P("expert", None, "dp"),
        P("dp", None),
        P(None, "dp"),
    )
    out_specs = (
        P("expert", "dp"),
        P("expert", "dp", None),
        P("expert", None, "dp"),
        P("dp", "expert"),
        P("expert", "dp"),
    )
    return jax.shard_map(
        on_device, mesh=mesh, in_specs=in_specs, out_specs=out_specs, check_vma=False
    )
```

time: 441 us -> 221 us (0.50)
  waiting for transfers between devices: 351 us -> 40.7 us
  blocking collectives: 0 us -> 74.9 us
  starting transfers between devices: 45.5 us -> 56.9 us
  local copies, waits for them, and re-layouts: 9.75 us -> 15.4 us
    psum x1 -> x0, waiting for transfers between devices: 242 us -> none  [on_device(): routed_grad, shared_grad = lax.psum((routed_part, shared_part), 'dp')]
    unnamed x4 -> x1, waiting for transfers between devices: 95.7 us -> 0.02 us
    all_gather x0 -> x1, blocking collectives: none -> 51.1 us  [on_device(): full = lax.all_gather(own, 'dp', axis=0, tiled=False)]
    all_to_all x2 -> x3, waiting for transfers between devices: 13.9 us -> 40.7 us  [the longest x1 24.1 us: on_device(): lax.all_to_all(near, 'dp', split_axis=0, concat_axis=0, tiled=True, axis_...]
    all_to_all x0 -> x1, blocking collectives: none -> 23.8 us  [on_device(): lax.all_to_all(part.reshape(NEAR, rows, hidden_width), 'dp', split_axis=0...]
    all_to_all x2 -> x3, starting transfers between devices: 45.4 us -> 56.8 us  [the longest x1 20.5 us: on_device(): lax.all_to_all(jnp.concatenate([shared_cols, low, high], axis=1), 'expert...]
    unnamed x25, local copies, waits for them, and re-layouts: 7.2 us -> 2.64 us
    dot_general x10 -> x9, matrix products: 10.5 us -> 10.7 us  [dot(): lax.dot_general(a, b, (((ca,), (cb,)), ((), ())), preferred_element_type=...]
  transfers between devices with their start and end apart: 5 -> 4, of which waited for: 4 -> 3; matrix products, arithmetic and copies ran while one was open for 4% -> 10% of each run, Pallas kernels for 0% -> 0%
where the time goes in v1:
time: 221 us; the launch traced here: 220 us
  blocking collectives  74.9 us (34%)
  starting transfers between devices  56.9 us (26%)
  waiting for transfers between devices  40.7 us (18%)
  local copies, waits for them, and re-layouts  15.4 us (7%)
  between operations  14.3 us (6%)
  matrix products  10.7 us (5%)
  other arithmetic  4.75 us (2%)
    all_gather x1, blocking collectives, on_device(): full = lax.all_gather(own, 'dp', axis=0, tiled=False)  51.1 us
    all_to_all x1, waiting for transfers between devices, on_device(): lax.all_to_all(near, 'dp', split_axis=0, concat_axis=0, tiled=True, axis_...  24.1 us
    all_to_all x1, blocking collectives, on_device(): lax.all_to_all(part.reshape(NEAR, rows, hidden_width), 'dp', split_axis=0...  23.8 us
    all_to_all x1, starting transfers between devices, on_device(): lax.all_to_all(jnp.concatenate([shared_cols, low, high], axis=1), 'expert...  20.5 us
    all_to_all x1, starting transfers between devices, on_device(): lax.all_to_all(near, 'dp', split_axis=0, concat_axis=0, tiled=True, axis_...  18.7 us
    all_to_all x1, starting transfers between devices, on_device(): lax.all_to_all(outgoing.reshape(groups, capacity, width), 'expert', split...  17.7 us
    dot_general x9, matrix products, dot(): lax.dot_general(a, b, (((ca,), (cb,)), ((), ())), preferred_element_type=...  10.7 us
    all_to_all x1, waiting for transfers between devices, on_device(): lax.all_to_all(jnp.concatenate([shared_cols, low, high], axis=1), 'expert...  8.86 us
  transfers between devices with their start and end apart: 4, of which 3 were waited for; matrix products, arithmetic and copies ran while one was open for 10% of the time, Pallas kernels for 0%

profile of v1, /device:TPU:1, one launch (start us, length us, event | category | flops | bytes accessed | tf_op | source)
XLA Modules:
  0.0 219.7 jit_solution(11431467756478045187)
XLA Ops:
  7.2 2.0 route.1
  9.1 1.7 reshape.61
  10.8 17.7 %all-to-all-start = ((bf16[32,12,224]{2,1,0:T(8,128)(2,1)}), bf16[32,12,224]{2,1,0:T(8,128)(2,1)S(1)}, u32[]{:S(2)}, u32[]{:S(2)}) async-start(bf16[32,12,224]{2,1,0:T(8,128)(2,1)} %reshape.61), calls=%async_computation | async-start | bytes 524288 | tf_op jit(solution)/shard_map/all_to_all | solution.py:97
  28.5 1.2 convolution_convert_fusion.4
  29.7 7.8 %all-to-all-done = bf16[32,12,224]{2,1,0:T(8,128)(2,1)S(1)} async-done(((bf16[32,12,224]{2,1,0:T(8,128)(2,1)}), bf16[32,12,224]{2,1,0:T(8,128)(2,1)S(1)}, u32[]{:S(2)}, u32[]{:S(2)}) %all-to-all-start) | async-done | bytes 172064 | tf_op jit(solution)/shard_map/all_to_all | solution.py:97
  38.1 23.8 %all_to_all.20 = bf16[4,104,1024]{2,1,0:T(8,128)(2,1)S(1)} all-to-all(bf16[4,104,1024]{2,1,0:T(8,128)(2,1)S(1)} %bitcast.49), channel_id=1, replica_groups={{0,1,2,3},{4,5,6,7},{8,9,10,11},{12,13,14,15},{16,17,18,19},{20,21,22,2..., dimensions={0} | all-to-all | bytes 1703936 | tf_op jit(solution)/shard_map/all_to_all | solution.py:106
  62.1 0.7 copy.29
  62.8 18.7 %all-to-all-start.2 = ((bf16[8,104,128]{2,1,0:T(8,128)(2,1)}), bf16[8,104,128]{2,1,0:T(8,128)(2,1)S(1)}, u32[]{:S(2)}, u32[]{:S(2)}) async-start(bf16[8,104,128]{2,1,0:T(8,128)(2,1)} %copy.29), calls=%async_computation.2 | async-start | bytes 425984 | tf_op jit(solution)/shard_map/all_to_all | solution.py:116
  81.6 0.7 maximum_maximum_fusion
  82.4 1.5 fusion.9
  83.9 24.1 %all-to-all-done.2 = bf16[8,104,128]{2,1,0:T(8,128)(2,1)S(1)} async-done(((bf16[8,104,128]{2,1,0:T(8,128)(2,1)}), bf16[8,104,128]{2,1,0:T(8,128)(2,1)S(1)}, u32[]{:S(2)}, u32[]{:S(2)}) %all-to-all-start.2) | async-done | bytes 213024 | tf_op jit(solution)/shard_map/all_to_all | solution.py:116
  108.0 51.1 %all_gather.7 = bf16[32,104,128]{2,1,0:T(8,128)(2,1)S(1)} all-gather(bf16[1,104,128]{2,1,0:T(8,128)(2,1)S(1)} %add_convert_fusion.1), channel_id=1, replica_groups=mesh['expert'=32,'dp'=32] {'dp'}, dimensions={0}, use_global_device_ids=true | all-gather | bytes 878592 | tf_op jit(solution)/shard_map/all_gather | solution.py:125
  159.3 1.0 copy.30
  160.6 1.0 copy-done.2
  161.7 0.9 fusion.3
  162.6 0.7 convolution_convert_fusion.3
  164.7 1.0 copy.36
  166.4 0.9 reshape.65
  167.3 0.7 copy.34
  168.0 1.6 copy.31
  169.6 0.9 reshape.64
  170.5 0.7 copy.33
  171.2 1.6 fusion.26
  172.8 1.1 reshape.63
  174.2 1.2 pad_maximum_fusion.4
  175.4 1.0 copy.35
  176.4 20.5 %all-to-all-start.3 = ((bf16[32,56,128]{2,1,0:T(8,128)(2,1)}), bf16[32,56,128]{2,1,0:T(8,128)(2,1)S(1)}, u32[]{:S(2)}, u32[]{:S(2)}) async-start(bf16[32,56,128]{2,1,0:T(8,128)(2,1)} %copy.35), calls=%async_computation.3 | async-start | bytes 917504 | tf_op jit(solution)/shard_map/all_to_all | solution.py:147
  196.9 1.6 fusion
  198.9 8.9 %all-to-all-done.3 = bf16[32,56,128]{2,1,0:T(8,128)(2,1)S(1)} async-done(((bf16[32,56,128]{2,1,0:T(8,128)(2,1)}), bf16[32,56,128]{2,1,0:T(8,128)(2,1)S(1)}, u32[]{:S(2)}, u32[]{:S(2)}) %all-to-all-start.3) | async-done | bytes 458784 | tf_op jit(solution)/shard_map/all_to_all | solution.py:147
  207.9 0.8 fusion.10
  208.7 2.2 convolution_convert_fusion.5
  210.9 2.0 convolution_convert_fusion.6
  (47 shorter events, 4.4 us)
Async XLA Ops:
  7.2 155.4 %copy-start = (bf16[1,224,2048]{2,1,0:T(8,128)(2,1)S(1)}, bf16[1,224,2048]{2,1,0:T(8,128)(2,1)}, u32[]{:S(2)}) copy-start(bf16[1,224,2048]{2,1,0:T(8,128)(2,1)} %param.18) | copy-start | bytes 2752516
  7.2 30.4 %copy-start.6 = (bf16[1,1024,224]{1,2,0:T(8,128)(2,1)S(1)}, bf16[1,1024,224]{1,2,0:T(8,128)(2,1)}, u32[]{:S(2)}) copy-start(bf16[1,1024,224]{1,2,0:T(8,128)(2,1)} %param.19) | copy-start | bytes 1376260
  10.8 26.7 %all-to-all-start = ((bf16[32,12,224]{2,1,0:T(8,128)(2,1)}), bf16[32,12,224]{2,1,0:T(8,128)(2,1)S(1)}, u32[]{:S(2)}, u32[]{:S(2)}) async-start(bf16[32,12,224]{2,1,0:T(8,128)(2,1)} %reshape.61), calls=%async_computation | async-start | bytes 524288 | tf_op jit(solution)/shard_map/all_to_all | solution.py:97
  61.9 19.7 %copy-start.7 = (bf16[32,224]{1,0:T(8,128)(2,1)S(1)}, bf16[32,224]{1,0:T(8,128)(2,1)}, u32[]{:S(2)}) copy-start(bf16[32,224]{1,0:T(8,128)(2,1)} %refs_2_.1) | copy-start | bytes 43012
  61.9 19.7 %copy-start.8 = (bf16[32,224]{1,0:T(8,128)(2,1)S(1)}, bf16[32,224]{1,0:T(8,128)(2,1)}, u32[]{:S(2)}) copy-start(bf16[32,224]{1,0:T(8,128)(2,1)} %param.14) | copy-start | bytes 43012
  61.9 20.5 %copy-start.1 = (bf16[1,384,2048]{2,1,0:T(8,128)(2,1)S(1)}, bf16[1,384,2048]{2,1,0:T(8,128)(2,1)}, u32[]{:S(2)}) copy-start(bf16[1,384,2048]{2,1,0:T(8,128)(2,1)} %param.17) | copy-start | bytes 4718596
  62.8 45.2 %all-to-all-start.2 = ((bf16[8,104,128]{2,1,0:T(8,128)(2,1)}), bf16[8,104,128]{2,1,0:T(8,128)(2,1)S(1)}, u32[]{:S(2)}, u32[]{:S(2)}) async-start(bf16[8,104,128]{2,1,0:T(8,128)(2,1)} %copy.29), calls=%async_computation.2 | async-start | bytes 425984 | tf_op jit(solution)/shard_map/all_to_all | solution.py:116
  81.5 127.2 %all-gather.2.cloned.1.call-start = ((), (), s32[]{:S(2)}) async-start(), calls=%async_computation.4 | async-start | bytes 1081344 | tf_op jit(solution)/shard_map/all_gather | solution.py:85
  160.3 1.4 copy-start.2
  162.5 0.9 copy-start.4
  174.2 22.7 %copy-start.5 = (bf16[384,1024]{1,0:T(8,128)(2,1)S(1)}, bf16[384,1024]{1,0:T(8,128)(2,1)}, u32[]{:S(2)}) copy-start(bf16[384,1024]{1,0:T(8,128)(2,1)} %copy-done.4) | copy-start | bytes 2359300
  174.2 22.7 %copy-start.9 = (bf16[1,384,224]{1,2,0:T(8,128)(2,1)S(1)}, bf16[1,384,224]{1,2,0:T(8,128)(2,1)}, u32[]{:S(2)}) copy-start(bf16[1,384,224]{1,2,0:T(8,128)(2,1)} %param.16) | copy-start | bytes 516100
  176.4 31.3 %all-to-all-start.3 = ((bf16[32,56,128]{2,1,0:T(8,128)(2,1)}), bf16[32,56,128]{2,1,0:T(8,128)(2,1)S(1)}, u32[]{:S(2)}, u32[]{:S(2)}) async-start(bf16[32,56,128]{2,1,0:T(8,128)(2,1)} %copy.35), calls=%async_computation.3 | async-start | bytes 917504 | tf_op jit(solution)/shard_map/all_to_all | solution.py:147
  196.9 1.6 copy-start.3
  198.5 9.4 %copy-start.10 = (bf16[384,32]{1,0:T(8,128)(2,1)S(1)}, bf16[384,32]{1,0:T(8,128)(2,1)}, u32[]{:S(2)}) copy-start(bf16[384,32]{1,0:T(8,128)(2,1)} %get-tuple-element.8) | copy-start | bytes 73732
Sparse Core Ops, SparseCore 0:
  87.2 77.3 all-gather.1

commit v2 on v1

v2 whole, which is shorter than its diff:
```python
import jax
import jax.numpy as jnp
from jax import lax
from jax.experimental import pallas as pl
from jax.experimental.pallas import tpu as pltpu
from jax.sharding import PartitionSpec as P

NEAR = 4


LANES = 128
SLOT_ROWS = 16


def vmem(count):
    return [pl.BlockSpec(memory_space=pltpu.VMEM) for _ in range(count)]


def dot(a, b, ca, cb):
    return lax.dot_general(a, b, (((ca,), (cb,)), ((), ())), preferred_element_type=jnp.float32)


def route_kernel(capacity, ids_ref, gates_ref, grad_ref, sel_ref, out_ref):
    slots, tokens = sel_ref.shape
    slot = lax.broadcasted_iota(jnp.int32, (slots, 1), 0)
    expert = slot // SLOT_ROWS
    place = slot - expert * SLOT_ROWS
    place = jnp.where(place < capacity, place, tokens).astype(jnp.float32)
    ids = ids_ref[...]
    gates = gates_ref[...]
    hit = jnp.zeros((slots, tokens), jnp.float32)
    weight = jnp.zeros((slots, tokens), jnp.float32)
    for k in range(ids.shape[0]):
        same = ids[k : k + 1, :] == expert
        hit = jnp.where(same, 1.0, hit)
        weight = jnp.where(same, gates[k : k + 1, :], weight)
    row = lax.broadcasted_iota(jnp.int32, (tokens, tokens), 0)
    col = lax.broadcasted_iota(jnp.int32, (tokens, tokens), 1)
    earlier = jnp.where(row < col, 1.0, 0.0).astype(jnp.bfloat16)
    rank = jnp.dot(hit.astype(jnp.bfloat16), earlier, preferred_element_type=jnp.float32)
    taken = (hit > 0.0) & (rank == place)
    sel = jnp.where(taken, 1.0, 0.0).astype(jnp.bfloat16)
    gate = jnp.sum(jnp.where(taken, weight, 0.0), axis=1, keepdims=True)
    rows = jnp.dot(sel, grad_ref[...], preferred_element_type=jnp.float32)
    sel_ref[...] = sel
    scaled = (gate * rows).reshape(slots // SLOT_ROWS, SLOT_ROWS, rows.shape[1])
    out_ref[...] = scaled[:, :capacity, :].astype(jnp.bfloat16)


def swiglu_terms(gate, up, grad_hidden):
    sig = jax.nn.sigmoid(gate)
    act = gate * sig
    return grad_hidden * up * sig * (1.0 + gate * (1.0 - sig)), grad_hidden * act, act * up


def middle_kernel(
    capacity,
    full_ref,
    routed_pre_ref,
    shared_pre_ref,
    w_ref,
    shared_w_ref,
    grad_pre_ref,
    payload_ref,
    shared_back_ref,
):
    slots = routed_pre_ref.shape[0]
    tokens = shared_pre_ref.shape[0]
    half = full_ref.shape[1]
    width = w_ref.shape[0]
    groups = payload_ref.shape[0]
    step = 16
    for r in range(0, slots, step):
        for c in range(0, half, half // 2):
            part = half // 2
            d_gate, d_up, _ = swiglu_terms(
                routed_pre_ref[r : r + step, c : c + part].astype(jnp.float32),
                routed_pre_ref[r : r + step, half + c : half + c + part].astype(jnp.float32),
                full_ref[r : r + step, c : c + part].astype(jnp.float32),
            )
            grad_pre_ref[r : r + step, c : c + part] = d_gate.astype(jnp.bfloat16)
            grad_pre_ref[r : r + step, half + c : half + c + part] = d_up.astype(jnp.bfloat16)
    d_gate, d_up, value = swiglu_terms(
        shared_pre_ref[:, :half].astype(jnp.float32),
        shared_pre_ref[:, half:].astype(jnp.float32),
        full_ref[slots:, :].astype(jnp.float32),
    )
    d_gate, d_up = d_gate.astype(jnp.bfloat16), d_up.astype(jnp.bfloat16)
    value = value.astype(jnp.bfloat16)
    shared_back_ref[...] = dot(d_gate, shared_w_ref[:, :half], 1, 1) + dot(
        d_up, shared_w_ref[:, half:], 1, 1
    )
    gu_cols, down_cols = 2 * half // groups, half // groups
    for j in range(groups):
        source = d_gate if j < groups // 2 else d_up
        at = j % (groups // 2) * gu_cols
        payload_ref[j, :tokens, :gu_cols] = source[:, at : at + gu_cols]
        payload_ref[j, :tokens, gu_cols : gu_cols + down_cols] = value[
            :, j * down_cols : (j + 1) * down_cols
        ]
    used = gu_cols + down_cols
    payload_ref[:, :tokens, used:] = jnp.zeros((groups, tokens, LANES - used), jnp.bfloat16)
    returned = dot(grad_pre_ref[...], w_ref[...], 1, 1).astype(jnp.bfloat16)
    row = lax.broadcasted_iota(jnp.int32, (groups * SLOT_ROWS, slots), 0)
    col = lax.broadcasted_iota(jnp.int32, (groups * SLOT_ROWS, slots), 1)
    expert = row // SLOT_ROWS
    place = row - expert * SLOT_ROWS
    wanted = jnp.where(place < capacity, expert * capacity + place, -1)
    spread = jnp.where(wanted == col, 1.0, 0.0).astype(jnp.bfloat16)
    spaced = dot(spread, returned, 1, 0).astype(jnp.bfloat16)
    spaced = spaced.reshape(groups, SLOT_ROWS, width)
    payload_ref[:, tokens : tokens + SLOT_ROWS, :] = spaced[:, :, :LANES]
    payload_ref[:, tokens + SLOT_ROWS :, : width - LANES] = spaced[:, :, LANES:]
    payload_ref[:, tokens + SLOT_ROWS :, width - LANES :] = jnp.zeros(
        (groups, SLOT_ROWS, 2 * LANES - width), jnp.bfloat16
    )


def last_kernel(
    back_ref, sel_ref, shared_back_ref, everyone_ref, grad_in_ref, shared_gu_ref, shared_dn_ref
):
    groups = back_ref.shape[0]
    slots, tokens = sel_ref.shape
    gu_cols, width = shared_gu_ref.shape
    down_cols = shared_dn_ref.shape[0]
    low = back_ref[:, tokens : tokens + SLOT_ROWS, :].reshape(slots, LANES)
    high = back_ref[:, tokens + SLOT_ROWS :, :].reshape(slots, LANES)
    sel = sel_ref[...]
    shared_back = shared_back_ref[...]
    grad_in_ref[:, :LANES] = (shared_back[:, :LANES] + dot(sel, low, 0, 0)).astype(jnp.bfloat16)
    grad_in_ref[:, LANES:] = (
        shared_back[:, LANES:] + dot(sel, high, 0, 0)[:, : width - LANES]
    ).astype(jnp.bfloat16)
    shared = back_ref[:, :tokens, :].reshape(groups * tokens, LANES)
    grads = dot(shared, everyone_ref[...], 0, 0)
    shared_gu_ref[...] = grads[:gu_cols, 2 * LANES : 2 * LANES + width].astype(jnp.bfloat16)
    shared_dn_ref[...] = grads[gu_cols : gu_cols + down_cols, :width].astype(jnp.bfloat16)


def total(parts):
    acc = parts[0].astype(jnp.float32)
    for i in range(1, parts.shape[0]):
        acc = acc + parts[i].astype(jnp.float32)
    return acc.astype(jnp.bfloat16)


def on_device(
    grad_out,
    expert_ids,
    gate_weights,
    layer_inputs,
    shared_pre,
    routed_inputs,
    routed_pre,
    w_gate_up,
    w_down,
    shared_gate_up,
    shared_down,
):
    groups = lax.axis_size("expert")
    ring = lax.axis_size("dp")
    far = ring // NEAR
    near_groups = [[NEAR * a + b for b in range(NEAR)] for a in range(far)]
    far_groups = [[NEAR * a + b for a in range(far)] for b in range(NEAR)]
    slots = routed_pre.shape[1]
    capacity = slots // groups
    tokens, width = grad_out.shape
    hidden_width = w_down.shape[1]
    routed_pre, routed_inputs = routed_pre[0], routed_inputs[0]
    w_gate_up, w_down = w_gate_up[0], w_down[0]

    limit = pltpu.CompilerParams(vmem_limit_bytes=16 * 1024 * 1024)
    pad = jnp.zeros((tokens, 2 * LANES - width), jnp.bfloat16)
    everyone = lax.all_gather(
        jnp.concatenate([grad_out, pad, layer_inputs, pad], axis=1), "expert", axis=0, tiled=True
    )

    sel, outgoing = pl.pallas_call(
        lambda *refs: route_kernel(capacity, *refs),
        out_shape=(
            jax.ShapeDtypeStruct((groups * SLOT_ROWS, tokens), jnp.bfloat16),
            jax.ShapeDtypeStruct((groups, capacity, width), jnp.bfloat16),
        ),
        compiler_params=limit,
        name="route",
    )(expert_ids.T, gate_weights.T, grad_out)
    arrived = lax.all_to_all(
        outgoing, "expert", split_axis=0, concat_axis=0, tiled=True
    ).reshape(slots, width)

    part = jnp.concatenate(
        [dot(arrived, w_down, 1, 1), dot(grad_out, shared_down, 1, 1)], axis=0
    ).astype(jnp.bfloat16)
    rows = (slots + tokens) // NEAR
    cols = hidden_width // far
    near = lax.all_to_all(
        part.reshape(NEAR, rows, hidden_width),
        "dp",
        split_axis=0,
        concat_axis=0,
        tiled=True,
        axis_index_groups=near_groups,
    )
    near = total(near)
    near = near.reshape(rows, far, cols).transpose(1, 0, 2)
    distant = lax.all_to_all(
        near,
        "dp",
        split_axis=0,
        concat_axis=0,
        tiled=True,
        axis_index_groups=far_groups,
    )
    own = total(distant)
    full = lax.all_gather(own, "dp", axis=1, tiled=True, axis_index_groups=far_groups)
    full = lax.all_gather(full, "dp", axis=0, tiled=True, axis_index_groups=near_groups)

    grad_pre, payload, shared_back = pl.pallas_call(
        lambda *refs: middle_kernel(capacity, *refs),
        out_shape=(
            jax.ShapeDtypeStruct((slots, 2 * hidden_width), jnp.bfloat16),
            jax.ShapeDtypeStruct((groups, tokens + 2 * SLOT_ROWS, LANES), jnp.bfloat16),
            jax.ShapeDtypeStruct((tokens, width), jnp.float32),
        ),
        in_specs=vmem(5),
        out_specs=vmem(3),
        compiler_params=limit,
        name="middle",
    )(full, routed_pre, shared_pre, w_gate_up, shared_gate_up)
    back = lax.all_to_all(payload, "expert", split_axis=0, concat_axis=0, tiled=True)

    gate = routed_pre[:, :hidden_width].astype(jnp.float32)
    up = routed_pre[:, hidden_width:].astype(jnp.float32)
    hidden = (gate * jax.nn.sigmoid(gate) * up).astype(jnp.bfloat16)
    grad_down = dot(hidden, arrived, 0, 0).astype(jnp.bfloat16)
    grad_gate_up = dot(routed_inputs, grad_pre, 0, 0).astype(jnp.bfloat16)

    gu_cols = 2 * hidden_width // groups
    down_cols = hidden_width // groups
    grad_in, shared_gu, shared_dn = pl.pallas_call(
        last_kernel,
        out_shape=(
            jax.ShapeDtypeStruct((tokens, width), jnp.bfloat16),
            jax.ShapeDtypeStruct((gu_cols, width), jnp.bfloat16),
            jax.ShapeDtypeStruct((down_cols, width), jnp.bfloat16),
        ),
        in_specs=vmem(4),
        compiler_params=limit,
        name="last",
    )(back, sel, shared_back, everyone)
    return (
        grad_in,
        grad_gate_up[None],
        grad_down[None],
        shared_gu.T,
        shared_dn,
    )


def solution(mesh):
    in_specs = (
        P("expert", "dp"),
        P("expert", None),
        P("expert", None),
        P("expert", "dp"),
        P("expert", None),
        P("expert", None, "dp"),
        P("expert", None, None),
        P("expert", "dp", None),
        P("expert", None, "dp"),
        P("dp", None),
        P(None, "dp"),
    )
    out_specs = (
        P("expert", "dp"),
        P("expert", "dp", None),
        P("expert", None, "dp"),
        P("dp", "expert"),
        P("expert", "dp"),
    )
    return jax.shard_map(
        on_device, mesh=mesh, in_specs=in_specs, out_specs=out_specs, check_vma=False
    )
```

time: 221 us -> 201 us (0.910)
  local copies, waits for them, and re-layouts: 15.4 us -> 7.29 us
  starting transfers between devices: 56.9 us -> 49.3 us
  matrix products: 10.7 us -> 4.64 us
  other arithmetic: 4.75 us -> 0.92 us
  Pallas kernels: 1.95 us -> 4.72 us
    all_to_all x2, starting transfers between devices: 38.1 us -> 30.4 us  [the longest x1 17.7 us: on_device(): lax.all_to_all(outgoing, 'expert', split_axis=0, concat_axis=0, tiled=True)]
    dot_general x9 -> x4, matrix products: 10.7 us -> 4.64 us  [dot(): lax.dot_general(a, b, (((ca,), (cb,)), ((), ())), preferred_element_type=...]
    reshape x9 -> x1, local copies, waits for them, and re-layouts: 6.05 us -> 0.09 us  [on_device(): arrived = lax.all_to_all(outgoing, 'expert', split_axis=0, concat_axis=0,...]
    unnamed x25 -> x33, local copies, waits for them, and re-layouts: 2.64 us -> 6.48 us
    pallas_call x0 -> x2, Pallas kernels: none -> 3.49 us  [the longest x1 2.48 us: on_device(): pl.pallas_call(lambda *refs: middle_kernel(capacity, *refs), out_shape=(j...]
    slice x5 -> x0, local copies, waits for them, and re-layouts: 2.99 us -> none  [the longest x2 2.28 us: on_device(): low = returned[:, :lanes].reshape(groups, capacity, lanes)]
    another operation x2 -> x0, other arithmetic: 2.43 us -> none
    all_gather x1 -> x2, blocking collectives: 51.1 us -> 53.1 us  [the longest x1 37.8 us: on_device(): lax.all_gather(own, 'dp', axis=1, tiled=True, axis_index_groups=far_groups)]
  transfers between devices with their start and end apart: 4 -> 4, of which waited for: 3 -> 3; matrix products, arithmetic and copies ran while one was open for 10% -> 3% of each run, Pallas kernels for 0% -> 1%
where the time goes in v2:
time: 201 us; the launch traced here: 200 us
  blocking collectives  77 us (38%)
  starting transfers between devices  49.3 us (25%)
  waiting for transfers between devices  42.1 us (21%)
  between operations  14.2 us (7%)
  local copies, waits for them, and re-layouts  7.29 us (4%)
  Pallas kernels  4.72 us (2%)
  matrix products  4.64 us (2%)
    all_gather x1, blocking collectives, on_device(): lax.all_gather(own, 'dp', axis=1, tiled=True, axis_index_groups=far_groups)  37.8 us
    all_to_all x1, waiting for transfers between devices, on_device(): lax.all_to_all(near, 'dp', split_axis=0, concat_axis=0, tiled=True, axis_...  25.7 us
    all_to_all x1, blocking collectives, on_device(): lax.all_to_all(part.reshape(NEAR, rows, hidden_width), 'dp', split_axis=0...  23.8 us
    all_to_all x1, starting transfers between devices, on_device(): lax.all_to_all(near, 'dp', split_axis=0, concat_axis=0, tiled=True, axis_...  18.8 us
    all_to_all x1, starting transfers between devices, on_device(): lax.all_to_all(outgoing, 'expert', split_axis=0, concat_axis=0, tiled=True)  17.7 us
    all_gather x1, blocking collectives, on_device(): lax.all_gather(full, 'dp', axis=0, tiled=True, axis_index_groups=near_gro...  15.3 us
    all_to_all x1, starting transfers between devices, on_device(): lax.all_to_all(payload, 'expert', split_axis=0, concat_axis=0, tiled=True)  12.7 us
    all_to_all x1, waiting for transfers between devices, on_device(): lax.all_to_all(payload, 'expert', split_axis=0, concat_axis=0, tiled=True)  8.55 us
  transfers between devices with their start and end apart: 4, of which 3 were waited for; matrix products, arithmetic and copies ran while one was open for 3% of the time, Pallas kernels for 1%

profile of v2, /device:TPU:1, one launch (start us, length us, event | category | flops | bytes accessed | tf_op | source)
XLA Modules:
  0.0 200.1 jit_solution(8496819978296978702)
XLA Ops:
  7.2 0.0 copy-start
  7.2 0.8 copy-done.7
  8.0 0.7 copy-done.10
  8.6 0.7 copy-done.11
  9.3 1.2 route.1
  10.6 17.7 %all-to-all-start = ((bf16[32,12,224]{2,1,0:T(8,128)(2,1)}), bf16[32,12,224]{2,1,0:T(8,128)(2,1)S(1)}, u32[]{:S(2)}, u32[]{:S(2)}) async-start(bf16[32,12,224]{2,1,0:T(8,128)(2,1)} %get-tuple-element.13), calls=%async_computation | async-start | bytes 524288 | tf_op jit(solution)/shard_map/all_to_all | solution.py:187
  28.2 1.2 convolution_convert_fusion.3
  29.4 7.8 %all-to-all-done = bf16[32,12,224]{2,1,0:T(8,128)(2,1)S(1)} async-done(((bf16[32,12,224]{2,1,0:T(8,128)(2,1)}), bf16[32,12,224]{2,1,0:T(8,128)(2,1)S(1)}, u32[]{:S(2)}, u32[]{:S(2)}) %all-to-all-start) | async-done | bytes 172064 | tf_op jit(solution)/shard_map/all_to_all | solution.py:187
  37.3 0.1 reshape.44
  37.3 0.0 copy-start.12
  37.4 0.7 copy-done.12
  38.0 0.4 convolution_convert_fusion.1
  38.4 0.1 pad_maximum_fusion
  38.5 23.8 %all_to_all.20 = bf16[4,104,1024]{2,1,0:T(8,128)(2,1)S(1)} all-to-all(bf16[4,104,1024]{2,1,0:T(8,128)(2,1)S(1)} %bitcast.37), channel_id=1, replica_groups={{0,1,2,3},{4,5,6,7},{8,9,10,11},{12,13,14,15},{16,17,18,19},{20,21,22,2..., dimensions={0} | all-to-all | bytes 1703936 | tf_op jit(solution)/shard_map/all_to_all | solution.py:196
  62.3 0.1 fusion.9
  62.5 0.7 copy.19
  63.2 18.8 %all-to-all-start.2 = ((bf16[8,104,128]{2,1,0:T(8,128)(2,1)}), bf16[8,104,128]{2,1,0:T(8,128)(2,1)S(1)}, u32[]{:S(2)}, u32[]{:S(2)}) async-start(bf16[8,104,128]{2,1,0:T(8,128)(2,1)} %bitcast.38), calls=%async_computation.2 | async-start | bytes 425984 | tf_op jit(solution)/shard_map/all_to_all | solution.py:206
  82.0 0.0 all-gather.4.cloned.1.call-start
  82.1 0.7 pad_maximum_fusion.1
  82.8 0.0 all-gather.4.cloned.1.call-update
  82.8 25.7 %all-to-all-done.2 = bf16[8,104,128]{2,1,0:T(8,128)(2,1)S(1)} async-done(((bf16[8,104,128]{2,1,0:T(8,128)(2,1)}), bf16[8,104,128]{2,1,0:T(8,128)(2,1)S(1)}, u32[]{:S(2)}, u32[]{:S(2)}) %all-to-all-start.2) | async-done | bytes 213024 | tf_op jit(solution)/shard_map/all_to_all | solution.py:206
  108.6 37.8 %all-gather = bf16[1,104,1024]{2,1,0:T(8,128)(2,1)S(1)} all-gather(bf16[1,104,128]{2,1,0:T(8,128)(2,1)S(1)} %add_convert_fusion.1), channel_id=2, replica_groups={{0,4,8,12,16,20,24,28},{1,5,9,13,17,21,25,29},{2,6,10,14,18,22,26,30},{..., dimensions={2}, use_global_device_ids=true | all-gather | bytes 239616 | tf_op jit(solution)/shard_map/all_gather | solution.py:215
  146.4 15.3 %all-gather.1 = bf16[1,416,1024]{2,1,0:T(8,128)(2,1)S(1)} all-gather(bf16[1,104,1024]{2,1,0:T(8,128)(2,1)S(1)} %all-gather), channel_id=3, replica_groups={{0,1,2,3},{4,5,6,7},{8,9,10,11},{12,13,14,15},{16,17,18,19},{20,21,22,2..., dimensions={1}, use_global_device_ids=true | all-gather | bytes 1064960 | tf_op jit(solution)/shard_map/all_gather | solution.py:216
  161.7 1.2 copy-done.6
  162.9 2.5 %middle.1 = (bf16[384,2048]{1,0:T(8,128)(2,1)S(1)}, bf16[32,64,128]{2,1,0:T(8,128)(2,1)}, f32[32,224]{1,0:T(8,128)S(1)}) custom-call(bf16[416,1024]{1,0:T(8,128)(2,1)S(1)} %bitcast.31, bf16[384,2048]{1,0:T(8,128)(2,1)S(1)} %bitcast.32, bf16[32,2048]{1,0:T(8,128)(2,1)S(1)} %copy-done.9, bf16[224,2048]{1,0:T(8,128)(2,1)S(1)} %bitcast.34, ...), custom_call_target="tpu_custom_call" | custom-call | tf_op jit(solution)/shard_map/middle/pallas_call | solution.py:218
  165.4 1.2 copy-done.2
  166.6 12.7 %all-to-all-start.3 = ((bf16[32,64,128]{2,1,0:T(8,128)(2,1)}), bf16[32,64,128]{2,1,0:T(8,128)(2,1)S(1)}, u32[]{:S(2)}, u32[]{:S(2)}) async-start(bf16[32,64,128]{2,1,0:T(8,128)(2,1)} %get-tuple-element.14), calls=%async_computation.3 | async-start | bytes 1048576 | tf_op jit(solution)/shard_map/all_to_all | solution.py:230
  179.4 1.5 fusion.6
  180.9 1.6 fusion
  182.5 8.6 %all-to-all-done.3.back_ref = bf16[32,64,128]{2,1,0:T(8,128)(2,1)S(1)} async-done(((bf16[32,64,128]{2,1,0:T(8,128)(2,1)}), bf16[32,64,128]{2,1,0:T(8,128)(2,1)S(1)}, u32[]{:S(2)}, u32[]{:S(2)}) %all-to-all-start.3) | async-done | bytes 524320 | tf_op jit(solution)/shard_map/all_to_all | solution.py:230
  191.0 1.2 copy-done.4
  192.2 1.0 last.1
  (27 shorter events, 0.1 us)
Async XLA Ops:
  7.2 30.9 %copy-start = (bf16[1,1024,224]{1,2,0:T(8,128)(2,1)S(1)}, bf16[1,1024,224]{1,2,0:T(8,128)(2,1)}, u32[]{:S(2)}) copy-start(bf16[1,1024,224]{1,2,0:T(8,128)(2,1)} %param.19) | copy-start | bytes 1376260
  7.2 0.8 copy-start.7
  8.0 0.7 copy-start.10
  8.6 0.7 copy-start.11
  10.6 26.7 %all-to-all-start = ((bf16[32,12,224]{2,1,0:T(8,128)(2,1)}), bf16[32,12,224]{2,1,0:T(8,128)(2,1)S(1)}, u32[]{:S(2)}, u32[]{:S(2)}) async-start(bf16[32,12,224]{2,1,0:T(8,128)(2,1)} %get-tuple-element.13), calls=%async_computation | async-start | bytes 524288 | tf_op jit(solution)/shard_map/all_to_all | solution.py:187
  37.3 0.7 copy-start.12
  62.3 19.8 %copy-start.8 = (bf16[32,224]{1,0:T(8,128)(2,1)S(1)}, bf16[32,224]{1,0:T(8,128)(2,1)}, u32[]{:S(2)}) copy-start(bf16[32,224]{1,0:T(8,128)(2,1)} %refs_2_.2) | copy-start | bytes 43012
  62.3 19.8 %copy-start.15 = (bf16[32,224]{1,0:T(8,128)(2,1)S(1)}, bf16[32,224]{1,0:T(8,128)(2,1)}, u32[]{:S(2)}) copy-start(bf16[32,224]{1,0:T(8,128)(2,1)} %param.14) | copy-start | bytes 43012
  62.4 99.3 %copy-start.1 = (bf16[1,384,2048]{2,1,0:T(8,128)(2,1)S(1)}, bf16[1,384,2048]{2,1,0:T(8,128)(2,1)}, u32[]{:S(2)}) copy-start(bf16[1,384,2048]{2,1,0:T(8,128)(2,1)} %param.17) | copy-start | bytes 4718596
  62.4 99.3 %copy-start.5 = (bf16[1,224,2048]{2,1,0:T(8,128)(2,1)S(1)}, bf16[1,224,2048]{2,1,0:T(8,128)(2,1)}, u32[]{:S(2)}) copy-start(bf16[1,224,2048]{2,1,0:T(8,128)(2,1)} %param.18) | copy-start | bytes 2752516
  62.4 99.3 %copy-start.9 = (bf16[32,2048]{1,0:T(8,128)(2,1)S(1)}, bf16[32,2048]{1,0:T(8,128)(2,1)}, u32[]{:S(2)}) copy-start(bf16[32,2048]{1,0:T(8,128)(2,1)} %refs_2_.3) | copy-start | bytes 393220
  63.2 45.3 %all-to-all-start.2 = ((bf16[8,104,128]{2,1,0:T(8,128)(2,1)}), bf16[8,104,128]{2,1,0:T(8,128)(2,1)S(1)}, u32[]{:S(2)}, u32[]{:S(2)}) async-start(bf16[8,104,128]{2,1,0:T(8,128)(2,1)} %bitcast.38), calls=%async_computation.2 | async-start | bytes 425984 | tf_op jit(solution)/shard_map/all_to_all | solution.py:206
  82.0 100.4 %all-gather.4.cloned.1.call-start = ((), (), s32[]{:S(2)}) async-start(), calls=%async_computation.4 | async-start | bytes 1081344 | tf_op jit(solution)/shard_map/all_gather | solution.py:174
  161.7 1.2 copy-start.6
  162.9 16.4 %copy-start.13 = (bf16[384,224]{1,0:T(8,128)(2,1)S(1)}, bf16[384,224]{1,0:T(8,128)(2,1)}, u32[]{:S(2)}) copy-start(bf16[384,224]{1,0:T(8,128)(2,1)} %copy-done.12) | copy-start | bytes 516100
  165.4 1.2 copy-start.2
  166.6 24.4 %all-to-all-start.3 = ((bf16[32,64,128]{2,1,0:T(8,128)(2,1)}), bf16[32,64,128]{2,1,0:T(8,128)(2,1)S(1)}, u32[]{:S(2)}, u32[]{:S(2)}) async-start(bf16[32,64,128]{2,1,0:T(8,128)(2,1)} %get-tuple-element.14), calls=%async_computation.3 | async-start | bytes 1048576 | tf_op jit(solution)/shard_map/all_to_all | solution.py:230
  179.4 1.5 copy-start.3
  179.4 1.5 copy-start.14
  191.0 1.2 copy-start.4
Sparse Core Ops, SparseCore 0:
  87.7 77.3 all-gather.3

commit v3 on v2

--- a/solution.py
+++ b/solution.py
@@ -12,6 +12,10 @@
 SLOT_ROWS = 16
 
 
+def in_hbm(x):
+    return pltpu.with_memory_space_constraint(x, pltpu.HBM)
+
+
 def vmem(count):
     return [pl.BlockSpec(memory_space=pltpu.VMEM) for _ in range(count)]
 
@@ -20,12 +24,22 @@
     return lax.dot_general(a, b, (((ca,), (cb,)), ((), ())), preferred_element_type=jnp.float32)
 
 
-def route_kernel(capacity, ids_ref, gates_ref, grad_ref, sel_ref, out_ref):
+def route_kernel(capacity, ids_hbm, gates_hbm, grad_hbm, sel_ref, out_ref, ids_ref, gates_ref, grad_ref, sems):
+    copies = [
+        pltpu.make_async_copy(source, target, sems.at[i])
+        for i, (source, target) in enumerate(
+            ((ids_hbm, ids_ref), (gates_hbm, gates_ref), (grad_hbm, grad_ref))
+        )
+    ]
+    for copy in copies:
+        copy.start()
     slots, tokens = sel_ref.shape
     slot = lax.broadcasted_iota(jnp.int32, (slots, 1), 0)
     expert = slot // SLOT_ROWS
     place = slot - expert * SLOT_ROWS
     place = jnp.where(place < capacity, place, tokens).astype(jnp.float32)
+    for copy in copies:
+        copy.wait()
     ids = ids_ref[...]
     gates = gates_ref[...]
     hit = jnp.zeros((slots, tokens), jnp.float32)
@@ -59,11 +73,16 @@
     routed_pre_ref,
     shared_pre_ref,
     w_ref,
+    shared_w_hbm,
+    grad_pre_hbm,
+    payload_ref,
+    shared_back_ref,
     shared_w_ref,
     grad_pre_ref,
-    payload_ref,
-    shared_back_ref,
+    sems,
 ):
+    shared_in = pltpu.make_async_copy(shared_w_hbm, shared_w_ref, sems.at[0])
+    shared_in.start()
     slots = routed_pre_ref.shape[0]
     tokens = shared_pre_ref.shape[0]
     half = full_ref.shape[1]
@@ -80,6 +99,8 @@
             )
             grad_pre_ref[r : r + step, c : c + part] = d_gate.astype(jnp.bfloat16)
             grad_pre_ref[r : r + step, half + c : half + c + part] = d_up.astype(jnp.bfloat16)
+    grad_pre_out = pltpu.make_async_copy(grad_pre_ref, grad_pre_hbm, sems.at[1])
+    grad_pre_out.start()
     d_gate, d_up, value = swiglu_terms(
         shared_pre_ref[:, :half].astype(jnp.float32),
         shared_pre_ref[:, half:].astype(jnp.float32),
@@ -87,6 +108,7 @@
     )
     d_gate, d_up = d_gate.astype(jnp.bfloat16), d_up.astype(jnp.bfloat16)
     value = value.astype(jnp.bfloat16)
+    shared_in.wait()
     shared_back_ref[...] = dot(d_gate, shared_w_ref[:, :half], 1, 1) + dot(
         d_up, shared_w_ref[:, half:], 1, 1
     )
@@ -114,11 +136,22 @@
     payload_ref[:, tokens + SLOT_ROWS :, width - LANES :] = jnp.zeros(
         (groups, SLOT_ROWS, 2 * LANES - width), jnp.bfloat16
     )
+    grad_pre_out.wait()
 
 
 def last_kernel(
-    back_ref, sel_ref, shared_back_ref, everyone_ref, grad_in_ref, shared_gu_ref, shared_dn_ref
+    back_ref,
+    sel_ref,
+    shared_back_ref,
+    everyone_hbm,
+    grad_in_ref,
+    shared_gu_ref,
+    shared_dn_ref,
+    everyone_ref,
+    sem,
 ):
+    everyone_in = pltpu.make_async_copy(everyone_hbm, everyone_ref, sem)
+    everyone_in.start()
     groups = back_ref.shape[0]
     slots, tokens = sel_ref.shape
     gu_cols, width = shared_gu_ref.shape
@@ -132,6 +165,7 @@
         shared_back[:, LANES:] + dot(sel, high, 0, 0)[:, : width - LANES]
     ).astype(jnp.bfloat16)
     shared = back_ref[:, :tokens, :].reshape(groups * tokens, LANES)
+    everyone_in.wait()
     grads = dot(shared, everyone_ref[...], 0, 0)
     shared_gu_ref[...] = grads[:gu_cols, 2 * LANES : 2 * LANES + width].astype(jnp.bfloat16)
     shared_dn_ref[...] = grads[gu_cols : gu_cols + down_cols, :width].astype(jnp.bfloat16)
@@ -181,9 +215,16 @@
             jax.ShapeDtypeStruct((groups * SLOT_ROWS, tokens), jnp.bfloat16),
             jax.ShapeDtypeStruct((groups, capacity, width), jnp.bfloat16),
         ),
+        in_specs=[pl.BlockSpec(memory_space=pltpu.HBM)] * 3,
+        scratch_shapes=[
+            pltpu.VMEM(expert_ids.shape[::-1], jnp.int32),
+            pltpu.VMEM(gate_weights.shape[::-1], jnp.float32),
+            pltpu.VMEM(grad_out.shape, jnp.bfloat16),
+            pltpu.SemaphoreType.DMA((3,)),
+        ],
         compiler_params=limit,
         name="route",
-    )(expert_ids.T, gate_weights.T, grad_out)
+    )(*[in_hbm(x) for x in (expert_ids.T, gate_weights.T, grad_out)])
     arrived = lax.all_to_all(
         outgoing, "expert", split_axis=0, concat_axis=0, tiled=True
     ).reshape(slots, width)
@@ -218,15 +259,20 @@
     grad_pre, payload, shared_back = pl.pallas_call(
         lambda *refs: middle_kernel(capacity, *refs),
         out_shape=(
-            jax.ShapeDtypeStruct((slots, 2 * hidden_width), jnp.bfloat16),
+            pltpu.HBM((slots, 2 * hidden_width), jnp.bfloat16),
             jax.ShapeDtypeStruct((groups, tokens + 2 * SLOT_ROWS, LANES), jnp.bfloat16),
             jax.ShapeDtypeStruct((tokens, width), jnp.float32),
         ),
-        in_specs=vmem(5),
-        out_specs=vmem(3),
+        in_specs=vmem(4) + [pl.BlockSpec(memory_space=pltpu.HBM)],
+        out_specs=[pl.BlockSpec(memory_space=pltpu.HBM)] + vmem(2),
+        scratch_shapes=[
+            pltpu.VMEM(shared_gate_up.shape, jnp.bfloat16),
+            pltpu.VMEM((slots, 2 * hidden_width), jnp.bfloat16),
+            pltpu.SemaphoreType.DMA((2,)),
+        ],
         compiler_params=limit,
         name="middle",
-    )(full, routed_pre, shared_pre, w_gate_up, shared_gate_up)
+    )(full, routed_pre, shared_pre, w_gate_up, in_hbm(shared_gate_up))
     back = lax.all_to_all(payload, "expert", split_axis=0, concat_axis=0, tiled=True)
 
     gate = routed_pre[:, :hidden_width].astype(jnp.float32)
@@ -244,10 +290,11 @@
             jax.ShapeDtypeStruct((gu_cols, width), jnp.bfloat16),
             jax.ShapeDtypeStruct((down_cols, width), jnp.bfloat16),
         ),
-        in_specs=vmem(4),
+        in_specs=vmem(3) + [pl.BlockSpec(memory_space=pltpu.HBM)],
+        scratch_shapes=[pltpu.VMEM(everyone.shape, jnp.bfloat16), pltpu.SemaphoreType.DMA],
         compiler_params=limit,
         name="last",
-    )(back, sel, shared_back, everyone)
+    )(back, sel, shared_back, in_hbm(everyone))
     return (
         grad_in,
         grad_gate_up[None],

time: 201 us -> 198 us (0.985)
  local copies, waits for them, and re-layouts: 7.29 us -> 1.56 us
  Pallas kernels: 4.72 us -> 7.72 us
    unnamed x33 -> x21, local copies, waits for them, and re-layouts: 6.48 us -> 0.76 us
  transfers between devices with their start and end apart: 4 -> 4, of which waited for: 3 -> 3; matrix products, arithmetic and copies ran while one was open for 3% -> 3% of each run, Pallas kernels for 1% -> 2%
where the time goes in v3:
time: 198 us; the launch traced here: 197 us
  blocking collectives  77 us (39%)
  starting transfers between devices  49.3 us (25%)
  waiting for transfers between devices  42.1 us (21%)
  between operations  14.2 us (7%)
  Pallas kernels  7.72 us (4%)
  matrix products  4.65 us (2%)
    all_gather x1, blocking collectives, on_device(): lax.all_gather(own, 'dp', axis=1, tiled=True, axis_index_groups=far_groups)  37.8 us
    all_to_all x1, waiting for transfers between devices, on_device(): lax.all_to_all(near, 'dp', split_axis=0, concat_axis=0, tiled=True, axis_...  25.7 us
    all_to_all x1, blocking collectives, on_device(): lax.all_to_all(part.reshape(NEAR, rows, hidden_width), 'dp', split_axis=0...  23.8 us
    all_to_all x1, starting transfers between devices, on_device(): lax.all_to_all(near, 'dp', split_axis=0, concat_axis=0, tiled=True, axis_...  18.8 us
    all_to_all x1, starting transfers between devices, on_device(): lax.all_to_all(outgoing, 'expert', split_axis=0, concat_axis=0, tiled=True)  17.7 us
    all_gather x1, blocking collectives, on_device(): lax.all_gather(full, 'dp', axis=0, tiled=True, axis_index_groups=near_gro...  15.3 us
    all_to_all x1, starting transfers between devices, on_device(): lax.all_to_all(payload, 'expert', split_axis=0, concat_axis=0, tiled=True)  12.7 us
    all_to_all x1, waiting for transfers between devices, on_device(): lax.all_to_all(payload, 'expert', split_axis=0, concat_axis=0, tiled=True)  8.55 us
  transfers between devices with their start and end apart: 4, of which 3 were waited for; matrix products, arithmetic and copies ran while one was open for 3% of the time, Pallas kernels for 2%

profile of v3, /device:TPU:1, one launch (start us, length us, event | category | flops | bytes accessed | tf_op | source)
XLA Modules:
  0.0 197.4 jit_solution(5682978339785264948)
XLA Ops:
  7.2 0.0 copy-start
  7.2 2.2 %route.1 = (bf16[512,32]{1,0:T(8,128)(2,1)S(1)}, bf16[32,12,224]{2,1,0:T(8,128)(2,1)}) custom-call(s32[8,32]{1,0:T(8,128)} %bitcast.38, f32[8,32]{1,0:T(8,128)} %bitcast.39, bf16[32,224]{1,0:T(8,128)(2,1)} %refs_2_.2), custom_call_target="tpu_custom_call" | custom-call | tf_op jit(solution)/shard_map/route/pallas_call | solution.py:212
  9.3 17.7 %all-to-all-start = ((bf16[32,12,224]{2,1,0:T(8,128)(2,1)}), bf16[32,12,224]{2,1,0:T(8,128)(2,1)S(1)}, u32[]{:S(2)}, u32[]{:S(2)}) async-start(bf16[32,12,224]{2,1,0:T(8,128)(2,1)} %get-tuple-element.13), calls=%async_computation | async-start | bytes 524288 | tf_op jit(solution)/shard_map/all_to_all | solution.py:228
  27.0 1.2 convolution_convert_fusion.3
  28.3 7.8 %all-to-all-done = bf16[32,12,224]{2,1,0:T(8,128)(2,1)S(1)} async-done(((bf16[32,12,224]{2,1,0:T(8,128)(2,1)}), bf16[32,12,224]{2,1,0:T(8,128)(2,1)S(1)}, u32[]{:S(2)}, u32[]{:S(2)}) %all-to-all-start) | async-done | bytes 172064 | tf_op jit(solution)/shard_map/all_to_all | solution.py:228
  36.1 0.1 reshape.44
  36.1 0.0 copy-start.5
  36.2 0.7 copy-done.5
  36.8 0.4 convolution_convert_fusion.1
  37.2 0.1 pad_maximum_fusion
  37.3 23.8 %all_to_all.20 = bf16[4,104,1024]{2,1,0:T(8,128)(2,1)S(1)} all-to-all(bf16[4,104,1024]{2,1,0:T(8,128)(2,1)S(1)} %bitcast.35), channel_id=1, replica_groups={{0,1,2,3},{4,5,6,7},{8,9,10,11},{12,13,14,15},{16,17,18,19},{20,21,22,2..., dimensions={0} | all-to-all | bytes 1703936 | tf_op jit(solution)/shard_map/all_to_all | solution.py:237
  61.1 0.1 fusion.9
  61.2 0.0 copy-start.1
  61.2 0.0 copy-start.2
  61.2 0.0 copy-start.3
  61.3 0.7 copy.19
  62.0 18.8 %all-to-all-start.2 = ((bf16[8,104,128]{2,1,0:T(8,128)(2,1)}), bf16[8,104,128]{2,1,0:T(8,128)(2,1)S(1)}, u32[]{:S(2)}, u32[]{:S(2)}) async-start(bf16[8,104,128]{2,1,0:T(8,128)(2,1)} %bitcast.36), calls=%async_computation.2 | async-start | bytes 425984 | tf_op jit(solution)/shard_map/all_to_all | solution.py:247
  80.8 0.0 all-gather.4.cloned.1.call-start
  80.9 0.0 copy-done.8
  80.9 0.7 pad_maximum_fusion.1
  81.6 0.0 all-gather.4.cloned.1.call-update
  81.6 25.7 %all-to-all-done.2 = bf16[8,104,128]{2,1,0:T(8,128)(2,1)S(1)} async-done(((bf16[8,104,128]{2,1,0:T(8,128)(2,1)}), bf16[8,104,128]{2,1,0:T(8,128)(2,1)S(1)}, u32[]{:S(2)}, u32[]{:S(2)}) %all-to-all-start.2) | async-done | bytes 213024 | tf_op jit(solution)/shard_map/all_to_all | solution.py:247
  107.4 37.8 %all-gather = bf16[1,104,1024]{2,1,0:T(8,128)(2,1)S(1)} all-gather(bf16[1,104,128]{2,1,0:T(8,128)(2,1)S(1)} %add_convert_fusion.1), channel_id=2, replica_groups={{0,4,8,12,16,20,24,28},{1,5,9,13,17,21,25,29},{2,6,10,14,18,22,26,30},{..., dimensions={2}, use_global_device_ids=true | all-gather | bytes 239616 | tf_op jit(solution)/shard_map/all_gather | solution.py:256
  145.2 15.3 %all-gather.1 = bf16[1,416,1024]{2,1,0:T(8,128)(2,1)S(1)} all-gather(bf16[1,104,1024]{2,1,0:T(8,128)(2,1)S(1)} %all-gather), channel_id=3, replica_groups={{0,1,2,3},{4,5,6,7},{8,9,10,11},{12,13,14,15},{16,17,18,19},{20,21,22,2..., dimensions={1}, use_global_device_ids=true | all-gather | bytes 1064960 | tf_op jit(solution)/shard_map/all_gather | solution.py:257
  160.5 0.0 copy-start.6
  160.5 3.4 %middle.1 = (bf16[384,2048]{1,0:T(8,128)(2,1)}, bf16[32,64,128]{2,1,0:T(8,128)(2,1)}, f32[32,224]{1,0:T(8,128)S(1)}) custom-call(bf16[416,1024]{1,0:T(8,128)(2,1)S(1)} %bitcast.31, bf16[384,2048]{1,0:T(8,128)(2,1)S(1)} %bitcast.32, bf16[32,2048]{1,0:T(8,128)(2,1)S(1)} %copy-done.3, bf16[224,2048]{1,0:T(8,128)(2,1)S(1)} %bitcast.34, bf16[224,2048]{1,0:T(8,128)(2,1)} %refs_4_.1), custom_call_target="tpu_custom_call" | custom-call | tf_op jit(solution)/shard_map/middle/pallas_call | solution.py:259
  163.9 12.7 %all-to-all-start.3 = ((bf16[32,64,128]{2,1,0:T(8,128)(2,1)}), bf16[32,64,128]{2,1,0:T(8,128)(2,1)S(1)}, u32[]{:S(2)}, u32[]{:S(2)}) async-start(bf16[32,64,128]{2,1,0:T(8,128)(2,1)} %get-tuple-element.14), calls=%async_computation.3 | async-start | bytes 1048576 | tf_op jit(solution)/shard_map/all_to_all | solution.py:276
  176.7 0.0 copy-start.7
  176.7 1.5 fusion.6
  178.2 1.6 fusion
  179.8 8.6 %all-to-all-done.3.back_ref = bf16[32,64,128]{2,1,0:T(8,128)(2,1)S(1)} async-done(((bf16[32,64,128]{2,1,0:T(8,128)(2,1)}), bf16[32,64,128]{2,1,0:T(8,128)(2,1)S(1)}, u32[]{:S(2)}, u32[]{:S(2)}) %all-to-all-start.3) | async-done | bytes 524320 | tf_op jit(solution)/shard_map/all_to_all | solution.py:276
  188.3 2.2 %last.1 = (bf16[32,224]{1,0:T(8,128)(2,1)}, bf16[64,224]{1,0:T(8,128)(2,1)}, bf16[32,224]{1,0:T(8,128)(2,1)}) custom-call(bf16[32,64,128]{2,1,0:T(8,128)(2,1)S(1)} %all-to-all-done.3.back_ref, bf16[512,32]{1,0:T(8,128)(2,1)S(1)} %get-tuple-element.15.sel_ref, f32[32,224]{1,0:T(8,128)S(1)} %get-tuple-element.16.shared_back_ref, ...), custom_call_target="tpu_custom_call" | custom-call | tf_op jit(solution)/shard_map/last/pallas_call | solution.py:286
  (15 shorter events, 0.1 us)
Async XLA Ops:
  7.2 29.7 %copy-start = (bf16[1,1024,224]{1,2,0:T(8,128)(2,1)S(1)}, bf16[1,1024,224]{1,2,0:T(8,128)(2,1)}, u32[]{:S(2)}) copy-start(bf16[1,1024,224]{1,2,0:T(8,128)(2,1)} %param.19) | copy-start | bytes 1376260
  9.3 26.7 %all-to-all-start = ((bf16[32,12,224]{2,1,0:T(8,128)(2,1)}), bf16[32,12,224]{2,1,0:T(8,128)(2,1)S(1)}, u32[]{:S(2)}, u32[]{:S(2)}) async-start(bf16[32,12,224]{2,1,0:T(8,128)(2,1)} %get-tuple-element.13), calls=%async_computation | async-start | bytes 524288 | tf_op jit(solution)/shard_map/all_to_all | solution.py:228
  36.1 0.7 copy-start.5
  61.1 19.8 %copy-start.8 = (bf16[32,224]{1,0:T(8,128)(2,1)S(1)}, bf16[32,224]{1,0:T(8,128)(2,1)}, u32[]{:S(2)}) copy-start(bf16[32,224]{1,0:T(8,128)(2,1)} %refs_2_.2) | copy-start | bytes 43012
  61.1 19.8 %copy-start.9 = (bf16[32,224]{1,0:T(8,128)(2,1)S(1)}, bf16[32,224]{1,0:T(8,128)(2,1)}, u32[]{:S(2)}) copy-start(bf16[32,224]{1,0:T(8,128)(2,1)} %param.14) | copy-start | bytes 43012
  61.2 99.3 %copy-start.1 = (bf16[1,384,2048]{2,1,0:T(8,128)(2,1)S(1)}, bf16[1,384,2048]{2,1,0:T(8,128)(2,1)}, u32[]{:S(2)}) copy-start(bf16[1,384,2048]{2,1,0:T(8,128)(2,1)} %param.17) | copy-start | bytes 4718596
  61.2 99.3 %copy-start.2 = (bf16[1,224,2048]{2,1,0:T(8,128)(2,1)S(1)}, bf16[1,224,2048]{2,1,0:T(8,128)(2,1)}, u32[]{:S(2)}) copy-start(bf16[1,224,2048]{2,1,0:T(8,128)(2,1)} %param.18) | copy-start | bytes 2752516
  61.2 99.3 %copy-start.3 = (bf16[32,2048]{1,0:T(8,128)(2,1)S(1)}, bf16[32,2048]{1,0:T(8,128)(2,1)}, u32[]{:S(2)}) copy-start(bf16[32,2048]{1,0:T(8,128)(2,1)} %refs_2_.3) | copy-start | bytes 393220
  62.0 45.3 %all-to-all-start.2 = ((bf16[8,104,128]{2,1,0:T(8,128)(2,1)}), bf16[8,104,128]{2,1,0:T(8,128)(2,1)S(1)}, u32[]{:S(2)}, u32[]{:S(2)}) async-start(bf16[8,104,128]{2,1,0:T(8,128)(2,1)} %bitcast.36), calls=%async_computation.2 | async-start | bytes 425984 | tf_op jit(solution)/shard_map/all_to_all | solution.py:247
  80.8 99.0 %all-gather.4.cloned.1.call-start = ((), (), s32[]{:S(2)}) async-start(), calls=%async_computation.4 | async-start | bytes 1081344 | tf_op jit(solution)/shard_map/all_gather | solution.py:208
  160.5 16.2 %copy-start.6 = (bf16[384,224]{1,0:T(8,128)(2,1)S(1)}, bf16[384,224]{1,0:T(8,128)(2,1)}, u32[]{:S(2)}) copy-start(bf16[384,224]{1,0:T(8,128)(2,1)} %copy-done.5) | copy-start | bytes 516100
  163.9 24.4 %all-to-all-start.3 = ((bf16[32,64,128]{2,1,0:T(8,128)(2,1)}), bf16[32,64,128]{2,1,0:T(8,128)(2,1)S(1)}, u32[]{:S(2)}, u32[]{:S(2)}) async-start(bf16[32,64,128]{2,1,0:T(8,128)(2,1)} %get-tuple-element.14), calls=%async_computation.3 | async-start | bytes 1048576 | tf_op jit(solution)/shard_map/all_to_all | solution.py:276
  176.7 1.5 copy-start.4
  176.7 1.5 copy-start.7
Sparse Core Ops, SparseCore 0:
  86.5 77.3 all-gather.3

commit v4 on v3

--- a/solution.py
+++ b/solution.py
@@ -24,11 +24,29 @@
     return lax.dot_general(a, b, (((ca,), (cb,)), ((), ())), preferred_element_type=jnp.float32)
 
 
-def route_kernel(capacity, ids_hbm, gates_hbm, grad_hbm, sel_ref, out_ref, ids_ref, gates_ref, grad_ref, sems):
+def route_kernel(
+    capacity,
+    ids_hbm,
+    gates_hbm,
+    grad_hbm,
+    inputs_hbm,
+    sel_ref,
+    out_ref,
+    ids_ref,
+    gates_ref,
+    grad_ref,
+    inputs_ref,
+    sems,
+):
     copies = [
         pltpu.make_async_copy(source, target, sems.at[i])
         for i, (source, target) in enumerate(
-            ((ids_hbm, ids_ref), (gates_hbm, gates_ref), (grad_hbm, grad_ref))
+            (
+                (ids_hbm, ids_ref),
+                (gates_hbm, gates_ref),
+                (grad_hbm, grad_ref),
+                (inputs_hbm, inputs_ref),
+            )
         )
     ]
     for copy in copies:
@@ -58,7 +76,9 @@
     rows = jnp.dot(sel, grad_ref[...], preferred_element_type=jnp.float32)
     sel_ref[...] = sel
     scaled = (gate * rows).reshape(slots // SLOT_ROWS, SLOT_ROWS, rows.shape[1])
-    out_ref[...] = scaled[:, :capacity, :].astype(jnp.bfloat16)
+    out_ref[:, tokens:, :] = scaled[:, :capacity, :].astype(jnp.bfloat16)
+    for j in range(out_ref.shape[0]):
+        out_ref[j, :tokens, :] = grad_ref[...] if j % 2 else inputs_ref[...]
 
 
 def swiglu_terms(gate, up, grad_hidden):
@@ -140,18 +160,31 @@
 
 
 def last_kernel(
+    parity_ref,
     back_ref,
     sel_ref,
     shared_back_ref,
-    everyone_hbm,
+    kept_hbm,
+    other_hbm,
     grad_in_ref,
     shared_gu_ref,
     shared_dn_ref,
-    everyone_ref,
-    sem,
+    inputs_ref,
+    grads_ref,
+    sems,
 ):
-    everyone_in = pltpu.make_async_copy(everyone_hbm, everyone_ref, sem)
-    everyone_in.start()
+    odd = parity_ref[0] == 1
+
+    @pl.when(odd)
+    def _():
+        pltpu.make_async_copy(other_hbm, inputs_ref, sems.at[0]).start()
+        pltpu.make_async_copy(kept_hbm, grads_ref, sems.at[1]).start()
+
+    @pl.when(jnp.logical_not(odd))
+    def _():
+        pltpu.make_async_copy(kept_hbm, inputs_ref, sems.at[0]).start()
+        pltpu.make_async_copy(other_hbm, grads_ref, sems.at[1]).start()
+
     groups = back_ref.shape[0]
     slots, tokens = sel_ref.shape
     gu_cols, width = shared_gu_ref.shape
@@ -165,10 +198,12 @@
         shared_back[:, LANES:] + dot(sel, high, 0, 0)[:, : width - LANES]
     ).astype(jnp.bfloat16)
     shared = back_ref[:, :tokens, :].reshape(groups * tokens, LANES)
-    everyone_in.wait()
-    grads = dot(shared, everyone_ref[...], 0, 0)
-    shared_gu_ref[...] = grads[:gu_cols, 2 * LANES : 2 * LANES + width].astype(jnp.bfloat16)
-    shared_dn_ref[...] = grads[gu_cols : gu_cols + down_cols, :width].astype(jnp.bfloat16)
+    pltpu.make_async_copy(kept_hbm, inputs_ref, sems.at[0]).wait()
+    pltpu.make_async_copy(other_hbm, grads_ref, sems.at[1]).wait()
+    shared_gu_ref[...] = dot(shared, inputs_ref[...], 0, 0)[:gu_cols].astype(jnp.bfloat16)
+    shared_dn_ref[...] = dot(shared, grads_ref[...], 0, 0)[gu_cols : gu_cols + down_cols].astype(
+        jnp.bfloat16
+    )
 
 
 def total(parts):
@@ -204,30 +239,28 @@
     w_gate_up, w_down = w_gate_up[0], w_down[0]
 
     limit = pltpu.CompilerParams(vmem_limit_bytes=16 * 1024 * 1024)
-    pad = jnp.zeros((tokens, 2 * LANES - width), jnp.bfloat16)
-    everyone = lax.all_gather(
-        jnp.concatenate([grad_out, pad, layer_inputs, pad], axis=1), "expert", axis=0, tiled=True
-    )
-
     sel, outgoing = pl.pallas_call(
         lambda *refs: route_kernel(capacity, *refs),
         out_shape=(
             jax.ShapeDtypeStruct((groups * SLOT_ROWS, tokens), jnp.bfloat16),
-            jax.ShapeDtypeStruct((groups, capacity, width), jnp.bfloat16),
+            jax.ShapeDtypeStruct((groups, tokens + capacity, width), jnp.bfloat16),
         ),
-        in_specs=[pl.BlockSpec(memory_space=pltpu.HBM)] * 3,
+        in_specs=[pl.BlockSpec(memory_space=pltpu.HBM)] * 4,
         scratch_shapes=[
             pltpu.VMEM(expert_ids.shape[::-1], jnp.int32),
             pltpu.VMEM(gate_weights.shape[::-1], jnp.float32),
             pltpu.VMEM(grad_out.shape, jnp.bfloat16),
-            pltpu.SemaphoreType.DMA((3,)),
+            pltpu.VMEM(layer_inputs.shape, jnp.bfloat16),
+            pltpu.SemaphoreType.DMA((4,)),
         ],
         compiler_params=limit,
         name="route",
-    )(*[in_hbm(x) for x in (expert_ids.T, gate_weights.T, grad_out)])
-    arrived = lax.all_to_all(
-        outgoing, "expert", split_axis=0, concat_axis=0, tiled=True
-    ).reshape(slots, width)
+    )(*[in_hbm(x) for x in (expert_ids.T, gate_weights.T, grad_out, layer_inputs)])
+    incoming = lax.all_to_all(outgoing, "expert", split_axis=0, concat_axis=0, tiled=True)
+    arrived = incoming[:, tokens:].reshape(slots, width)
+    kept = incoming[:, :tokens].reshape(groups * tokens, width)
+    other = lax.ppermute(kept, "expert", [(i, i ^ 1) for i in range(groups)])
+    parity = (lax.axis_index("expert") % 2).reshape(1).astype(jnp.int32)
 
     part = jnp.concatenate(
         [dot(arrived, w_down, 1, 1), dot(grad_out, shared_down, 1, 1)], axis=0
@@ -290,11 +323,17 @@
             jax.ShapeDtypeStruct((gu_cols, width), jnp.bfloat16),
             jax.ShapeDtypeStruct((down_cols, width), jnp.bfloat16),
         ),
-        in_specs=vmem(3) + [pl.BlockSpec(memory_space=pltpu.HBM)],
-        scratch_shapes=[pltpu.VMEM(everyone.shape, jnp.bfloat16), pltpu.SemaphoreType.DMA],
+        in_specs=[pl.BlockSpec(memory_space=pltpu.SMEM)]
+        + vmem(3)
+        + [pl.BlockSpec(memory_space=pltpu.HBM)] * 2,
+        scratch_shapes=[
+            pltpu.VMEM(kept.shape, jnp.bfloat16),
+            pltpu.VMEM(kept.shape, jnp.bfloat16),
+            pltpu.SemaphoreType.DMA((2,)),
+        ],
         compiler_params=limit,
         name="last",
-    )(back, sel, shared_back, in_hbm(everyone))
+    )(parity, back, sel, shared_back, in_hbm(kept), in_hbm(other))
     return (
         grad_in,
         grad_gate_up[None],

time: 198 us -> 190 us (0.960)
  between operations: 14.2 us -> 0.82 us
  starting transfers between devices: 49.3 us -> 56.2 us
  blocking collectives: 77 us -> 73.7 us
  waiting for transfers between devices: 42.1 us -> 44.2 us
    all_to_all x1, waiting for transfers between devices: 7.79 us -> 14.1 us  [on_device(): lax.all_to_all(outgoing, 'expert', split_axis=0, concat_axis=0, tiled=True)]
    all_to_all x1, waiting for transfers between devices: 25.7 us -> 21.6 us  [on_device(): lax.all_to_all(near, 'dp', split_axis=0, concat_axis=0, tiled=True, axis_...]
    ppermute x0 -> x1, starting transfers between devices: none -> 3.65 us  [on_device(): other = lax.ppermute(kept, 'expert', [(i, i ^ 1) for i in range(groups)])]
    all_to_all x1, starting transfers between devices: 12.7 us -> 15.4 us  [on_device(): lax.all_to_all(payload, 'expert', split_axis=0, concat_axis=0, tiled=True)]
where the time goes in v4:
time: 190 us
  blocking collectives  73.7 us (39%)
  starting transfers between devices  56.2 us (30%)
  waiting for transfers between devices  44.2 us (23%)
  Pallas kernels  7.9 us (4%)
  matrix products  3.62 us (2%)
  local copies, waits for them, and re-layouts  3.16 us (2%)
    all_gather x1, blocking collectives, on_device(): lax.all_gather(own, 'dp', axis=1, tiled=True, axis_index_groups=far_groups)  36.4 us
    all_to_all x1, blocking collectives, on_device(): lax.all_to_all(part.reshape(NEAR, rows, hidden_width), 'dp', split_axis=0...  23.3 us
    all_to_all x1, waiting for transfers between devices, on_device(): lax.all_to_all(near, 'dp', split_axis=0, concat_axis=0, tiled=True, axis_...  21.6 us
    all_to_all x1, starting transfers between devices, on_device(): lax.all_to_all(near, 'dp', split_axis=0, concat_axis=0, tiled=True, axis_...  19.4 us
    all_to_all x1, starting transfers between devices, on_device(): lax.all_to_all(outgoing, 'expert', split_axis=0, concat_axis=0, tiled=True)  17.7 us
    all_to_all x1, starting transfers between devices, on_device(): lax.all_to_all(payload, 'expert', split_axis=0, concat_axis=0, tiled=True)  15.4 us
    all_to_all x1, waiting for transfers between devices, on_device(): lax.all_to_all(outgoing, 'expert', split_axis=0, concat_axis=0, tiled=True)  14.1 us
    all_gather x1, blocking collectives, on_device(): lax.all_gather(full, 'dp', axis=0, tiled=True, axis_index_groups=near_gro...  14 us
  transfers between devices with their start and end apart: 4, of which 3 were waited for; matrix products, arithmetic and copies ran while one was open for 3% of the time, Pallas kernels for 2%

profile of v4, /device:TPU:1, one launch (start us, length us, event | category | flops | bytes accessed | tf_op | source)
XLA Modules:
  0.0 189.8 jit_solution(8119426577355093763)
XLA Ops:
  0.6 0.0 copy-start
  0.7 2.4 %route.1 = (bf16[512,32]{1,0:T(8,128)(2,1)S(1)}, bf16[32,44,224]{2,1,0:T(8,128)(2,1)}) custom-call(s32[8,32]{1,0:T(8,128)} %bitcast.40, f32[8,32]{1,0:T(8,128)} %bitcast.41, bf16[32,224]{1,0:T(8,128)(2,1)} %refs_2_.2, bf16[32,224]{1,0:T(8,128)(2,1)} %refs_3_.1), custom_call_target="tpu_custom_call" | custom-call | tf_op jit(solution)/shard_map/route/pallas_call | solution.py:242
  3.1 17.7 %all-to-all-start = ((bf16[32,44,224]{2,1,0:T(8,128)(2,1)}), bf16[32,44,224]{2,1,0:T(8,128)(2,1)S(1)}, u32[]{:S(2)}, u32[]{:S(2)}) async-start(bf16[32,44,224]{2,1,0:T(8,128)(2,1)} %get-tuple-element.13), calls=%async_computation | async-start | bytes 1572864 | tf_op jit(solution)/shard_map/all_to_all | solution.py:259
  20.8 0.2 convolution_convert_fusion.3
  21.0 14.1 %all-to-all-done = bf16[32,44,224]{2,1,0:T(8,128)(2,1)S(1)} async-done(((bf16[32,44,224]{2,1,0:T(8,128)(2,1)}), bf16[32,44,224]{2,1,0:T(8,128)(2,1)S(1)}, u32[]{:S(2)}, u32[]{:S(2)}) %all-to-all-start) | async-done | bytes 630816 | tf_op jit(solution)/shard_map/all_to_all | solution.py:259
  35.1 0.1 reshape.51
  35.2 0.0 copy-done
  35.3 0.0 copy-start.6
  35.3 0.4 convolution_convert_fusion.1
  35.6 0.1 pad_maximum_fusion
  35.7 0.3 copy-done.4
  36.0 0.1 copy-done.6
  36.1 23.3 %all_to_all.20 = bf16[4,104,1024]{2,1,0:T(8,128)(2,1)S(1)} all-to-all(bf16[4,104,1024]{2,1,0:T(8,128)(2,1)S(1)} %bitcast.37), channel_id=1, replica_groups={{0,1,2,3},{4,5,6,7},{8,9,10,11},{12,13,14,15},{16,17,18,19},{20,21,22,2..., dimensions={0} | all-to-all | bytes 1703936 | tf_op jit(solution)/shard_map/all_to_all | solution.py:270
  59.4 0.1 fusion.9
  59.6 0.7 copy.19
  60.3 19.4 %all-to-all-start.2 = ((bf16[8,104,128]{2,1,0:T(8,128)(2,1)}), bf16[8,104,128]{2,1,0:T(8,128)(2,1)S(1)}, u32[]{:S(2)}, u32[]{:S(2)}) async-start(bf16[8,104,128]{2,1,0:T(8,128)(2,1)} %bitcast.38), calls=%async_computation.2 | async-start | bytes 425984 | tf_op jit(solution)/shard_map/all_to_all | solution.py:280
  79.7 1.9 %slice.77 = bf16[32,32,224]{2,1,0:T(8,128)(2,1)} slice(bf16[32,44,224]{2,1,0:T(8,128)(2,1)} %copy-done.4), slice={[0:32], [0:32], [0:224]} | slice | bytes 917504 | tf_op jit(solution)/shard_map/slice | solution.py:261
  81.7 3.6 %collective-permute-start = (bf16[1024,224]{1,0:T(8,128)(2,1)}, bf16[1024,224]{1,0:T(8,128)(2,1)}, u32[]{:S(2)}, u32[]{:S(2)}) collective-permute-start(bf16[1024,224]{1,0:T(8,128)(2,1)} %bitcast.9.kept_hbm), channel_id=1, source_target_pairs={{0,32},{32,0},{64,96},{96,64},{128,160},{160,128},{192,224},{224,1... | collective-permute-start | bytes 1376264 | tf_op jit(solution)/shard_map/ppermute | solution.py:262
  85.3 21.6 %all-to-all-done.2 = bf16[8,104,128]{2,1,0:T(8,128)(2,1)S(1)} async-done(((bf16[8,104,128]{2,1,0:T(8,128)(2,1)}), bf16[8,104,128]{2,1,0:T(8,128)(2,1)S(1)}, u32[]{:S(2)}, u32[]{:S(2)}) %all-to-all-start.2) | async-done | bytes 213024 | tf_op jit(solution)/shard_map/all_to_all | solution.py:280
  107.0 36.4 %all-gather = bf16[1,104,1024]{2,1,0:T(8,128)(2,1)S(1)} all-gather(bf16[1,104,128]{2,1,0:T(8,128)(2,1)S(1)} %add_convert_fusion.1), channel_id=2, replica_groups={{0,4,8,12,16,20,24,28},{1,5,9,13,17,21,25,29},{2,6,10,14,18,22,26,30},{..., dimensions={2}, use_global_device_ids=true | all-gather | bytes 239616 | tf_op jit(solution)/shard_map/all_gather | solution.py:289
  143.4 14.0 %all-gather.1 = bf16[1,416,1024]{2,1,0:T(8,128)(2,1)S(1)} all-gather(bf16[1,104,1024]{2,1,0:T(8,128)(2,1)S(1)} %all-gather), channel_id=3, replica_groups={{0,1,2,3},{4,5,6,7},{8,9,10,11},{12,13,14,15},{16,17,18,19},{20,21,22,2..., dimensions={1}, use_global_device_ids=true | all-gather | bytes 1064960 | tf_op jit(solution)/shard_map/all_gather | solution.py:290
  157.4 0.0 copy-done.1
  157.4 3.4 %middle.1 = (bf16[384,2048]{1,0:T(8,128)(2,1)}, bf16[32,64,128]{2,1,0:T(8,128)(2,1)}, f32[32,224]{1,0:T(8,128)S(1)}) custom-call(bf16[416,1024]{1,0:T(8,128)(2,1)S(1)} %bitcast.33, bf16[384,2048]{1,0:T(8,128)(2,1)S(1)} %bitcast.34, bf16[32,2048]{1,0:T(8,128)(2,1)S(1)} %copy-done.3, bf16[224,2048]{1,0:T(8,128)(2,1)S(1)} %bitcast.36, bf16[224,2048]{1,0:T(8,128)(2,1)} %refs_4_.1), custom_call_target="tpu_custom_call" | custom-call | tf_op jit(solution)/shard_map/middle/pallas_call | solution.py:292
  160.7 15.4 %all-to-all-start.3 = ((bf16[32,64,128]{2,1,0:T(8,128)(2,1)}), bf16[32,64,128]{2,1,0:T(8,128)(2,1)S(1)}, u32[]{:S(2)}, u32[]{:S(2)}) async-start(bf16[32,64,128]{2,1,0:T(8,128)(2,1)} %get-tuple-element.14), calls=%async_computation.3 | async-start | bytes 1048576 | tf_op jit(solution)/shard_map/all_to_all | solution.py:309
  176.1 0.0 copy-done.7
  176.1 0.0 copy-start.5
  176.1 0.0 copy-start.9
  176.2 1.5 fusion.6
  177.7 1.6 fusion
  179.2 0.0 collective-permute-done.other_hbm
  179.2 8.4 %all-to-all-done.3.back_ref = bf16[32,64,128]{2,1,0:T(8,128)(2,1)S(1)} async-done(((bf16[32,64,128]{2,1,0:T(8,128)(2,1)}), bf16[32,64,128]{2,1,0:T(8,128)(2,1)S(1)}, u32[]{:S(2)}, u32[]{:S(2)}) %all-to-all-start.3) | async-done | bytes 524320 | tf_op jit(solution)/shard_map/all_to_all | solution.py:309
  187.7 2.2 %last.1 = (bf16[32,224]{1,0:T(8,128)(2,1)}, bf16[64,224]{1,0:T(8,128)(2,1)}, bf16[32,224]{1,0:T(8,128)(2,1)}) custom-call(s32[1]{0:T(128)} %bitcast.parity_ref, bf16[32,64,128]{2,1,0:T(8,128)(2,1)S(1)} %all-to-all-done.3.back_ref, bf16[512,32]{1,0:T(8,128)(2,1)S(1)} %get-tuple-element.15.sel_ref, f32[32,224]{1,0:T(8,128)S(1)} %get-tuple-element.16.shared_back_ref, ...), custom_call_target="tpu_custom_call" | custom-call | tf_op jit(solution)/shard_map/last/pallas_call | solution.py:319
  (16 shorter events, 0.1 us)
Async XLA Ops:
  0.6 34.6 %copy-start = (bf16[1,1024,224]{1,2,0:T(8,128)(2,1)S(1)}, bf16[1,1024,224]{1,2,0:T(8,128)(2,1)}, u32[]{:S(2)}) copy-start(bf16[1,1024,224]{1,2,0:T(8,128)(2,1)} %param.19) | copy-start | bytes 1376260
  0.6 20.1 %copy-start.10 = (bf16[32,224]{1,0:T(8,128)(2,1)S(1)}, bf16[32,224]{1,0:T(8,128)(2,1)}, u32[]{:S(2)}) copy-start(bf16[32,224]{1,0:T(8,128)(2,1)} %refs_2_.2) | copy-start | bytes 43012
  0.7 20.1 %copy-start.8 = (bf16[1024,224]{0,1:T(8,128)(2,1)S(1)}, bf16[1024,224]{0,1:T(8,128)(2,1)}, u32[]{:S(2)}) copy-start(bf16[1024,224]{0,1:T(8,128)(2,1)} %param.21) | copy-start | bytes 1376260
  3.1 32.1 %all-to-all-start = ((bf16[32,44,224]{2,1,0:T(8,128)(2,1)}), bf16[32,44,224]{2,1,0:T(8,128)(2,1)S(1)}, u32[]{:S(2)}, u32[]{:S(2)}) async-start(bf16[32,44,224]{2,1,0:T(8,128)(2,1)} %get-tuple-element.13), calls=%async_computation | async-start | bytes 1572864 | tf_op jit(solution)/shard_map/all_to_all | solution.py:259
  35.1 0.9 copy-start.4
  35.3 0.8 copy-start.6
  60.3 97.1 %copy-start.1 = (bf16[1,384,2048]{2,1,0:T(8,128)(2,1)S(1)}, bf16[1,384,2048]{2,1,0:T(8,128)(2,1)}, u32[]{:S(2)}) copy-start(bf16[1,384,2048]{2,1,0:T(8,128)(2,1)} %param.17) | copy-start | bytes 4718596
  60.3 97.1 %copy-start.2 = (bf16[1,224,2048]{2,1,0:T(8,128)(2,1)S(1)}, bf16[1,224,2048]{2,1,0:T(8,128)(2,1)}, u32[]{:S(2)}) copy-start(bf16[1,224,2048]{2,1,0:T(8,128)(2,1)} %param.18) | copy-start | bytes 2752516
  60.3 97.1 %copy-start.3 = (bf16[32,2048]{1,0:T(8,128)(2,1)S(1)}, bf16[32,2048]{1,0:T(8,128)(2,1)}, u32[]{:S(2)}) copy-start(bf16[32,2048]{1,0:T(8,128)(2,1)} %refs_2_.3) | copy-start | bytes 393220
  60.3 46.6 %all-to-all-start.2 = ((bf16[8,104,128]{2,1,0:T(8,128)(2,1)}), bf16[8,104,128]{2,1,0:T(8,128)(2,1)S(1)}, u32[]{:S(2)}, u32[]{:S(2)}) async-start(bf16[8,104,128]{2,1,0:T(8,128)(2,1)} %bitcast.38), calls=%async_computation.2 | async-start | bytes 425984 | tf_op jit(solution)/shard_map/all_to_all | solution.py:280
  81.7 97.6 %collective-permute-start = (bf16[1024,224]{1,0:T(8,128)(2,1)}, bf16[1024,224]{1,0:T(8,128)(2,1)}, u32[]{:S(2)}, u32[]{:S(2)}) collective-permute-start(bf16[1024,224]{1,0:T(8,128)(2,1)} %bitcast.9.kept_hbm), channel_id=1, source_target_pairs={{0,32},{32,0},{64,96},{96,64},{128,160},{160,128},{192,224},{224,1... | collective-permute-start | bytes 1376264 | tf_op jit(solution)/shard_map/ppermute | solution.py:262
  157.4 18.8 %copy-start.7 = (bf16[384,224]{1,0:T(8,128)(2,1)S(1)}, bf16[384,224]{1,0:T(8,128)(2,1)}, u32[]{:S(2)}) copy-start(bf16[384,224]{1,0:T(8,128)(2,1)} %copy-done.6) | copy-start | bytes 516100
  160.7 26.9 %all-to-all-start.3 = ((bf16[32,64,128]{2,1,0:T(8,128)(2,1)}), bf16[32,64,128]{2,1,0:T(8,128)(2,1)S(1)}, u32[]{:S(2)}, u32[]{:S(2)}) async-start(bf16[32,64,128]{2,1,0:T(8,128)(2,1)} %get-tuple-element.14), calls=%async_computation.3 | async-start | bytes 1048576 | tf_op jit(solution)/shard_map/all_to_all | solution.py:309
  176.1 1.5 copy-start.5
  176.1 1.5 copy-start.9

commit v5 on v4

--- a/solution.py
+++ b/solution.py
@@ -81,6 +81,46 @@
         out_ref[j, :tokens, :] = grad_ref[...] if j % 2 else inputs_ref[...]
 
 
+def part_kernel(
+    at_ref,
+    arrived_ref,
+    grad_ref,
+    w_ref,
+    shared_w_ref,
+    own_ref,
+    next_ref,
+    last_ref,
+    left_ref,
+    right_ref,
+    blocks_ref,
+):
+    rows, columns = own_ref.shape
+    routed = dot(arrived_ref[...], w_ref[...], 1, 0)
+    shared = dot(grad_ref[...], shared_w_ref[...], 1, 0)
+    both = jnp.concatenate([routed, shared], axis=0)
+    for b in range(NEAR):
+        blocks_ref[b] = both[b * rows : (b + 1) * rows].astype(jnp.bfloat16)
+    at = at_ref[0]
+    own_ref[...] = blocks_ref[at]
+    next_ref[...] = blocks_ref[lax.rem(at + 1, NEAR)]
+    last_ref[...] = blocks_ref[lax.rem(at + NEAR - 1, NEAR)]
+    opposite = lax.rem(at + 2, NEAR)
+    left_ref[...] = blocks_ref[opposite, :, : columns // 2]
+    right_ref[...] = blocks_ref[opposite, :, columns // 2 :]
+
+
+def near_kernel(own_ref, after_ref, before_ref, ahead_ref, behind_ref, out_ref):
+    far, _, cols = out_ref.shape
+    f32 = jnp.float32
+    for a in range(far):
+        lanes = slice(a * cols, (a + 1) * cols)
+        total = own_ref[:, lanes].astype(f32) + after_ref[:, lanes].astype(f32)
+        total = total + before_ref[:, lanes].astype(f32)
+        half = ahead_ref if a < far // 2 else behind_ref
+        at = a % (far // 2) * cols
+        out_ref[a] = (total + half[:, at : at + cols].astype(f32)).astype(jnp.bfloat16)
+
+
 def swiglu_terms(gate, up, grad_hidden):
     sig = jax.nn.sigmoid(gate)
     act = gate * sig
@@ -262,21 +302,34 @@
     other = lax.ppermute(kept, "expert", [(i, i ^ 1) for i in range(groups)])
     parity = (lax.axis_index("expert") % 2).reshape(1).astype(jnp.int32)
 
-    part = jnp.concatenate(
-        [dot(arrived, w_down, 1, 1), dot(grad_out, shared_down, 1, 1)], axis=0
-    ).astype(jnp.bfloat16)
     rows = (slots + tokens) // NEAR
     cols = hidden_width // far
-    near = lax.all_to_all(
-        part.reshape(NEAR, rows, hidden_width),
-        "dp",
-        split_axis=0,
-        concat_axis=0,
-        tiled=True,
-        axis_index_groups=near_groups,
-    )
-    near = total(near)
-    near = near.reshape(rows, far, cols).transpose(1, 0, 2)
+    half = hidden_width // 2
+
+    def shift(x, by):
+        return lax.ppermute(x, "dp", [(i, (i + by) % ring) for i in range(ring)])
+
+    def block(columns):
+        return jax.ShapeDtypeStruct((rows, columns), jnp.bfloat16)
+
+    quarter = (lax.axis_index("dp") % NEAR).reshape(1).astype(jnp.int32)
+    own, to_next, to_last, to_right, to_left = pl.pallas_call(
+        part_kernel,
+        out_shape=(block(hidden_width),) * 3 + (block(half),) * 2,
+        in_specs=[pl.BlockSpec(memory_space=pltpu.SMEM)] + vmem(4),
+        out_specs=vmem(5),
+        scratch_shapes=[pltpu.VMEM((NEAR, rows, hidden_width), jnp.bfloat16)],
+        compiler_params=limit,
+        name="part",
+    )(quarter, arrived, grad_out, w_down.T, shared_down.T)
+    near = pl.pallas_call(
+        near_kernel,
+        out_shape=jax.ShapeDtypeStruct((far, rows, cols), jnp.bfloat16),
+        in_specs=vmem(5),
+        out_specs=vmem(1)[0],
+        compiler_params=limit,
+        name="near",
+    )(own, shift(to_next, 1), shift(to_last, -1), shift(to_right, 2), shift(to_left, -2))
     distant = lax.all_to_all(
         near,
         "dp",

time: 190 us -> 185 us (0.974)
  blocking collectives: 73.7 us -> 48.1 us
  starting transfers between devices: 56.2 us -> 71.6 us
  waiting for transfers between devices: 44.2 us -> 49.8 us
    all_to_all x1 -> x0, blocking collectives: 23.3 us -> none  [on_device(): lax.all_to_all(part.reshape(NEAR, rows, hidden_width), 'dp', split_axis=0...]
    ppermute x0 -> x4, starting transfers between devices: none -> 18.5 us  [shift(): return lax.ppermute(x, 'dp', [(i, (i + by) % ring) for i in range(ring)])]
    all_gather x1, blocking collectives: 36.4 us -> 30.6 us  [on_device(): lax.all_gather(own, 'dp', axis=1, tiled=True, axis_index_groups=far_groups)]
    all_to_all x1, starting transfers between devices: 19.4 us -> 15.5 us  [on_device(): lax.all_to_all(near, 'dp', split_axis=0, concat_axis=0, tiled=True, axis_...]
    all_gather x1, blocking collectives: 14 us -> 17.5 us  [on_device(): lax.all_gather(full, 'dp', axis=0, tiled=True, axis_index_groups=near_gro...]
    ppermute x0 -> x4, waiting for transfers between devices: none -> 2.89 us  [shift(): return lax.ppermute(x, 'dp', [(i, (i + by) % ring) for i in range(ring)])]
    all_to_all x1, waiting for transfers between devices: 21.6 us -> 24.1 us  [on_device(): lax.all_to_all(near, 'dp', split_axis=0, concat_axis=0, tiled=True, axis_...]
  transfers between devices with their start and end apart: 4 -> 8, of which waited for: 3 -> 4; matrix products, arithmetic and copies ran while one was open for 3% -> 3% of each run, Pallas kernels for 2% -> 2%
where the time goes in v5:
time: 185 us
  starting transfers between devices  71.6 us (39%)
  waiting for transfers between devices  49.8 us (27%)
  blocking collectives  48.1 us (26%)
  Pallas kernels  9.17 us (5%)
  matrix products  3.07 us (2%)
  local copies, waits for them, and re-layouts  2.03 us (1%)
    all_gather x1, blocking collectives, on_device(): lax.all_gather(own, 'dp', axis=1, tiled=True, axis_index_groups=far_groups)  30.6 us
    all_to_all x1, waiting for transfers between devices, on_device(): lax.all_to_all(near, 'dp', split_axis=0, concat_axis=0, tiled=True, axis_...  24.1 us
    ppermute x4, starting transfers between devices, shift(): return lax.ppermute(x, 'dp', [(i, (i + by) % ring) for i in range(ring)])  18.5 us
    all_to_all x1, starting transfers between devices, on_device(): lax.all_to_all(outgoing, 'expert', split_axis=0, concat_axis=0, tiled=True)  17.7 us
    all_gather x1, blocking collectives, on_device(): lax.all_gather(full, 'dp', axis=0, tiled=True, axis_index_groups=near_gro...  17.5 us
    all_to_all x1, starting transfers between devices, on_device(): lax.all_to_all(payload, 'expert', split_axis=0, concat_axis=0, tiled=True)  16.5 us
    all_to_all x1, starting transfers between devices, on_device(): lax.all_to_all(near, 'dp', split_axis=0, concat_axis=0, tiled=True, axis_...  15.5 us
    all_to_all x1, waiting for transfers between devices, on_device(): lax.all_to_all(outgoing, 'expert', split_axis=0, concat_axis=0, tiled=True)  14.3 us
  transfers between devices with their start and end apart: 8, of which 4 were waited for; matrix products, arithmetic and copies ran while one was open for 3% of the time, Pallas kernels for 2%

profile of v5, /device:TPU:1, one launch (start us, length us, event | category | flops | bytes accessed | tf_op | source)
XLA Modules:
  0.0 184.6 jit_solution(7840349580479306322)
XLA Ops:
  0.6 0.0 copy-start
  0.6 0.0 copy-start.6
  0.7 0.0 copy-start.3
  0.7 0.0 copy-start.4
  0.7 2.4 %route.1 = (bf16[512,32]{1,0:T(8,128)(2,1)S(1)}, bf16[32,44,224]{2,1,0:T(8,128)(2,1)}) custom-call(s32[8,32]{1,0:T(8,128)} %bitcast.30, f32[8,32]{1,0:T(8,128)} %bitcast.31, bf16[32,224]{1,0:T(8,128)(2,1)} %grad_ref.1, bf16[32,224]{1,0:T(8,128)(2,1)} %refs_3_.1), custom_call_target="tpu_custom_call" | custom-call | tf_op jit(solution)/shard_map/route/pallas_call | solution.py:282
  3.1 17.7 %all-to-all-start = ((bf16[32,44,224]{2,1,0:T(8,128)(2,1)}), bf16[32,44,224]{2,1,0:T(8,128)(2,1)S(1)}, u32[]{:S(2)}, u32[]{:S(2)}) async-start(bf16[32,44,224]{2,1,0:T(8,128)(2,1)} %get-tuple-element.18), calls=%async_computation | async-start | bytes 1572864 | tf_op jit(solution)/shard_map/all_to_all | solution.py:299
  20.8 14.3 %all-to-all-done = bf16[32,44,224]{2,1,0:T(8,128)(2,1)S(1)} async-done(((bf16[32,44,224]{2,1,0:T(8,128)(2,1)}), bf16[32,44,224]{2,1,0:T(8,128)(2,1)S(1)}, u32[]{:S(2)}, u32[]{:S(2)}) %all-to-all-start) | async-done | bytes 630816 | tf_op jit(solution)/shard_map/all_to_all | solution.py:299
  35.2 0.1 reshape.39.arrived_ref
  35.3 0.5 part.1
  35.8 1.9 %collective-permute-start = (bf16[104,1024]{1,0:T(8,128)(2,1)S(1)}, bf16[104,1024]{1,0:T(8,128)(2,1)S(1)}, u32[]{:S(2)}, u32[]{:S(2)}) collective-permute-start(bf16[104,1024]{1,0:T(8,128)(2,1)S(1)} %get-tuple-element.20), channel_id=1, source_target_pairs={{0,1},{1,2},{2,3},{3,4},{4,5},{5,6},{6,7},{7,8},{8,9},{9,10},{10,1... | collective-permute-start | bytes 638984 | tf_op jit(solution)/shard_map/ppermute | solution.py:310
  37.7 9.1 %collective-permute-start.1 = (bf16[104,1024]{1,0:T(8,128)(2,1)S(1)}, bf16[104,1024]{1,0:T(8,128)(2,1)S(1)}, u32[]{:S(2)}, u32[]{:S(2)}) collective-permute-start(bf16[104,1024]{1,0:T(8,128)(2,1)S(1)} %get-tuple-element.21), channel_id=1, source_target_pairs={{0,31},{1,0},{2,1},{3,2},{4,3},{5,4},{6,5},{7,6},{8,7},{9,8},{10,9... | collective-permute-start | bytes 638984 | tf_op jit(solution)/shard_map/ppermute | solution.py:310
  46.9 1.9 %collective-permute-start.2 = (bf16[104,512]{1,0:T(8,128)(2,1)S(1)}, bf16[104,512]{1,0:T(8,128)(2,1)S(1)}, u32[]{:S(2)}, u32[]{:S(2)}) collective-permute-start(bf16[104,512]{1,0:T(8,128)(2,1)S(1)} %get-tuple-element.22), channel_id=1, source_target_pairs={{0,2},{1,3},{2,4},{3,5},{4,6},{5,7},{6,8},{7,9},{8,10},{9,11},{10,... | collective-permute-start | bytes 319496 | tf_op jit(solution)/shard_map/ppermute | solution.py:310
  48.8 5.5 %collective-permute-start.3 = (bf16[104,512]{1,0:T(8,128)(2,1)S(1)}, bf16[104,512]{1,0:T(8,128)(2,1)S(1)}, u32[]{:S(2)}, u32[]{:S(2)}) collective-permute-start(bf16[104,512]{1,0:T(8,128)(2,1)S(1)} %get-tuple-element.23), channel_id=1, source_target_pairs={{0,30},{1,31},{2,0},{3,1},{4,2},{5,3},{6,4},{7,5},{8,6},{9,7},{10,... | collective-permute-start | bytes 319496 | tf_op jit(solution)/shard_map/ppermute | solution.py:310
  54.3 2.9 %collective-permute-done.2.ahead_ref = bf16[104,512]{1,0:T(8,128)(2,1)S(1)} collective-permute-done((bf16[104,512]{1,0:T(8,128)(2,1)S(1)}, bf16[104,512]{1,0:T(8,128)(2,1)S(1)}, u32[]{:S(2)}, u32[]{:S(2)}) %collective-permute-start.2) | collective-permute-done | bytes 106528 | tf_op jit(solution)/shard_map/ppermute | solution.py:310
  57.2 0.0 collective-permute-done.3.behind_ref
  57.2 0.0 collective-permute-done.after_ref
  57.2 0.0 collective-permute-done.1.before_ref
  57.2 0.8 near.1
  58.0 15.5 %all-to-all-start.1 = ((bf16[8,104,128]{2,1,0:T(8,128)(2,1)}), bf16[8,104,128]{2,1,0:T(8,128)(2,1)S(1)}, u32[]{:S(2)}, u32[]{:S(2)}) async-start(bf16[8,104,128]{2,1,0:T(8,128)(2,1)} %near.1), calls=%async_computation.1 | async-start | bytes 425984 | tf_op jit(solution)/shard_map/all_to_all | solution.py:333
  73.5 1.9 %slice.57 = bf16[32,32,224]{2,1,0:T(8,128)(2,1)} slice(bf16[32,44,224]{2,1,0:T(8,128)(2,1)} %copy-done.7), slice={[0:32], [0:32], [0:224]} | slice | bytes 917504 | tf_op jit(solution)/shard_map/slice | solution.py:301
  75.4 3.4 %collective-permute-start.4 = (bf16[1024,224]{1,0:T(8,128)(2,1)}, bf16[1024,224]{1,0:T(8,128)(2,1)}, u32[]{:S(2)}, u32[]{:S(2)}) collective-permute-start(bf16[1024,224]{1,0:T(8,128)(2,1)} %bitcast.10.kept_hbm), channel_id=1, source_target_pairs={{0,32},{32,0},{64,96},{96,64},{128,160},{160,128},{192,224},{224,1... | collective-permute-start | bytes 1376264 | tf_op jit(solution)/shard_map/ppermute | solution.py:302
  78.8 24.1 %all-to-all-done.1 = bf16[8,104,128]{2,1,0:T(8,128)(2,1)S(1)} async-done(((bf16[8,104,128]{2,1,0:T(8,128)(2,1)}), bf16[8,104,128]{2,1,0:T(8,128)(2,1)S(1)}, u32[]{:S(2)}, u32[]{:S(2)}) %all-to-all-start.1) | async-done | bytes 213024 | tf_op jit(solution)/shard_map/all_to_all | solution.py:333
  103.0 30.6 %all-gather = bf16[1,104,1024]{2,1,0:T(8,128)(2,1)S(1)} all-gather(bf16[1,104,128]{2,1,0:T(8,128)(2,1)S(1)} %add_convert_fusion), channel_id=2, replica_groups={{0,4,8,12,16,20,24,28},{1,5,9,13,17,21,25,29},{2,6,10,14,18,22,26,30},{..., dimensions={2}, use_global_device_ids=true | all-gather | bytes 239616 | tf_op jit(solution)/shard_map/all_gather | solution.py:342
  133.6 17.5 %all-gather.1 = bf16[1,416,1024]{2,1,0:T(8,128)(2,1)S(1)} all-gather(bf16[1,104,1024]{2,1,0:T(8,128)(2,1)S(1)} %all-gather), channel_id=3, replica_groups={{0,1,2,3},{4,5,6,7},{8,9,10,11},{12,13,14,15},{16,17,18,19},{20,21,22,2..., dimensions={1}, use_global_device_ids=true | all-gather | bytes 1064960 | tf_op jit(solution)/shard_map/all_gather | solution.py:343
  151.1 0.0 copy-done.1
  151.1 3.3 %middle.1 = (bf16[384,2048]{1,0:T(8,128)(2,1)}, bf16[32,64,128]{2,1,0:T(8,128)(2,1)}, f32[32,224]{1,0:T(8,128)S(1)}) custom-call(bf16[416,1024]{1,0:T(8,128)(2,1)S(1)} %bitcast.24, bf16[384,2048]{1,0:T(8,128)(2,1)S(1)} %bitcast.25, bf16[32,2048]{1,0:T(8,128)(2,1)S(1)} %copy-done.5, bf16[224,2048]{1,0:T(8,128)(2,1)S(1)} %bitcast.27, bf16[224,2048]{1,0:T(8,128)(2,1)} %refs_4_.1), custom_call_target="tpu_custom_call" | custom-call | tf_op jit(solution)/shard_map/middle/pallas_call | solution.py:345
  154.4 16.5 %all-to-all-start.2 = ((bf16[32,64,128]{2,1,0:T(8,128)(2,1)}), bf16[32,64,128]{2,1,0:T(8,128)(2,1)S(1)}, u32[]{:S(2)}, u32[]{:S(2)}) async-start(bf16[32,64,128]{2,1,0:T(8,128)(2,1)} %get-tuple-element.24), calls=%async_computation.2 | async-start | bytes 1048576 | tf_op jit(solution)/shard_map/all_to_all | solution.py:362
  170.9 1.5 fusion.6
  172.4 1.6 fusion
  174.0 0.0 collective-permute-done.4.other_hbm
  174.0 8.5 %all-to-all-done.2.back_ref = bf16[32,64,128]{2,1,0:T(8,128)(2,1)S(1)} async-done(((bf16[32,64,128]{2,1,0:T(8,128)(2,1)}), bf16[32,64,128]{2,1,0:T(8,128)(2,1)S(1)}, u32[]{:S(2)}, u32[]{:S(2)}) %all-to-all-start.2) | async-done | bytes 524320 | tf_op jit(solution)/shard_map/all_to_all | solution.py:362
  182.4 2.2 %last.1 = (bf16[32,224]{1,0:T(8,128)(2,1)}, bf16[64,224]{1,0:T(8,128)(2,1)}, bf16[32,224]{1,0:T(8,128)(2,1)}) custom-call(s32[1]{0:T(128)} %bitcast.parity_ref, bf16[32,64,128]{2,1,0:T(8,128)(2,1)S(1)} %all-to-all-done.2.back_ref, bf16[512,32]{1,0:T(8,128)(2,1)S(1)} %get-tuple-element.25.sel_ref, f32[32,224]{1,0:T(8,128)S(1)} %get-tuple-element.26.shared_back_ref, ...), custom_call_target="tpu_custom_call" | custom-call | tf_op jit(solution)/shard_map/last/pallas_call | solution.py:372
  (15 shorter events, 0.1 us)
Async XLA Ops:
  0.6 171.8 %copy-start = (bf16[1,384,224]{1,2,0:T(8,128)(2,1)S(1)}, bf16[1,384,224]{1,2,0:T(8,128)(2,1)}, u32[]{:S(2)}) copy-start(bf16[1,384,224]{1,2,0:T(8,128)(2,1)} %param.16) | copy-start | bytes 516100
  0.6 34.6 %copy-start.6 = (bf16[32,224]{1,0:T(8,128)(2,1)S(1)}, bf16[32,224]{1,0:T(8,128)(2,1)}, u32[]{:S(2)}) copy-start(bf16[32,224]{1,0:T(8,128)(2,1)} %grad_ref.1) | copy-start | bytes 43012
  0.7 34.6 %copy-start.3 = (bf16[1,1024,224]{1,2,0:T(8,128)(2,1)S(1)}, bf16[1,1024,224]{1,2,0:T(8,128)(2,1)}, u32[]{:S(2)}) copy-start(bf16[1,1024,224]{1,2,0:T(8,128)(2,1)} %param.19) | copy-start | bytes 1376260
  0.7 34.6 %copy-start.4 = (bf16[1024,224]{0,1:T(8,128)(2,1)S(1)}, bf16[1024,224]{0,1:T(8,128)(2,1)}, u32[]{:S(2)}) copy-start(bf16[1024,224]{0,1:T(8,128)(2,1)} %param.21) | copy-start | bytes 1376260
  3.1 32.1 %all-to-all-start = ((bf16[32,44,224]{2,1,0:T(8,128)(2,1)}), bf16[32,44,224]{2,1,0:T(8,128)(2,1)S(1)}, u32[]{:S(2)}, u32[]{:S(2)}) async-start(bf16[32,44,224]{2,1,0:T(8,128)(2,1)} %get-tuple-element.18), calls=%async_computation | async-start | bytes 1572864 | tf_op jit(solution)/shard_map/all_to_all | solution.py:299
  35.1 22.0 %copy-start.7 = (bf16[32,44,224]{2,1,0:T(8,128)(2,1)}, bf16[32,44,224]{2,1,0:T(8,128)(2,1)S(1)}, u32[]{:S(2)}) copy-start(bf16[32,44,224]{2,1,0:T(8,128)(2,1)S(1)} %all-to-all-done) | copy-start | bytes 1892356
  35.8 21.4 %collective-permute-start = (bf16[104,1024]{1,0:T(8,128)(2,1)S(1)}, bf16[104,1024]{1,0:T(8,128)(2,1)S(1)}, u32[]{:S(2)}, u32[]{:S(2)}) collective-permute-start(bf16[104,1024]{1,0:T(8,128)(2,1)S(1)} %get-tuple-element.20), channel_id=1, source_target_pairs={{0,1},{1,2},{2,3},{3,4},{4,5},{5,6},{6,7},{7,8},{8,9},{9,10},{10,1... | collective-permute-start | bytes 638984 | tf_op jit(solution)/shard_map/ppermute | solution.py:310
  37.7 19.5 %collective-permute-start.1 = (bf16[104,1024]{1,0:T(8,128)(2,1)S(1)}, bf16[104,1024]{1,0:T(8,128)(2,1)S(1)}, u32[]{:S(2)}, u32[]{:S(2)}) collective-permute-start(bf16[104,1024]{1,0:T(8,128)(2,1)S(1)} %get-tuple-element.21), channel_id=1, source_target_pairs={{0,31},{1,0},{2,1},{3,2},{4,3},{5,4},{6,5},{7,6},{8,7},{9,8},{10,9... | collective-permute-start | bytes 638984 | tf_op jit(solution)/shard_map/ppermute | solution.py:310
  46.9 10.3 %collective-permute-start.2 = (bf16[104,512]{1,0:T(8,128)(2,1)S(1)}, bf16[104,512]{1,0:T(8,128)(2,1)S(1)}, u32[]{:S(2)}, u32[]{:S(2)}) collective-permute-start(bf16[104,512]{1,0:T(8,128)(2,1)S(1)} %get-tuple-element.22), channel_id=1, source_target_pairs={{0,2},{1,3},{2,4},{3,5},{4,6},{5,7},{6,8},{7,9},{8,10},{9,11},{10,... | collective-permute-start | bytes 319496 | tf_op jit(solution)/shard_map/ppermute | solution.py:310
  48.8 8.4 %collective-permute-start.3 = (bf16[104,512]{1,0:T(8,128)(2,1)S(1)}, bf16[104,512]{1,0:T(8,128)(2,1)S(1)}, u32[]{:S(2)}, u32[]{:S(2)}) collective-permute-start(bf16[104,512]{1,0:T(8,128)(2,1)S(1)} %get-tuple-element.23), channel_id=1, source_target_pairs={{0,30},{1,31},{2,0},{3,1},{4,2},{5,3},{6,4},{7,5},{8,6},{9,7},{10,... | collective-permute-start | bytes 319496 | tf_op jit(solution)/shard_map/ppermute | solution.py:310
  58.0 93.1 %copy-start.1 = (bf16[1,384,2048]{2,1,0:T(8,128)(2,1)S(1)}, bf16[1,384,2048]{2,1,0:T(8,128)(2,1)}, u32[]{:S(2)}) copy-start(bf16[1,384,2048]{2,1,0:T(8,128)(2,1)} %param.17) | copy-start | bytes 4718596
  58.0 93.1 %copy-start.2 = (bf16[1,224,2048]{2,1,0:T(8,128)(2,1)S(1)}, bf16[1,224,2048]{2,1,0:T(8,128)(2,1)}, u32[]{:S(2)}) copy-start(bf16[1,224,2048]{2,1,0:T(8,128)(2,1)} %param.18) | copy-start | bytes 2752516
  58.0 93.1 %copy-start.5 = (bf16[32,2048]{1,0:T(8,128)(2,1)S(1)}, bf16[32,2048]{1,0:T(8,128)(2,1)}, u32[]{:S(2)}) copy-start(bf16[32,2048]{1,0:T(8,128)(2,1)} %refs_2_.3) | copy-start | bytes 393220
  58.0 44.9 %all-to-all-start.1 = ((bf16[8,104,128]{2,1,0:T(8,128)(2,1)}), bf16[8,104,128]{2,1,0:T(8,128)(2,1)S(1)}, u32[]{:S(2)}, u32[]{:S(2)}) async-start(bf16[8,104,128]{2,1,0:T(8,128)(2,1)} %near.1), calls=%async_computation.1 | async-start | bytes 425984 | tf_op jit(solution)/shard_map/all_to_all | solution.py:333
  75.4 98.6 %collective-permute-start.4 = (bf16[1024,224]{1,0:T(8,128)(2,1)}, bf16[1024,224]{1,0:T(8,128)(2,1)}, u32[]{:S(2)}, u32[]{:S(2)}) collective-permute-start(bf16[1024,224]{1,0:T(8,128)(2,1)} %bitcast.10.kept_hbm), channel_id=1, source_target_pairs={{0,32},{32,0},{64,96},{96,64},{128,160},{160,128},{192,224},{224,1... | collective-permute-start | bytes 1376264 | tf_op jit(solution)/shard_map/ppermute | solution.py:302
  154.4 28.1 %all-to-all-start.2 = ((bf16[32,64,128]{2,1,0:T(8,128)(2,1)}), bf16[32,64,128]{2,1,0:T(8,128)(2,1)S(1)}, u32[]{:S(2)}, u32[]{:S(2)}) async-start(bf16[32,64,128]{2,1,0:T(8,128)(2,1)} %get-tuple-element.24), calls=%async_computation.2 | async-start | bytes 1048576 | tf_op jit(solution)/shard_map/all_to_all | solution.py:362
  170.9 1.5 copy-start.8

commit v6 on v5

--- a/solution.py
+++ b/solution.py
@@ -76,9 +76,12 @@
     rows = jnp.dot(sel, grad_ref[...], preferred_element_type=jnp.float32)
     sel_ref[...] = sel
     scaled = (gate * rows).reshape(slots // SLOT_ROWS, SLOT_ROWS, rows.shape[1])
-    out_ref[:, tokens:, :] = scaled[:, :capacity, :].astype(jnp.bfloat16)
+    part = tokens // 2
+    out_ref[:, part:, :] = scaled[:, :capacity, :].astype(jnp.bfloat16)
     for j in range(out_ref.shape[0]):
-        out_ref[j, :tokens, :] = grad_ref[...] if j % 2 else inputs_ref[...]
+        source = grad_ref if j % 2 else inputs_ref
+        at = j // 2 % 2 * part
+        out_ref[j, :part, :] = source[at : at + part, :]
 
 
 def part_kernel(
@@ -129,7 +132,12 @@
 
 def middle_kernel(
     capacity,
-    full_ref,
+    at_ref,
+    own_ref,
+    next_ref,
+    last_ref,
+    left_ref,
+    right_ref,
     routed_pre_ref,
     shared_pre_ref,
     w_ref,
@@ -139,10 +147,23 @@
     shared_back_ref,
     shared_w_ref,
     grad_pre_ref,
+    full_ref,
     sems,
 ):
     shared_in = pltpu.make_async_copy(shared_w_hbm, shared_w_ref, sems.at[0])
     shared_in.start()
+    rows, columns = own_ref.shape
+    middle = columns // 2
+
+    def place(turn, lanes, source_ref):
+        row = pl.multiple_of(lax.rem(at_ref[0] + turn, NEAR) * rows, 8)
+        full_ref[pl.ds(row, rows), lanes] = source_ref[...].astype(jnp.float32)
+
+    place(0, slice(None), own_ref)
+    place(1, slice(None), next_ref)
+    place(NEAR - 1, slice(None), last_ref)
+    place(2, slice(0, middle), left_ref)
+    place(2, slice(middle, columns), right_ref)
     slots = routed_pre_ref.shape[0]
     tokens = shared_pre_ref.shape[0]
     half = full_ref.shape[1]
@@ -155,7 +176,7 @@
             d_gate, d_up, _ = swiglu_terms(
                 routed_pre_ref[r : r + step, c : c + part].astype(jnp.float32),
                 routed_pre_ref[r : r + step, half + c : half + c + part].astype(jnp.float32),
-                full_ref[r : r + step, c : c + part].astype(jnp.float32),
+                full_ref[r : r + step, c : c + part],
             )
             grad_pre_ref[r : r + step, c : c + part] = d_gate.astype(jnp.bfloat16)
             grad_pre_ref[r : r + step, half + c : half + c + part] = d_up.astype(jnp.bfloat16)
@@ -164,7 +185,7 @@
     d_gate, d_up, value = swiglu_terms(
         shared_pre_ref[:, :half].astype(jnp.float32),
         shared_pre_ref[:, half:].astype(jnp.float32),
-        full_ref[slots:, :].astype(jnp.float32),
+        full_ref[slots:, :],
     )
     d_gate, d_up = d_gate.astype(jnp.bfloat16), d_up.astype(jnp.bfloat16)
     value = value.astype(jnp.bfloat16)
@@ -200,31 +221,26 @@
 
 
 def last_kernel(
-    parity_ref,
+    order_ref,
     back_ref,
     sel_ref,
     shared_back_ref,
-    kept_hbm,
-    other_hbm,
+    first_hbm,
+    second_hbm,
+    third_hbm,
+    fourth_hbm,
     grad_in_ref,
     shared_gu_ref,
     shared_dn_ref,
-    inputs_ref,
-    grads_ref,
+    pieces_ref,
     sems,
 ):
-    odd = parity_ref[0] == 1
-
-    @pl.when(odd)
-    def _():
-        pltpu.make_async_copy(other_hbm, inputs_ref, sems.at[0]).start()
-        pltpu.make_async_copy(kept_hbm, grads_ref, sems.at[1]).start()
-
-    @pl.when(jnp.logical_not(odd))
-    def _():
-        pltpu.make_async_copy(kept_hbm, inputs_ref, sems.at[0]).start()
-        pltpu.make_async_copy(other_hbm, grads_ref, sems.at[1]).start()
-
+    copies = [
+        pltpu.make_async_copy(source, pieces_ref.at[i], sems.at[i])
+        for i, source in enumerate((first_hbm, second_hbm, third_hbm, fourth_hbm))
+    ]
+    for copy in copies:
+        copy.start()
     groups = back_ref.shape[0]
     slots, tokens = sel_ref.shape
     gu_cols, width = shared_gu_ref.shape
@@ -237,13 +253,19 @@
     grad_in_ref[:, LANES:] = (
         shared_back[:, LANES:] + dot(sel, high, 0, 0)[:, : width - LANES]
     ).astype(jnp.bfloat16)
-    shared = back_ref[:, :tokens, :].reshape(groups * tokens, LANES)
-    pltpu.make_async_copy(kept_hbm, inputs_ref, sems.at[0]).wait()
-    pltpu.make_async_copy(other_hbm, grads_ref, sems.at[1]).wait()
-    shared_gu_ref[...] = dot(shared, inputs_ref[...], 0, 0)[:gu_cols].astype(jnp.bfloat16)
-    shared_dn_ref[...] = dot(shared, grads_ref[...], 0, 0)[gu_cols : gu_cols + down_cols].astype(
-        jnp.bfloat16
-    )
+    for copy in copies:
+        copy.wait()
+    part = tokens // 2
+    shared_gu = jnp.zeros((LANES, width), jnp.float32)
+    shared_dn = jnp.zeros((LANES, width), jnp.float32)
+    for h in range(2):
+        shared = back_ref[:, h * part : (h + 1) * part, :].reshape(groups * part, LANES)
+        inputs = pieces_ref[order_ref[2 * h]].reshape(groups * part, width)
+        grads = pieces_ref[order_ref[2 * h + 1]].reshape(groups * part, width)
+        shared_gu = shared_gu + dot(shared, inputs, 0, 0)
+        shared_dn = shared_dn + dot(shared, grads, 0, 0)
+    shared_gu_ref[...] = shared_gu[:gu_cols].astype(jnp.bfloat16)
+    shared_dn_ref[...] = shared_dn[gu_cols : gu_cols + down_cols].astype(jnp.bfloat16)
 
 
 def total(parts):
@@ -269,7 +291,6 @@
     groups = lax.axis_size("expert")
     ring = lax.axis_size("dp")
     far = ring // NEAR
-    near_groups = [[NEAR * a + b for b in range(NEAR)] for a in range(far)]
     far_groups = [[NEAR * a + b for a in range(far)] for b in range(NEAR)]
     slots = routed_pre.shape[1]
     capacity = slots // groups
@@ -283,7 +304,7 @@
         lambda *refs: route_kernel(capacity, *refs),
         out_shape=(
             jax.ShapeDtypeStruct((groups * SLOT_ROWS, tokens), jnp.bfloat16),
-            jax.ShapeDtypeStruct((groups, tokens + capacity, width), jnp.bfloat16),
+            jax.ShapeDtypeStruct((groups, tokens // 2 + capacity, width), jnp.bfloat16),
         ),
         in_specs=[pl.BlockSpec(memory_space=pltpu.HBM)] * 4,
         scratch_shapes=[
@@ -297,10 +318,8 @@
         name="route",
     )(*[in_hbm(x) for x in (expert_ids.T, gate_weights.T, grad_out, layer_inputs)])
     incoming = lax.all_to_all(outgoing, "expert", split_axis=0, concat_axis=0, tiled=True)
-    arrived = incoming[:, tokens:].reshape(slots, width)
-    kept = incoming[:, :tokens].reshape(groups * tokens, width)
-    other = lax.ppermute(kept, "expert", [(i, i ^ 1) for i in range(groups)])
-    parity = (lax.axis_index("expert") % 2).reshape(1).astype(jnp.int32)
+    arrived = incoming[:, tokens // 2 :].reshape(slots, width)
+    order = (lax.axis_index("expert") % 4).astype(jnp.int32) ^ jnp.arange(4, dtype=jnp.int32)
 
     rows = (slots + tokens) // NEAR
     cols = hidden_width // far
@@ -330,6 +349,10 @@
         compiler_params=limit,
         name="near",
     )(own, shift(to_next, 1), shift(to_last, -1), shift(to_right, 2), shift(to_left, -2))
+    near, piece = lax.optimization_barrier((near, incoming[:, : tokens // 2]))
+    pieces = [piece]
+    for turn in (1, 2, 3):
+        pieces.append(lax.ppermute(piece, "expert", [(i, i ^ turn) for i in range(groups)]))
     distant = lax.all_to_all(
         near,
         "dp",
@@ -338,9 +361,14 @@
         tiled=True,
         axis_index_groups=far_groups,
     )
-    own = total(distant)
+    own, *pieces = lax.optimization_barrier((total(distant), *pieces))
     full = lax.all_gather(own, "dp", axis=1, tiled=True, axis_index_groups=far_groups)
-    full = lax.all_gather(full, "dp", axis=0, tiled=True, axis_index_groups=near_groups)
+    around = (
+        shift(full, -1),
+        shift(full, 1),
+        shift(full[:, :half], 2),
+        shift(full[:, half:], -2),
+    )
 
     grad_pre, payload, shared_back = pl.pallas_call(
         lambda *refs: middle_kernel(capacity, *refs),
@@ -349,16 +377,19 @@
             jax.ShapeDtypeStruct((groups, tokens + 2 * SLOT_ROWS, LANES), jnp.bfloat16),
             jax.ShapeDtypeStruct((tokens, width), jnp.float32),
         ),
-        in_specs=vmem(4) + [pl.BlockSpec(memory_space=pltpu.HBM)],
+        in_specs=[pl.BlockSpec(memory_space=pltpu.SMEM)]
+        + vmem(8)
+        + [pl.BlockSpec(memory_space=pltpu.HBM)],
         out_specs=[pl.BlockSpec(memory_space=pltpu.HBM)] + vmem(2),
         scratch_shapes=[
             pltpu.VMEM(shared_gate_up.shape, jnp.bfloat16),
             pltpu.VMEM((slots, 2 * hidden_width), jnp.bfloat16),
+            pltpu.VMEM((slots + tokens, hidden_width), jnp.float32),
             pltpu.SemaphoreType.DMA((2,)),
         ],
         compiler_params=limit,
         name="middle",
-    )(full, routed_pre, shared_pre, w_gate_up, in_hbm(shared_gate_up))
+    )(quarter, full, *around, routed_pre, shared_pre, w_gate_up, in_hbm(shared_gate_up))
     back = lax.all_to_all(payload, "expert", split_axis=0, concat_axis=0, tiled=True)
 
     gate = routed_pre[:, :hidden_width].astype(jnp.float32)
@@ -378,15 +409,14 @@
         ),
         in_specs=[pl.BlockSpec(memory_space=pltpu.SMEM)]
         + vmem(3)
-        + [pl.BlockSpec(memory_space=pltpu.HBM)] * 2,
+        + [pl.BlockSpec(memory_space=pltpu.HBM)] * 4,
         scratch_shapes=[
-            pltpu.VMEM(kept.shape, jnp.bfloat16),
-            pltpu.VMEM(kept.shape, jnp.bfloat16),
-            pltpu.SemaphoreType.DMA((2,)),
+            pltpu.VMEM((4, *pieces[0].shape), jnp.bfloat16),
+            pltpu.SemaphoreType.DMA((4,)),
         ],
         compiler_params=limit,
         name="last",
-    )(parity, back, sel, shared_back, in_hbm(kept), in_hbm(other))
+    )(order, back, sel, shared_back, *[in_hbm(piece) for piece in pieces])
     return (
         grad_in,
         grad_gate_up[None],

time: 185 us -> 187 us (1.011)
  starting transfers between devices: 71.6 us -> 90.6 us
  blocking collectives: 48.1 us -> 30.6 us
    ppermute x4 -> x8, starting transfers between devices: 18.5 us -> 36.2 us  [shift(): return lax.ppermute(x, 'dp', [(i, (i + by) % ring) for i in range(ring)])]
    all_gather x1 -> x0, blocking collectives: 17.5 us -> none  [on_device(): lax.all_gather(full, 'dp', axis=0, tiled=True, axis_index_groups=near_gro...]
    ppermute x1 -> x3, starting transfers between devices: 3.42 us -> 8.75 us  [on_device(): lax.ppermute(piece, 'expert', [(i, i ^ turn) for i in range(groups)])]
    ppermute x4 -> x8, waiting for transfers between devices: 2.89 us -> 7.66 us  [shift(): return lax.ppermute(x, 'dp', [(i, (i + by) % ring) for i in range(ring)])]
    all_to_all x1, starting transfers between devices: 16.5 us -> 12.6 us  [on_device(): lax.all_to_all(payload, 'expert', split_axis=0, concat_axis=0, tiled=True)]
    all_to_all x1, waiting for transfers between devices: 24.1 us -> 20.5 us  [on_device(): lax.all_to_all(near, 'dp', split_axis=0, concat_axis=0, tiled=True, axis_...]
    all_to_all x1, waiting for transfers between devices: 14.3 us -> 11.6 us  [on_device(): lax.all_to_all(outgoing, 'expert', split_axis=0, concat_axis=0, tiled=True)]
  transfers between devices with their start and end apart: 8 -> 14, of which waited for: 4 -> 6; matrix products, arithmetic and copies ran while one was open for 3% -> 3% of each run, Pallas kernels for 2% -> 0%
where the time goes in v6:
time: 187 us; the launch traced here: 186 us
  starting transfers between devices  90.6 us (48%)
  waiting for transfers between devices  48.3 us (26%)
  blocking collectives  30.6 us (16%)
  Pallas kernels  9.61 us (5%)
  matrix products  3.07 us (2%)
    ppermute x8, starting transfers between devices, shift(): return lax.ppermute(x, 'dp', [(i, (i + by) % ring) for i in range(ring)])  36.2 us
    all_gather x1, blocking collectives, on_device(): lax.all_gather(own, 'dp', axis=1, tiled=True, axis_index_groups=far_groups)  30.6 us
    all_to_all x1, waiting for transfers between devices, on_device(): lax.all_to_all(near, 'dp', split_axis=0, concat_axis=0, tiled=True, axis_...  20.5 us
    all_to_all x1, starting transfers between devices, on_device(): lax.all_to_all(outgoing, 'expert', split_axis=0, concat_axis=0, tiled=True)  17.7 us
    all_to_all x1, starting transfers between devices, on_device(): lax.all_to_all(near, 'dp', split_axis=0, concat_axis=0, tiled=True, axis_...  15.3 us
    all_to_all x1, starting transfers between devices, on_device(): lax.all_to_all(payload, 'expert', split_axis=0, concat_axis=0, tiled=True)  12.6 us
    all_to_all x1, waiting for transfers between devices, on_device(): lax.all_to_all(outgoing, 'expert', split_axis=0, concat_axis=0, tiled=True)  11.6 us
    ppermute x3, starting transfers between devices, on_device(): lax.ppermute(piece, 'expert', [(i, i ^ turn) for i in range(groups)])  8.75 us
  transfers between devices with their start and end apart: 14, of which 6 were waited for; matrix products, arithmetic and copies ran while one was open for 3% of the time, Pallas kernels for 0%

profile of v6, /device:TPU:1, one launch (start us, length us, event | category | flops | bytes accessed | tf_op | source)
XLA Modules:
  0.0 185.8 jit_solution(4842922869016490886)
XLA Ops:
  0.7 2.3 %route.1 = (bf16[512,32]{1,0:T(8,128)(2,1)S(1)}, bf16[32,28,224]{2,1,0:T(8,128)(2,1)}) custom-call(s32[8,32]{1,0:T(8,128)} %bitcast.28, f32[8,32]{1,0:T(8,128)} %bitcast.29, bf16[32,224]{1,0:T(8,128)(2,1)} %grad_ref.1, bf16[32,224]{1,0:T(8,128)(2,1)} %refs_3_.1), custom_call_target="tpu_custom_call" | custom-call | tf_op jit(solution)/shard_map/route/pallas_call | solution.py:303
  3.0 17.7 %all-to-all-start = ((bf16[32,28,224]{2,1,0:T(8,128)(2,1)}), bf16[32,28,224]{2,1,0:T(8,128)(2,1)S(1)}, u32[]{:S(2)}, u32[]{:S(2)}) async-start(bf16[32,28,224]{2,1,0:T(8,128)(2,1)} %get-tuple-element.25), calls=%async_computation | async-start | bytes 1048576 | tf_op jit(solution)/shard_map/all_to_all | solution.py:320
  20.7 11.6 %all-to-all-done = bf16[32,28,224]{2,1,0:T(8,128)(2,1)S(1)} async-done(((bf16[32,28,224]{2,1,0:T(8,128)(2,1)}), bf16[32,28,224]{2,1,0:T(8,128)(2,1)S(1)}, u32[]{:S(2)}, u32[]{:S(2)}) %all-to-all-start) | async-done | bytes 401440 | tf_op jit(solution)/shard_map/all_to_all | solution.py:320
  32.4 0.1 reshape.32.arrived_ref
  32.5 0.7 copy-done.7
  33.2 0.5 part.1
  33.7 2.1 %collective-permute-start = (bf16[104,1024]{1,0:T(8,128)(2,1)S(1)}, bf16[104,1024]{1,0:T(8,128)(2,1)S(1)}, u32[]{:S(2)}, u32[]{:S(2)}) collective-permute-start(bf16[104,1024]{1,0:T(8,128)(2,1)S(1)} %get-tuple-element.27), channel_id=1, source_target_pairs={{0,1},{1,2},{2,3},{3,4},{4,5},{5,6},{6,7},{7,8},{8,9},{9,10},{10,1... | collective-permute-start | bytes 638984 | tf_op jit(solution)/shard_map/ppermute | solution.py:329
  35.8 9.2 %collective-permute-start.1 = (bf16[104,1024]{1,0:T(8,128)(2,1)S(1)}, bf16[104,1024]{1,0:T(8,128)(2,1)S(1)}, u32[]{:S(2)}, u32[]{:S(2)}) collective-permute-start(bf16[104,1024]{1,0:T(8,128)(2,1)S(1)} %get-tuple-element.28), channel_id=1, source_target_pairs={{0,31},{1,0},{2,1},{3,2},{4,3},{5,4},{6,5},{7,6},{8,7},{9,8},{10,9... | collective-permute-start | bytes 638984 | tf_op jit(solution)/shard_map/ppermute | solution.py:329
  44.9 1.9 %collective-permute-start.2 = (bf16[104,512]{1,0:T(8,128)(2,1)S(1)}, bf16[104,512]{1,0:T(8,128)(2,1)S(1)}, u32[]{:S(2)}, u32[]{:S(2)}) collective-permute-start(bf16[104,512]{1,0:T(8,128)(2,1)S(1)} %get-tuple-element.29), channel_id=1, source_target_pairs={{0,2},{1,3},{2,4},{3,5},{4,6},{5,7},{6,8},{7,9},{8,10},{9,11},{10,... | collective-permute-start | bytes 319496 | tf_op jit(solution)/shard_map/ppermute | solution.py:329
  46.9 5.5 %collective-permute-start.3 = (bf16[104,512]{1,0:T(8,128)(2,1)S(1)}, bf16[104,512]{1,0:T(8,128)(2,1)S(1)}, u32[]{:S(2)}, u32[]{:S(2)}) collective-permute-start(bf16[104,512]{1,0:T(8,128)(2,1)S(1)} %get-tuple-element.30), channel_id=1, source_target_pairs={{0,30},{1,31},{2,0},{3,1},{4,2},{5,3},{6,4},{7,5},{8,6},{9,7},{10,... | collective-permute-start | bytes 319496 | tf_op jit(solution)/shard_map/ppermute | solution.py:329
  52.3 1.0 slice.57.first_hbm
  53.3 1.9 %collective-permute-done.2.ahead_ref = bf16[104,512]{1,0:T(8,128)(2,1)S(1)} collective-permute-done((bf16[104,512]{1,0:T(8,128)(2,1)S(1)}, bf16[104,512]{1,0:T(8,128)(2,1)S(1)}, u32[]{:S(2)}, u32[]{:S(2)}) %collective-permute-start.2) | collective-permute-done | bytes 106528 | tf_op jit(solution)/shard_map/ppermute | solution.py:329
  55.2 0.8 near.1
  56.1 15.3 %all-to-all-start.1 = ((bf16[8,104,128]{2,1,0:T(8,128)(2,1)}), bf16[8,104,128]{2,1,0:T(8,128)(2,1)}, u32[]{:S(2)}, u32[]{:S(2)}) async-start(bf16[8,104,128]{2,1,0:T(8,128)(2,1)} %near.1), calls=%async_computation.1 | async-start | bytes 425984 | tf_op jit(solution)/shard_map/all_to_all | solution.py:356
  71.4 3.3 %collective-permute-start.4 = (bf16[32,16,224]{2,1,0:T(8,128)(2,1)S(1)}, bf16[32,16,224]{2,1,0:T(8,128)(2,1)}, u32[]{:S(2)}, u32[]{:S(2)}) collective-permute-start(bf16[32,16,224]{2,1,0:T(8,128)(2,1)S(1)} %slice.57.first_hbm), channel_id=1, source_target_pairs={{0,32},{32,0},{64,96},{96,64},{128,160},{160,128},{192,224},{224,1... | collective-permute-start | bytes 688136 | tf_op jit(solution)/shard_map/ppermute | solution.py:355
  74.7 2.5 %collective-permute-start.5 = (bf16[32,16,224]{2,1,0:T(8,128)(2,1)S(1)}, bf16[32,16,224]{2,1,0:T(8,128)(2,1)}, u32[]{:S(2)}, u32[]{:S(2)}) collective-permute-start(bf16[32,16,224]{2,1,0:T(8,128)(2,1)S(1)} %slice.57.first_hbm), channel_id=1, source_target_pairs={{0,64},{32,96},{64,0},{96,32},{128,192},{160,224},{192,128},{224,1... | collective-permute-start | bytes 688136 | tf_op jit(solution)/shard_map/ppermute | solution.py:355
  77.2 3.0 %collective-permute-start.6 = (bf16[32,16,224]{2,1,0:T(8,128)(2,1)S(1)}, bf16[32,16,224]{2,1,0:T(8,128)(2,1)}, u32[]{:S(2)}, u32[]{:S(2)}) collective-permute-start(bf16[32,16,224]{2,1,0:T(8,128)(2,1)S(1)} %slice.57.first_hbm), channel_id=1, source_target_pairs={{0,96},{32,64},{64,32},{96,0},{128,224},{160,192},{192,160},{224,1... | collective-permute-start | bytes 688136 | tf_op jit(solution)/shard_map/ppermute | solution.py:355
  80.2 20.5 %all-to-all-done.1 = bf16[8,104,128]{2,1,0:T(8,128)(2,1)} async-done(((bf16[8,104,128]{2,1,0:T(8,128)(2,1)}), bf16[8,104,128]{2,1,0:T(8,128)(2,1)}, u32[]{:S(2)}, u32[]{:S(2)}) %all-to-all-start.1) | async-done | bytes 213024 | tf_op jit(solution)/shard_map/all_to_all | solution.py:356
  100.7 0.9 fusion.9
  101.7 30.6 %all_gather.3.refs_1_ = bf16[104,1024]{1,0:T(8,128)(2,1)S(1)} all-gather(bf16[104,128]{1,0:T(8,128)(2,1)S(1)} %fusion.9), channel_id=1, replica_groups={{0,4,8,12,16,20,24,28},{1,5,9,13,17,21,25,29},{2,6,10,14,18,22,26,30},{..., dimensions={1}, use_global_device_ids=true | all-gather | bytes 239616 | tf_op jit(solution)/shard_map/all_gather | solution.py:365
  132.2 1.9 %collective-permute-start.7 = (bf16[104,1024]{1,0:T(8,128)(2,1)S(1)}, bf16[104,1024]{1,0:T(8,128)(2,1)S(1)}, u32[]{:S(2)}, u32[]{:S(2)}) collective-permute-start(bf16[104,1024]{1,0:T(8,128)(2,1)S(1)} %all_gather.3.refs_1_), channel_id=1, source_target_pairs={{0,31},{1,0},{2,1},{3,2},{4,3},{5,4},{6,5},{7,6},{8,7},{9,8},{10,9... | collective-permute-start | bytes 638984 | tf_op jit(solution)/shard_map/ppermute | solution.py:329
  134.1 3.4 %collective-permute-start.8 = (bf16[104,1024]{1,0:T(8,128)(2,1)S(1)}, bf16[104,1024]{1,0:T(8,128)(2,1)S(1)}, u32[]{:S(2)}, u32[]{:S(2)}) collective-permute-start(bf16[104,1024]{1,0:T(8,128)(2,1)S(1)} %all_gather.3.refs_1_), channel_id=1, source_target_pairs={{0,1},{1,2},{2,3},{3,4},{4,5},{5,6},{6,7},{7,8},{8,9},{9,10},{10,1... | collective-permute-start | bytes 638984 | tf_op jit(solution)/shard_map/ppermute | solution.py:329
  137.5 10.4 %collective-permute-start.9 = (bf16[104,512]{1,0:T(8,128)(2,1)S(1)}, bf16[104,512]{1,0:T(8,128)(2,1)S(1)}, u32[]{:S(2)}, u32[]{:S(2)}) collective-permute-start(bf16[104,512]{1,0:T(8,128)(2,1)S(1)} %get-tuple-element.46), channel_id=1, source_target_pairs={{0,2},{1,3},{2,4},{3,5},{4,6},{5,7},{6,8},{7,9},{8,10},{9,11},{10,... | collective-permute-start | bytes 319496 | tf_op jit(solution)/shard_map/ppermute | solution.py:329
  147.9 1.9 %collective-permute-start.10 = (bf16[104,512]{1,0:T(8,128)(2,1)S(1)}, bf16[104,512]{1,0:T(8,128)(2,1)S(1)}, u32[]{:S(2)}, u32[]{:S(2)}) collective-permute-start(bf16[104,512]{1,0:T(8,128)(2,1)S(1)} %get-tuple-element.45), channel_id=1, source_target_pairs={{0,30},{1,31},{2,0},{3,1},{4,2},{5,3},{6,4},{7,5},{8,6},{9,7},{10,... | collective-permute-start | bytes 319496 | tf_op jit(solution)/shard_map/ppermute | solution.py:329
  149.9 1.6 collective-permute-done.9.refs_4_
  151.4 4.2 %collective-permute-done.10.refs_5_ = bf16[104,512]{1,0:T(8,128)(2,1)S(1)} collective-permute-done((bf16[104,512]{1,0:T(8,128)(2,1)S(1)}, bf16[104,512]{1,0:T(8,128)(2,1)S(1)}, u32[]{:S(2)}, u32[]{:S(2)}) %collective-permute-start.10) | collective-permute-done | bytes 106528 | tf_op jit(solution)/shard_map/ppermute | solution.py:329
  155.6 3.3 %middle.1 = (bf16[384,2048]{1,0:T(8,128)(2,1)}, bf16[32,64,128]{2,1,0:T(8,128)(2,1)}, f32[32,224]{1,0:T(8,128)S(1)}) custom-call(s32[1]{0:T(128)} %bitcast.at_ref.refs_0_, bf16[104,1024]{1,0:T(8,128)(2,1)S(1)} %all_gather.3.refs_1_, bf16[104,1024]{1,0:T(8,128)(2,1)S(1)} %collective-permute-done.7.refs_2_, ...), custom_call_target="tpu_custom_call" | custom-call | tf_op jit(solution)/shard_map/middle/pallas_call | solution.py:373
  159.0 12.6 %all-to-all-start.2 = ((bf16[32,64,128]{2,1,0:T(8,128)(2,1)}), bf16[32,64,128]{2,1,0:T(8,128)(2,1)S(1)}, u32[]{:S(2)}, u32[]{:S(2)}) async-start(bf16[32,64,128]{2,1,0:T(8,128)(2,1)} %get-tuple-element.34), calls=%async_computation.2 | async-start | bytes 1048576 | tf_op jit(solution)/shard_map/all_to_all | solution.py:393
  171.6 1.5 fusion.6
  173.1 1.6 fusion
  174.7 8.5 %all-to-all-done.2.back_ref = bf16[32,64,128]{2,1,0:T(8,128)(2,1)S(1)} async-done(((bf16[32,64,128]{2,1,0:T(8,128)(2,1)}), bf16[32,64,128]{2,1,0:T(8,128)(2,1)S(1)}, u32[]{:S(2)}, u32[]{:S(2)}) %all-to-all-start.2) | async-done | bytes 524320 | tf_op jit(solution)/shard_map/all_to_all | solution.py:393
  183.1 2.7 %last.1 = (bf16[32,224]{1,0:T(8,128)(2,1)}, bf16[64,224]{1,0:T(8,128)(2,1)}, bf16[32,224]{1,0:T(8,128)(2,1)}) custom-call(s32[4]{0:T(128)S(1)} %iota_xor_fusion.order_ref, bf16[32,64,128]{2,1,0:T(8,128)(2,1)S(1)} %all-to-all-done.2.back_ref, bf16[512,32]{1,0:T(8,128)(2,1)S(1)} %get-tuple-element.35.sel_ref, f32[32,224]{1,0:T(8,128)S(1)} %get-tuple-element.36.shared_back_ref, ...), custom_call_target="tpu_custom_call" | custom-call | tf_op jit(solution)/shard_map/last/pallas_call | solution.py:403
  (30 shorter events, 0.1 us)
Async XLA Ops:
  0.6 172.5 %copy-start = (bf16[1,384,224]{1,2,0:T(8,128)(2,1)S(1)}, bf16[1,384,224]{1,2,0:T(8,128)(2,1)}, u32[]{:S(2)}) copy-start(bf16[1,384,224]{1,2,0:T(8,128)(2,1)} %param.16) | copy-start | bytes 516100
  0.6 32.5 %copy-start.6 = (bf16[32,224]{1,0:T(8,128)(2,1)S(1)}, bf16[32,224]{1,0:T(8,128)(2,1)}, u32[]{:S(2)}) copy-start(bf16[32,224]{1,0:T(8,128)(2,1)} %grad_ref.1) | copy-start | bytes 43012
  0.7 32.5 %copy-start.3 = (bf16[1,1024,224]{1,2,0:T(8,128)(2,1)S(1)}, bf16[1,1024,224]{1,2,0:T(8,128)(2,1)}, u32[]{:S(2)}) copy-start(bf16[1,1024,224]{1,2,0:T(8,128)(2,1)} %param.19) | copy-start | bytes 1376260
  0.7 32.5 %copy-start.4 = (bf16[1024,224]{0,1:T(8,128)(2,1)S(1)}, bf16[1024,224]{0,1:T(8,128)(2,1)}, u32[]{:S(2)}) copy-start(bf16[1024,224]{0,1:T(8,128)(2,1)} %param.21) | copy-start | bytes 1376260
  3.0 29.4 %all-to-all-start = ((bf16[32,28,224]{2,1,0:T(8,128)(2,1)}), bf16[32,28,224]{2,1,0:T(8,128)(2,1)S(1)}, u32[]{:S(2)}, u32[]{:S(2)}) async-start(bf16[32,28,224]{2,1,0:T(8,128)(2,1)} %get-tuple-element.25), calls=%async_computation | async-start | bytes 1048576 | tf_op jit(solution)/shard_map/all_to_all | solution.py:320
  32.4 0.8 copy-start.7
  33.7 122.0 %copy-start.1 = (bf16[1,384,2048]{2,1,0:T(8,128)(2,1)S(1)}, bf16[1,384,2048]{2,1,0:T(8,128)(2,1)}, u32[]{:S(2)}) copy-start(bf16[1,384,2048]{2,1,0:T(8,128)(2,1)} %param.17) | copy-start | bytes 4718596
  33.7 121.9 %copy-start.2 = (bf16[1,224,2048]{2,1,0:T(8,128)(2,1)S(1)}, bf16[1,224,2048]{2,1,0:T(8,128)(2,1)}, u32[]{:S(2)}) copy-start(bf16[1,224,2048]{2,1,0:T(8,128)(2,1)} %param.18) | copy-start | bytes 2752516
  33.7 121.9 %copy-start.5 = (bf16[32,2048]{1,0:T(8,128)(2,1)S(1)}, bf16[32,2048]{1,0:T(8,128)(2,1)}, u32[]{:S(2)}) copy-start(bf16[32,2048]{1,0:T(8,128)(2,1)} %refs_7_.1) | copy-start | bytes 393220
  33.7 21.5 %collective-permute-start = (bf16[104,1024]{1,0:T(8,128)(2,1)S(1)}, bf16[104,1024]{1,0:T(8,128)(2,1)S(1)}, u32[]{:S(2)}, u32[]{:S(2)}) collective-permute-start(bf16[104,1024]{1,0:T(8,128)(2,1)S(1)} %get-tuple-element.27), channel_id=1, source_target_pairs={{0,1},{1,2},{2,3},{3,4},{4,5},{5,6},{6,7},{7,8},{8,9},{9,10},{10,1... | collective-permute-start | bytes 638984 | tf_op jit(solution)/shard_map/ppermute | solution.py:329
  35.8 19.5 %collective-permute-start.1 = (bf16[104,1024]{1,0:T(8,128)(2,1)S(1)}, bf16[104,1024]{1,0:T(8,128)(2,1)S(1)}, u32[]{:S(2)}, u32[]{:S(2)}) collective-permute-start(bf16[104,1024]{1,0:T(8,128)(2,1)S(1)} %get-tuple-element.28), channel_id=1, source_target_pairs={{0,31},{1,0},{2,1},{3,2},{4,3},{5,4},{6,5},{7,6},{8,7},{9,8},{10,9... | collective-permute-start | bytes 638984 | tf_op jit(solution)/shard_map/ppermute | solution.py:329
  44.9 10.3 %collective-permute-start.2 = (bf16[104,512]{1,0:T(8,128)(2,1)S(1)}, bf16[104,512]{1,0:T(8,128)(2,1)S(1)}, u32[]{:S(2)}, u32[]{:S(2)}) collective-permute-start(bf16[104,512]{1,0:T(8,128)(2,1)S(1)} %get-tuple-element.29), channel_id=1, source_target_pairs={{0,2},{1,3},{2,4},{3,5},{4,6},{5,7},{6,8},{7,9},{8,10},{9,11},{10,... | collective-permute-start | bytes 319496 | tf_op jit(solution)/shard_map/ppermute | solution.py:329
  46.9 8.4 %collective-permute-start.3 = (bf16[104,512]{1,0:T(8,128)(2,1)S(1)}, bf16[104,512]{1,0:T(8,128)(2,1)S(1)}, u32[]{:S(2)}, u32[]{:S(2)}) collective-permute-start(bf16[104,512]{1,0:T(8,128)(2,1)S(1)} %get-tuple-element.30), channel_id=1, source_target_pairs={{0,30},{1,31},{2,0},{3,1},{4,2},{5,3},{6,4},{7,5},{8,6},{9,7},{10,... | collective-permute-start | bytes 319496 | tf_op jit(solution)/shard_map/ppermute | solution.py:329
  53.3 105.6 %copy-start.9 = (bf16[32,16,224]{2,1,0:T(8,128)(2,1)}, bf16[32,16,224]{2,1,0:T(8,128)(2,1)S(1)}, u32[]{:S(2)}) copy-start(bf16[32,16,224]{2,1,0:T(8,128)(2,1)S(1)} %slice.57.first_hbm) | copy-start | bytes 688132
  56.1 44.7 %all-to-all-start.1 = ((bf16[8,104,128]{2,1,0:T(8,128)(2,1)}), bf16[8,104,128]{2,1,0:T(8,128)(2,1)}, u32[]{:S(2)}, u32[]{:S(2)}) async-start(bf16[8,104,128]{2,1,0:T(8,128)(2,1)} %near.1), calls=%async_computation.1 | async-start | bytes 425984 | tf_op jit(solution)/shard_map/all_to_all | solution.py:356
  71.4 30.2 %collective-permute-start.4 = (bf16[32,16,224]{2,1,0:T(8,128)(2,1)S(1)}, bf16[32,16,224]{2,1,0:T(8,128)(2,1)}, u32[]{:S(2)}, u32[]{:S(2)}) collective-permute-start(bf16[32,16,224]{2,1,0:T(8,128)(2,1)S(1)} %slice.57.first_hbm), channel_id=1, source_target_pairs={{0,32},{32,0},{64,96},{96,64},{128,160},{160,128},{192,224},{224,1... | collective-permute-start | bytes 688136 | tf_op jit(solution)/shard_map/ppermute | solution.py:355
  74.7 26.9 %collective-permute-start.5 = (bf16[32,16,224]{2,1,0:T(8,128)(2,1)S(1)}, bf16[32,16,224]{2,1,0:T(8,128)(2,1)}, u32[]{:S(2)}, u32[]{:S(2)}) collective-permute-start(bf16[32,16,224]{2,1,0:T(8,128)(2,1)S(1)} %slice.57.first_hbm), channel_id=1, source_target_pairs={{0,64},{32,96},{64,0},{96,32},{128,192},{160,224},{192,128},{224,1... | collective-permute-start | bytes 688136 | tf_op jit(solution)/shard_map/ppermute | solution.py:355
  77.2 24.5 %collective-permute-start.6 = (bf16[32,16,224]{2,1,0:T(8,128)(2,1)S(1)}, bf16[32,16,224]{2,1,0:T(8,128)(2,1)}, u32[]{:S(2)}, u32[]{:S(2)}) collective-permute-start(bf16[32,16,224]{2,1,0:T(8,128)(2,1)S(1)} %slice.57.first_hbm), channel_id=1, source_target_pairs={{0,96},{32,64},{64,32},{96,0},{128,224},{160,192},{192,160},{224,1... | collective-permute-start | bytes 688136 | tf_op jit(solution)/shard_map/ppermute | solution.py:355
  132.2 23.4 %collective-permute-start.7 = (bf16[104,1024]{1,0:T(8,128)(2,1)S(1)}, bf16[104,1024]{1,0:T(8,128)(2,1)S(1)}, u32[]{:S(2)}, u32[]{:S(2)}) collective-permute-start(bf16[104,1024]{1,0:T(8,128)(2,1)S(1)} %all_gather.3.refs_1_), channel_id=1, source_target_pairs={{0,31},{1,0},{2,1},{3,2},{4,3},{5,4},{6,5},{7,6},{8,7},{9,8},{10,9... | collective-permute-start | bytes 638984 | tf_op jit(solution)/shard_map/ppermute | solution.py:329
  134.1 21.5 %collective-permute-start.8 = (bf16[104,1024]{1,0:T(8,128)(2,1)S(1)}, bf16[104,1024]{1,0:T(8,128)(2,1)S(1)}, u32[]{:S(2)}, u32[]{:S(2)}) collective-permute-start(bf16[104,1024]{1,0:T(8,128)(2,1)S(1)} %all_gather.3.refs_1_), channel_id=1, source_target_pairs={{0,1},{1,2},{2,3},{3,4},{4,5},{5,6},{6,7},{7,8},{8,9},{9,10},{10,1... | collective-permute-start | bytes 638984 | tf_op jit(solution)/shard_map/ppermute | solution.py:329
  137.5 13.9 %collective-permute-start.9 = (bf16[104,512]{1,0:T(8,128)(2,1)S(1)}, bf16[104,512]{1,0:T(8,128)(2,1)S(1)}, u32[]{:S(2)}, u32[]{:S(2)}) collective-permute-start(bf16[104,512]{1,0:T(8,128)(2,1)S(1)} %get-tuple-element.46), channel_id=1, source_target_pairs={{0,2},{1,3},{2,4},{3,5},{4,6},{5,7},{6,8},{7,9},{8,10},{9,11},{10,... | collective-permute-start | bytes 319496 | tf_op jit(solution)/shard_map/ppermute | solution.py:329
  147.9 7.7 %collective-permute-start.10 = (bf16[104,512]{1,0:T(8,128)(2,1)S(1)}, bf16[104,512]{1,0:T(8,128)(2,1)S(1)}, u32[]{:S(2)}, u32[]{:S(2)}) collective-permute-start(bf16[104,512]{1,0:T(8,128)(2,1)S(1)} %get-tuple-element.45), channel_id=1, source_target_pairs={{0,30},{1,31},{2,0},{3,1},{4,2},{5,3},{6,4},{7,5},{8,6},{9,7},{10,... | collective-permute-start | bytes 319496 | tf_op jit(solution)/shard_map/ppermute | solution.py:329
  159.0 24.2 %all-to-all-start.2 = ((bf16[32,64,128]{2,1,0:T(8,128)(2,1)}), bf16[32,64,128]{2,1,0:T(8,128)(2,1)S(1)}, u32[]{:S(2)}, u32[]{:S(2)}) async-start(bf16[32,64,128]{2,1,0:T(8,128)(2,1)} %get-tuple-element.34), calls=%async_computation.2 | async-start | bytes 1048576 | tf_op jit(solution)/shard_map/all_to_all | solution.py:393
  171.6 1.5 copy-start.8

commit v7 on v6

--- a/solution.py
+++ b/solution.py
@@ -132,12 +132,7 @@
 
 def middle_kernel(
     capacity,
-    at_ref,
-    own_ref,
-    next_ref,
-    last_ref,
-    left_ref,
-    right_ref,
+    full_ref,
     routed_pre_ref,
     shared_pre_ref,
     w_ref,
@@ -147,23 +142,10 @@
     shared_back_ref,
     shared_w_ref,
     grad_pre_ref,
-    full_ref,
     sems,
 ):
     shared_in = pltpu.make_async_copy(shared_w_hbm, shared_w_ref, sems.at[0])
     shared_in.start()
-    rows, columns = own_ref.shape
-    middle = columns // 2
-
-    def place(turn, lanes, source_ref):
-        row = pl.multiple_of(lax.rem(at_ref[0] + turn, NEAR) * rows, 8)
-        full_ref[pl.ds(row, rows), lanes] = source_ref[...].astype(jnp.float32)
-
-    place(0, slice(None), own_ref)
-    place(1, slice(None), next_ref)
-    place(NEAR - 1, slice(None), last_ref)
-    place(2, slice(0, middle), left_ref)
-    place(2, slice(middle, columns), right_ref)
     slots = routed_pre_ref.shape[0]
     tokens = shared_pre_ref.shape[0]
     half = full_ref.shape[1]
@@ -176,7 +158,7 @@
             d_gate, d_up, _ = swiglu_terms(
                 routed_pre_ref[r : r + step, c : c + part].astype(jnp.float32),
                 routed_pre_ref[r : r + step, half + c : half + c + part].astype(jnp.float32),
-                full_ref[r : r + step, c : c + part],
+                full_ref[r : r + step, c : c + part].astype(jnp.float32),
             )
             grad_pre_ref[r : r + step, c : c + part] = d_gate.astype(jnp.bfloat16)
             grad_pre_ref[r : r + step, half + c : half + c + part] = d_up.astype(jnp.bfloat16)
@@ -185,7 +167,7 @@
     d_gate, d_up, value = swiglu_terms(
         shared_pre_ref[:, :half].astype(jnp.float32),
         shared_pre_ref[:, half:].astype(jnp.float32),
-        full_ref[slots:, :],
+        full_ref[slots:, :].astype(jnp.float32),
     )
     d_gate, d_up = d_gate.astype(jnp.bfloat16), d_up.astype(jnp.bfloat16)
     value = value.astype(jnp.bfloat16)
@@ -259,11 +241,11 @@
     shared_gu = jnp.zeros((LANES, width), jnp.float32)
     shared_dn = jnp.zeros((LANES, width), jnp.float32)
     for h in range(2):
-        shared = back_ref[:, h * part : (h + 1) * part, :].reshape(groups * part, LANES)
+        shared = back_ref[:, h * part : (h + 1) * part, :].reshape(groups * part, LANES).T
         inputs = pieces_ref[order_ref[2 * h]].reshape(groups * part, width)
         grads = pieces_ref[order_ref[2 * h + 1]].reshape(groups * part, width)
-        shared_gu = shared_gu + dot(shared, inputs, 0, 0)
-        shared_dn = shared_dn + dot(shared, grads, 0, 0)
+        shared_gu = shared_gu + dot(shared, inputs, 1, 0)
+        shared_dn = shared_dn + dot(shared, grads, 1, 0)
     shared_gu_ref[...] = shared_gu[:gu_cols].astype(jnp.bfloat16)
     shared_dn_ref[...] = shared_dn[gu_cols : gu_cols + down_cols].astype(jnp.bfloat16)
 
@@ -291,6 +273,7 @@
     groups = lax.axis_size("expert")
     ring = lax.axis_size("dp")
     far = ring // NEAR
+    near_groups = [[NEAR * a + b for b in range(NEAR)] for a in range(far)]
     far_groups = [[NEAR * a + b for a in range(far)] for b in range(NEAR)]
     slots = routed_pre.shape[1]
     capacity = slots // groups
@@ -361,14 +344,9 @@
         tiled=True,
         axis_index_groups=far_groups,
     )
-    own, *pieces = lax.optimization_barrier((total(distant), *pieces))
+    own = total(distant)
     full = lax.all_gather(own, "dp", axis=1, tiled=True, axis_index_groups=far_groups)
-    around = (
-        shift(full, -1),
-        shift(full, 1),
-        shift(full[:, :half], 2),
-        shift(full[:, half:], -2),
-    )
+    full = lax.all_gather(full, "dp", axis=0, tiled=True, axis_index_groups=near_groups)
 
     grad_pre, payload, shared_back = pl.pallas_call(
         lambda *refs: middle_kernel(capacity, *refs),
@@ -377,19 +355,16 @@
             jax.ShapeDtypeStruct((groups, tokens + 2 * SLOT_ROWS, LANES), jnp.bfloat16),
             jax.ShapeDtypeStruct((tokens, width), jnp.float32),
         ),
-        in_specs=[pl.BlockSpec(memory_space=pltpu.SMEM)]
-        + vmem(8)
-        + [pl.BlockSpec(memory_space=pltpu.HBM)],
+        in_specs=vmem(4) + [pl.BlockSpec(memory_space=pltpu.HBM)],
         out_specs=[pl.BlockSpec(memory_space=pltpu.HBM)] + vmem(2),
         scratch_shapes=[
             pltpu.VMEM(shared_gate_up.shape, jnp.bfloat16),
             pltpu.VMEM((slots, 2 * hidden_width), jnp.bfloat16),
-            pltpu.VMEM((slots + tokens, hidden_width), jnp.float32),
             pltpu.SemaphoreType.DMA((2,)),
         ],
         compiler_params=limit,
         name="middle",
-    )(quarter, full, *around, routed_pre, shared_pre, w_gate_up, in_hbm(shared_gate_up))
+    )(full, routed_pre, shared_pre, w_gate_up, in_hbm(shared_gate_up))
     back = lax.all_to_all(payload, "expert", split_axis=0, concat_axis=0, tiled=True)
 
     gate = routed_pre[:, :hidden_width].astype(jnp.float32)

time: 187 us -> 184 us (0.984)
  blocking collectives: 30.6 us -> 51.6 us
  starting transfers between devices: 90.6 us -> 73.6 us
  waiting for transfers between devices: 48.3 us -> 43.5 us
    all_gather x0 -> x1, blocking collectives: none -> 21.3 us  [on_device(): lax.all_gather(full, 'dp', axis=0, tiled=True, axis_index_groups=near_gro...]
    ppermute x8 -> x4, starting transfers between devices: 36.2 us -> 18.5 us  [shift(): return lax.ppermute(x, 'dp', [(i, (i + by) % ring) for i in range(ring)])]
    ppermute x8 -> x4, waiting for transfers between devices: 7.66 us -> 2.85 us  [shift(): return lax.ppermute(x, 'dp', [(i, (i + by) % ring) for i in range(ring)])]
  transfers between devices with their start and end apart: 14 -> 10, of which waited for: 6 -> 4; matrix products, arithmetic and copies ran while one was open for 3% -> 2% of each run, Pallas kernels for 0% -> 2%
where the time goes in v7:
time: 184 us; the launch traced here: 183 us
  starting transfers between devices  73.6 us (40%)
  blocking collectives  51.6 us (28%)
  waiting for transfers between devices  43.5 us (24%)
  Pallas kernels  9.61 us (5%)
  matrix products  3.07 us (2%)
    all_gather x1, blocking collectives, on_device(): lax.all_gather(own, 'dp', axis=1, tiled=True, axis_index_groups=far_groups)  30.3 us
    all_gather x1, blocking collectives, on_device(): lax.all_gather(full, 'dp', axis=0, tiled=True, axis_index_groups=near_gro...  21.3 us
    all_to_all x1, waiting for transfers between devices, on_device(): lax.all_to_all(near, 'dp', split_axis=0, concat_axis=0, tiled=True, axis_...  20.5 us
    ppermute x4, starting transfers between devices, shift(): return lax.ppermute(x, 'dp', [(i, (i + by) % ring) for i in range(ring)])  18.5 us
    all_to_all x1, starting transfers between devices, on_device(): lax.all_to_all(outgoing, 'expert', split_axis=0, concat_axis=0, tiled=True)  17.7 us
    all_to_all x1, starting transfers between devices, on_device(): lax.all_to_all(near, 'dp', split_axis=0, concat_axis=0, tiled=True, axis_...  15.3 us
    all_to_all x1, starting transfers between devices, on_device(): lax.all_to_all(payload, 'expert', split_axis=0, concat_axis=0, tiled=True)  13.3 us
    all_to_all x1, waiting for transfers between devices, on_device(): lax.all_to_all(outgoing, 'expert', split_axis=0, concat_axis=0, tiled=True)  11.6 us
  transfers between devices with their start and end apart: 10, of which 4 were waited for; matrix products, arithmetic and copies ran while one was open for 2% of the time, Pallas kernels for 2%

profile of v7, /device:TPU:1, one launch (start us, length us, event | category | flops | bytes accessed | tf_op | source)
XLA Modules:
  0.0 183.3 jit_solution(14348436693852520430)
XLA Ops:
  0.6 0.0 copy-start
  0.7 2.3 %route.1 = (bf16[512,32]{1,0:T(8,128)(2,1)S(1)}, bf16[32,28,224]{2,1,0:T(8,128)(2,1)}) custom-call(s32[8,32]{1,0:T(8,128)} %bitcast.28, f32[8,32]{1,0:T(8,128)} %bitcast.29, bf16[32,224]{1,0:T(8,128)(2,1)} %grad_ref.1, bf16[32,224]{1,0:T(8,128)(2,1)} %refs_3_.1), custom_call_target="tpu_custom_call" | custom-call | tf_op jit(solution)/shard_map/route/pallas_call | solution.py:286
  3.0 17.7 %all-to-all-start = ((bf16[32,28,224]{2,1,0:T(8,128)(2,1)}), bf16[32,28,224]{2,1,0:T(8,128)(2,1)S(1)}, u32[]{:S(2)}, u32[]{:S(2)}) async-start(bf16[32,28,224]{2,1,0:T(8,128)(2,1)} %get-tuple-element.20), calls=%async_computation | async-start | bytes 1048576 | tf_op jit(solution)/shard_map/all_to_all | solution.py:303
  20.7 11.6 %all-to-all-done = bf16[32,28,224]{2,1,0:T(8,128)(2,1)S(1)} async-done(((bf16[32,28,224]{2,1,0:T(8,128)(2,1)}), bf16[32,28,224]{2,1,0:T(8,128)(2,1)S(1)}, u32[]{:S(2)}, u32[]{:S(2)}) %all-to-all-start) | async-done | bytes 401440 | tf_op jit(solution)/shard_map/all_to_all | solution.py:303
  32.4 0.1 reshape.32.arrived_ref
  32.5 0.5 part.1
  33.0 1.9 %collective-permute-start = (bf16[104,1024]{1,0:T(8,128)(2,1)S(1)}, bf16[104,1024]{1,0:T(8,128)(2,1)S(1)}, u32[]{:S(2)}, u32[]{:S(2)}) collective-permute-start(bf16[104,1024]{1,0:T(8,128)(2,1)S(1)} %get-tuple-element.22), channel_id=1, source_target_pairs={{0,1},{1,2},{2,3},{3,4},{4,5},{5,6},{6,7},{7,8},{8,9},{9,10},{10,1... | collective-permute-start | bytes 638984 | tf_op jit(solution)/shard_map/ppermute | solution.py:312
  34.9 9.2 %collective-permute-start.1 = (bf16[104,1024]{1,0:T(8,128)(2,1)S(1)}, bf16[104,1024]{1,0:T(8,128)(2,1)S(1)}, u32[]{:S(2)}, u32[]{:S(2)}) collective-permute-start(bf16[104,1024]{1,0:T(8,128)(2,1)S(1)} %get-tuple-element.23), channel_id=1, source_target_pairs={{0,31},{1,0},{2,1},{3,2},{4,3},{5,4},{6,5},{7,6},{8,7},{9,8},{10,9... | collective-permute-start | bytes 638984 | tf_op jit(solution)/shard_map/ppermute | solution.py:312
  44.1 1.9 %collective-permute-start.2 = (bf16[104,512]{1,0:T(8,128)(2,1)S(1)}, bf16[104,512]{1,0:T(8,128)(2,1)S(1)}, u32[]{:S(2)}, u32[]{:S(2)}) collective-permute-start(bf16[104,512]{1,0:T(8,128)(2,1)S(1)} %get-tuple-element.24), channel_id=1, source_target_pairs={{0,2},{1,3},{2,4},{3,5},{4,6},{5,7},{6,8},{7,9},{8,10},{9,11},{10,... | collective-permute-start | bytes 319496 | tf_op jit(solution)/shard_map/ppermute | solution.py:312
  46.0 5.5 %collective-permute-start.3 = (bf16[104,512]{1,0:T(8,128)(2,1)S(1)}, bf16[104,512]{1,0:T(8,128)(2,1)S(1)}, u32[]{:S(2)}, u32[]{:S(2)}) collective-permute-start(bf16[104,512]{1,0:T(8,128)(2,1)S(1)} %get-tuple-element.25), channel_id=1, source_target_pairs={{0,30},{1,31},{2,0},{3,1},{4,2},{5,3},{6,4},{7,5},{8,6},{9,7},{10,... | collective-permute-start | bytes 319496 | tf_op jit(solution)/shard_map/ppermute | solution.py:312
  51.5 0.0 copy-start.1
  51.6 0.0 copy-start.2
  51.6 0.0 copy-start.5
  51.6 2.8 %collective-permute-done.2.ahead_ref = bf16[104,512]{1,0:T(8,128)(2,1)S(1)} collective-permute-done((bf16[104,512]{1,0:T(8,128)(2,1)S(1)}, bf16[104,512]{1,0:T(8,128)(2,1)S(1)}, u32[]{:S(2)}, u32[]{:S(2)}) %collective-permute-start.2) | collective-permute-done | bytes 106528 | tf_op jit(solution)/shard_map/ppermute | solution.py:312
  54.4 0.0 collective-permute-done.3.behind_ref
  54.4 0.0 collective-permute-done.after_ref
  54.4 0.0 collective-permute-done.1.before_ref
  54.4 0.8 near.1
  55.3 15.3 %all-to-all-start.1 = ((bf16[8,104,128]{2,1,0:T(8,128)(2,1)}), bf16[8,104,128]{2,1,0:T(8,128)(2,1)}, u32[]{:S(2)}, u32[]{:S(2)}) async-start(bf16[8,104,128]{2,1,0:T(8,128)(2,1)} %near.1), calls=%async_computation.1 | async-start | bytes 425984 | tf_op jit(solution)/shard_map/all_to_all | solution.py:339
  70.6 3.3 %collective-permute-start.4 = (bf16[32,16,224]{2,1,0:T(8,128)(2,1)S(1)}, bf16[32,16,224]{2,1,0:T(8,128)(2,1)}, u32[]{:S(2)}, u32[]{:S(2)}) collective-permute-start(bf16[32,16,224]{2,1,0:T(8,128)(2,1)S(1)} %slice.49.first_hbm), channel_id=1, source_target_pairs={{0,32},{32,0},{64,96},{96,64},{128,160},{160,128},{192,224},{224,1... | collective-permute-start | bytes 688136 | tf_op jit(solution)/shard_map/ppermute | solution.py:338
  73.9 2.5 %collective-permute-start.5 = (bf16[32,16,224]{2,1,0:T(8,128)(2,1)S(1)}, bf16[32,16,224]{2,1,0:T(8,128)(2,1)}, u32[]{:S(2)}, u32[]{:S(2)}) collective-permute-start(bf16[32,16,224]{2,1,0:T(8,128)(2,1)S(1)} %slice.49.first_hbm), channel_id=1, source_target_pairs={{0,64},{32,96},{64,0},{96,32},{128,192},{160,224},{192,128},{224,1... | collective-permute-start | bytes 688136 | tf_op jit(solution)/shard_map/ppermute | solution.py:338
  76.4 3.0 %collective-permute-start.6 = (bf16[32,16,224]{2,1,0:T(8,128)(2,1)S(1)}, bf16[32,16,224]{2,1,0:T(8,128)(2,1)}, u32[]{:S(2)}, u32[]{:S(2)}) collective-permute-start(bf16[32,16,224]{2,1,0:T(8,128)(2,1)S(1)} %slice.49.first_hbm), channel_id=1, source_target_pairs={{0,96},{32,64},{64,32},{96,0},{128,224},{160,192},{192,160},{224,1... | collective-permute-start | bytes 688136 | tf_op jit(solution)/shard_map/ppermute | solution.py:338
  79.4 20.5 %all-to-all-done.1 = bf16[8,104,128]{2,1,0:T(8,128)(2,1)} async-done(((bf16[8,104,128]{2,1,0:T(8,128)(2,1)}), bf16[8,104,128]{2,1,0:T(8,128)(2,1)}, u32[]{:S(2)}, u32[]{:S(2)}) %all-to-all-start.1) | async-done | bytes 213024 | tf_op jit(solution)/shard_map/all_to_all | solution.py:339
  99.8 0.9 add_convert_fusion
  100.7 30.3 %all-gather = bf16[1,104,1024]{2,1,0:T(8,128)(2,1)S(1)} all-gather(bf16[1,104,128]{2,1,0:T(8,128)(2,1)S(1)} %add_convert_fusion), channel_id=2, replica_groups={{0,4,8,12,16,20,24,28},{1,5,9,13,17,21,25,29},{2,6,10,14,18,22,26,30},{..., dimensions={2}, use_global_device_ids=true | all-gather | bytes 239616 | tf_op jit(solution)/shard_map/all_gather | solution.py:348
  131.0 21.3 %all-gather.1 = bf16[1,416,1024]{2,1,0:T(8,128)(2,1)S(1)} all-gather(bf16[1,104,1024]{2,1,0:T(8,128)(2,1)S(1)} %all-gather), channel_id=3, replica_groups={{0,1,2,3},{4,5,6,7},{8,9,10,11},{12,13,14,15},{16,17,18,19},{20,21,22,2..., dimensions={1}, use_global_device_ids=true | all-gather | bytes 1064960 | tf_op jit(solution)/shard_map/all_gather | solution.py:349
  152.3 3.3 %middle.1 = (bf16[384,2048]{1,0:T(8,128)(2,1)}, bf16[32,64,128]{2,1,0:T(8,128)(2,1)}, f32[32,224]{1,0:T(8,128)S(1)}) custom-call(bf16[416,1024]{1,0:T(8,128)(2,1)S(1)} %bitcast.22, bf16[384,2048]{1,0:T(8,128)(2,1)S(1)} %bitcast.23, bf16[32,2048]{1,0:T(8,128)(2,1)S(1)} %copy-done.5, bf16[224,2048]{1,0:T(8,128)(2,1)S(1)} %bitcast.25, bf16[224,2048]{1,0:T(8,128)(2,1)} %refs_4_.1), custom_call_target="tpu_custom_call" | custom-call | tf_op jit(solution)/shard_map/middle/pallas_call | solution.py:351
  155.7 13.3 %all-to-all-start.2 = ((bf16[32,64,128]{2,1,0:T(8,128)(2,1)}), bf16[32,64,128]{2,1,0:T(8,128)(2,1)S(1)}, u32[]{:S(2)}, u32[]{:S(2)}) async-start(bf16[32,64,128]{2,1,0:T(8,128)(2,1)} %get-tuple-element.27), calls=%async_computation.2 | async-start | bytes 1048576 | tf_op jit(solution)/shard_map/all_to_all | solution.py:368
  169.0 1.5 fusion.6
  170.5 1.6 fusion
  172.1 8.6 %all-to-all-done.2.back_ref = bf16[32,64,128]{2,1,0:T(8,128)(2,1)S(1)} async-done(((bf16[32,64,128]{2,1,0:T(8,128)(2,1)}), bf16[32,64,128]{2,1,0:T(8,128)(2,1)S(1)}, u32[]{:S(2)}, u32[]{:S(2)}) %all-to-all-start.2) | async-done | bytes 524320 | tf_op jit(solution)/shard_map/all_to_all | solution.py:368
  180.7 2.7 %last.1 = (bf16[32,224]{1,0:T(8,128)(2,1)}, bf16[64,224]{1,0:T(8,128)(2,1)}, bf16[32,224]{1,0:T(8,128)(2,1)}) custom-call(s32[4]{0:T(128)S(1)} %iota_xor_fusion.order_ref, bf16[32,64,128]{2,1,0:T(8,128)(2,1)S(1)} %all-to-all-done.2.back_ref, bf16[512,32]{1,0:T(8,128)(2,1)S(1)} %get-tuple-element.28.sel_ref, f32[32,224]{1,0:T(8,128)S(1)} %get-tuple-element.29.shared_back_ref, ...), custom_call_target="tpu_custom_call" | custom-call | tf_op jit(solution)/shard_map/last/pallas_call | solution.py:378
  (20 shorter events, 0.1 us)
Async XLA Ops:
  0.6 169.9 %copy-start = (bf16[1,384,224]{1,2,0:T(8,128)(2,1)S(1)}, bf16[1,384,224]{1,2,0:T(8,128)(2,1)}, u32[]{:S(2)}) copy-start(bf16[1,384,224]{1,2,0:T(8,128)(2,1)} %param.16) | copy-start | bytes 516100
  0.6 31.8 %copy-start.6 = (bf16[32,224]{1,0:T(8,128)(2,1)S(1)}, bf16[32,224]{1,0:T(8,128)(2,1)}, u32[]{:S(2)}) copy-start(bf16[32,224]{1,0:T(8,128)(2,1)} %grad_ref.1) | copy-start | bytes 43012
  0.7 31.8 %copy-start.3 = (bf16[1,1024,224]{1,2,0:T(8,128)(2,1)S(1)}, bf16[1,1024,224]{1,2,0:T(8,128)(2,1)}, u32[]{:S(2)}) copy-start(bf16[1,1024,224]{1,2,0:T(8,128)(2,1)} %param.19) | copy-start | bytes 1376260
  0.7 31.8 %copy-start.4 = (bf16[1024,224]{0,1:T(8,128)(2,1)S(1)}, bf16[1024,224]{0,1:T(8,128)(2,1)}, u32[]{:S(2)}) copy-start(bf16[1024,224]{0,1:T(8,128)(2,1)} %param.21) | copy-start | bytes 1376260
  3.0 29.4 %all-to-all-start = ((bf16[32,28,224]{2,1,0:T(8,128)(2,1)}), bf16[32,28,224]{2,1,0:T(8,128)(2,1)S(1)}, u32[]{:S(2)}, u32[]{:S(2)}) async-start(bf16[32,28,224]{2,1,0:T(8,128)(2,1)} %get-tuple-element.20), calls=%async_computation | async-start | bytes 1048576 | tf_op jit(solution)/shard_map/all_to_all | solution.py:303
  33.0 21.4 %collective-permute-start = (bf16[104,1024]{1,0:T(8,128)(2,1)S(1)}, bf16[104,1024]{1,0:T(8,128)(2,1)S(1)}, u32[]{:S(2)}, u32[]{:S(2)}) collective-permute-start(bf16[104,1024]{1,0:T(8,128)(2,1)S(1)} %get-tuple-element.22), channel_id=1, source_target_pairs={{0,1},{1,2},{2,3},{3,4},{4,5},{5,6},{6,7},{7,8},{8,9},{9,10},{10,1... | collective-permute-start | bytes 638984 | tf_op jit(solution)/shard_map/ppermute | solution.py:312
  34.9 19.5 %collective-permute-start.1 = (bf16[104,1024]{1,0:T(8,128)(2,1)S(1)}, bf16[104,1024]{1,0:T(8,128)(2,1)S(1)}, u32[]{:S(2)}, u32[]{:S(2)}) collective-permute-start(bf16[104,1024]{1,0:T(8,128)(2,1)S(1)} %get-tuple-element.23), channel_id=1, source_target_pairs={{0,31},{1,0},{2,1},{3,2},{4,3},{5,4},{6,5},{7,6},{8,7},{9,8},{10,9... | collective-permute-start | bytes 638984 | tf_op jit(solution)/shard_map/ppermute | solution.py:312
  44.1 10.3 %collective-permute-start.2 = (bf16[104,512]{1,0:T(8,128)(2,1)S(1)}, bf16[104,512]{1,0:T(8,128)(2,1)S(1)}, u32[]{:S(2)}, u32[]{:S(2)}) collective-permute-start(bf16[104,512]{1,0:T(8,128)(2,1)S(1)} %get-tuple-element.24), channel_id=1, source_target_pairs={{0,2},{1,3},{2,4},{3,5},{4,6},{5,7},{6,8},{7,9},{8,10},{9,11},{10,... | collective-permute-start | bytes 319496 | tf_op jit(solution)/shard_map/ppermute | solution.py:312
  46.0 8.4 %collective-permute-start.3 = (bf16[104,512]{1,0:T(8,128)(2,1)S(1)}, bf16[104,512]{1,0:T(8,128)(2,1)S(1)}, u32[]{:S(2)}, u32[]{:S(2)}) collective-permute-start(bf16[104,512]{1,0:T(8,128)(2,1)S(1)} %get-tuple-element.25), channel_id=1, source_target_pairs={{0,30},{1,31},{2,0},{3,1},{4,2},{5,3},{6,4},{7,5},{8,6},{9,7},{10,... | collective-permute-start | bytes 319496 | tf_op jit(solution)/shard_map/ppermute | solution.py:312
  51.5 104.1 %copy-start.8 = (bf16[32,16,224]{2,1,0:T(8,128)(2,1)}, bf16[32,16,224]{2,1,0:T(8,128)(2,1)S(1)}, u32[]{:S(2)}) copy-start(bf16[32,16,224]{2,1,0:T(8,128)(2,1)S(1)} %slice.49.first_hbm) | copy-start | bytes 688132
  51.5 100.8 %copy-start.1 = (bf16[1,384,2048]{2,1,0:T(8,128)(2,1)S(1)}, bf16[1,384,2048]{2,1,0:T(8,128)(2,1)}, u32[]{:S(2)}) copy-start(bf16[1,384,2048]{2,1,0:T(8,128)(2,1)} %param.17) | copy-start | bytes 4718596
  51.6 100.8 %copy-start.2 = (bf16[1,224,2048]{2,1,0:T(8,128)(2,1)S(1)}, bf16[1,224,2048]{2,1,0:T(8,128)(2,1)}, u32[]{:S(2)}) copy-start(bf16[1,224,2048]{2,1,0:T(8,128)(2,1)} %param.18) | copy-start | bytes 2752516
  51.6 100.8 %copy-start.5 = (bf16[32,2048]{1,0:T(8,128)(2,1)S(1)}, bf16[32,2048]{1,0:T(8,128)(2,1)}, u32[]{:S(2)}) copy-start(bf16[32,2048]{1,0:T(8,128)(2,1)} %refs_2_.3) | copy-start | bytes 393220
  55.3 44.6 %all-to-all-start.1 = ((bf16[8,104,128]{2,1,0:T(8,128)(2,1)}), bf16[8,104,128]{2,1,0:T(8,128)(2,1)}, u32[]{:S(2)}, u32[]{:S(2)}) async-start(bf16[8,104,128]{2,1,0:T(8,128)(2,1)} %near.1), calls=%async_computation.1 | async-start | bytes 425984 | tf_op jit(solution)/shard_map/all_to_all | solution.py:339
  70.6 101.5 %collective-permute-start.4 = (bf16[32,16,224]{2,1,0:T(8,128)(2,1)S(1)}, bf16[32,16,224]{2,1,0:T(8,128)(2,1)}, u32[]{:S(2)}, u32[]{:S(2)}) collective-permute-start(bf16[32,16,224]{2,1,0:T(8,128)(2,1)S(1)} %slice.49.first_hbm), channel_id=1, source_target_pairs={{0,32},{32,0},{64,96},{96,64},{128,160},{160,128},{192,224},{224,1... | collective-permute-start | bytes 688136 | tf_op jit(solution)/shard_map/ppermute | solution.py:338
  73.9 98.2 %collective-permute-start.5 = (bf16[32,16,224]{2,1,0:T(8,128)(2,1)S(1)}, bf16[32,16,224]{2,1,0:T(8,128)(2,1)}, u32[]{:S(2)}, u32[]{:S(2)}) collective-permute-start(bf16[32,16,224]{2,1,0:T(8,128)(2,1)S(1)} %slice.49.first_hbm), channel_id=1, source_target_pairs={{0,64},{32,96},{64,0},{96,32},{128,192},{160,224},{192,128},{224,1... | collective-permute-start | bytes 688136 | tf_op jit(solution)/shard_map/ppermute | solution.py:338
  76.4 95.7 %collective-permute-start.6 = (bf16[32,16,224]{2,1,0:T(8,128)(2,1)S(1)}, bf16[32,16,224]{2,1,0:T(8,128)(2,1)}, u32[]{:S(2)}, u32[]{:S(2)}) collective-permute-start(bf16[32,16,224]{2,1,0:T(8,128)(2,1)S(1)} %slice.49.first_hbm), channel_id=1, source_target_pairs={{0,96},{32,64},{64,32},{96,0},{128,224},{160,192},{192,160},{224,1... | collective-permute-start | bytes 688136 | tf_op jit(solution)/shard_map/ppermute | solution.py:338
  155.7 25.0 %all-to-all-start.2 = ((bf16[32,64,128]{2,1,0:T(8,128)(2,1)}), bf16[32,64,128]{2,1,0:T(8,128)(2,1)S(1)}, u32[]{:S(2)}, u32[]{:S(2)}) async-start(bf16[32,64,128]{2,1,0:T(8,128)(2,1)} %get-tuple-element.27), calls=%async_computation.2 | async-start | bytes 1048576 | tf_op jit(solution)/shard_map/all_to_all | solution.py:368
  169.0 1.5 copy-start.7

commit v8 on v7

--- a/solution.py
+++ b/solution.py
@@ -203,7 +203,7 @@
 
 
 def last_kernel(
-    order_ref,
+    turn_ref,
     back_ref,
     sel_ref,
     shared_back_ref,
@@ -242,8 +242,8 @@
     shared_dn = jnp.zeros((LANES, width), jnp.float32)
     for h in range(2):
         shared = back_ref[:, h * part : (h + 1) * part, :].reshape(groups * part, LANES).T
-        inputs = pieces_ref[order_ref[2 * h]].reshape(groups * part, width)
-        grads = pieces_ref[order_ref[2 * h + 1]].reshape(groups * part, width)
+        inputs = pieces_ref[jnp.bitwise_xor(turn_ref[0], 2 * h)].reshape(groups * part, width)
+        grads = pieces_ref[jnp.bitwise_xor(turn_ref[0], 2 * h + 1)].reshape(groups * part, width)
         shared_gu = shared_gu + dot(shared, inputs, 1, 0)
         shared_dn = shared_dn + dot(shared, grads, 1, 0)
     shared_gu_ref[...] = shared_gu[:gu_cols].astype(jnp.bfloat16)
@@ -302,7 +302,7 @@
     )(*[in_hbm(x) for x in (expert_ids.T, gate_weights.T, grad_out, layer_inputs)])
     incoming = lax.all_to_all(outgoing, "expert", split_axis=0, concat_axis=0, tiled=True)
     arrived = incoming[:, tokens // 2 :].reshape(slots, width)
-    order = (lax.axis_index("expert") % 4).astype(jnp.int32) ^ jnp.arange(4, dtype=jnp.int32)
+    turn_of = (lax.axis_index("expert") % 4).reshape(1).astype(jnp.int32)
 
     rows = (slots + tokens) // NEAR
     cols = hidden_width // far
@@ -391,7 +391,7 @@
         ],
         compiler_params=limit,
         name="last",
-    )(order, back, sel, shared_back, *[in_hbm(piece) for piece in pieces])
+    )(turn_of, back, sel, shared_back, *[in_hbm(piece) for piece in pieces])
     return (
         grad_in,
         grad_gate_up[None],

time: 184 us -> 184 us (level)
  no operation moved by 1% of the time
where the time goes in v8:
time: 184 us; the launch traced here: 183 us
  starting transfers between devices  73.6 us (40%)
  blocking collectives  51.6 us (28%)
  waiting for transfers between devices  43.6 us (24%)
  Pallas kernels  9.1 us (5%)
  matrix products  3.07 us (2%)
    all_gather x1, blocking collectives, on_device(): lax.all_gather(own, 'dp', axis=1, tiled=True, axis_index_groups=far_groups)  30.3 us
    all_gather x1, blocking collectives, on_device(): lax.all_gather(full, 'dp', axis=0, tiled=True, axis_index_groups=near_gro...  21.3 us
    all_to_all x1, waiting for transfers between devices, on_device(): lax.all_to_all(near, 'dp', split_axis=0, concat_axis=0, tiled=True, axis_...  20.5 us
    ppermute x4, starting transfers between devices, shift(): return lax.ppermute(x, 'dp', [(i, (i + by) % ring) for i in range(ring)])  18.5 us
    all_to_all x1, starting transfers between devices, on_device(): lax.all_to_all(outgoing, 'expert', split_axis=0, concat_axis=0, tiled=True)  17.7 us
    all_to_all x1, starting transfers between devices, on_device(): lax.all_to_all(near, 'dp', split_axis=0, concat_axis=0, tiled=True, axis_...  15.3 us
    all_to_all x1, starting transfers between devices, on_device(): lax.all_to_all(payload, 'expert', split_axis=0, concat_axis=0, tiled=True)  13.3 us
    all_to_all x1, waiting for transfers between devices, on_device(): lax.all_to_all(outgoing, 'expert', split_axis=0, concat_axis=0, tiled=True)  11.6 us
  transfers between devices with their start and end apart: 10, of which 4 were waited for; matrix products, arithmetic and copies ran while one was open for 2% of the time, Pallas kernels for 2%

profile of v8, /device:TPU:1, one launch (start us, length us, event | category | flops | bytes accessed | tf_op | source)
XLA Modules:
  0.0 182.8 jit_solution(6735872376873760686)
XLA Ops:
  0.6 0.0 copy-start
  0.7 2.3 %route.1 = (bf16[512,32]{1,0:T(8,128)(2,1)S(1)}, bf16[32,28,224]{2,1,0:T(8,128)(2,1)}) custom-call(s32[8,32]{1,0:T(8,128)} %bitcast.29, f32[8,32]{1,0:T(8,128)} %bitcast.30, bf16[32,224]{1,0:T(8,128)(2,1)} %grad_ref.1, bf16[32,224]{1,0:T(8,128)(2,1)} %refs_3_.1), custom_call_target="tpu_custom_call" | custom-call | tf_op jit(solution)/shard_map/route/pallas_call | solution.py:286
  3.0 17.7 %all-to-all-start = ((bf16[32,28,224]{2,1,0:T(8,128)(2,1)}), bf16[32,28,224]{2,1,0:T(8,128)(2,1)S(1)}, u32[]{:S(2)}, u32[]{:S(2)}) async-start(bf16[32,28,224]{2,1,0:T(8,128)(2,1)} %get-tuple-element.20), calls=%async_computation | async-start | bytes 1048576 | tf_op jit(solution)/shard_map/all_to_all | solution.py:303
  20.7 11.6 %all-to-all-done = bf16[32,28,224]{2,1,0:T(8,128)(2,1)S(1)} async-done(((bf16[32,28,224]{2,1,0:T(8,128)(2,1)}), bf16[32,28,224]{2,1,0:T(8,128)(2,1)S(1)}, u32[]{:S(2)}, u32[]{:S(2)}) %all-to-all-start) | async-done | bytes 401440 | tf_op jit(solution)/shard_map/all_to_all | solution.py:303
  32.4 0.1 reshape.36.arrived_ref
  32.5 0.5 part.1
  33.0 1.9 %collective-permute-start = (bf16[104,1024]{1,0:T(8,128)(2,1)S(1)}, bf16[104,1024]{1,0:T(8,128)(2,1)S(1)}, u32[]{:S(2)}, u32[]{:S(2)}) collective-permute-start(bf16[104,1024]{1,0:T(8,128)(2,1)S(1)} %get-tuple-element.22), channel_id=1, source_target_pairs={{0,1},{1,2},{2,3},{3,4},{4,5},{5,6},{6,7},{7,8},{8,9},{9,10},{10,1... | collective-permute-start | bytes 638984 | tf_op jit(solution)/shard_map/ppermute | solution.py:312
  34.9 9.2 %collective-permute-start.1 = (bf16[104,1024]{1,0:T(8,128)(2,1)S(1)}, bf16[104,1024]{1,0:T(8,128)(2,1)S(1)}, u32[]{:S(2)}, u32[]{:S(2)}) collective-permute-start(bf16[104,1024]{1,0:T(8,128)(2,1)S(1)} %get-tuple-element.23), channel_id=1, source_target_pairs={{0,31},{1,0},{2,1},{3,2},{4,3},{5,4},{6,5},{7,6},{8,7},{9,8},{10,9... | collective-permute-start | bytes 638984 | tf_op jit(solution)/shard_map/ppermute | solution.py:312
  44.1 1.9 %collective-permute-start.2 = (bf16[104,512]{1,0:T(8,128)(2,1)S(1)}, bf16[104,512]{1,0:T(8,128)(2,1)S(1)}, u32[]{:S(2)}, u32[]{:S(2)}) collective-permute-start(bf16[104,512]{1,0:T(8,128)(2,1)S(1)} %get-tuple-element.24), channel_id=1, source_target_pairs={{0,2},{1,3},{2,4},{3,5},{4,6},{5,7},{6,8},{7,9},{8,10},{9,11},{10,... | collective-permute-start | bytes 319496 | tf_op jit(solution)/shard_map/ppermute | solution.py:312
  46.0 5.5 %collective-permute-start.3 = (bf16[104,512]{1,0:T(8,128)(2,1)S(1)}, bf16[104,512]{1,0:T(8,128)(2,1)S(1)}, u32[]{:S(2)}, u32[]{:S(2)}) collective-permute-start(bf16[104,512]{1,0:T(8,128)(2,1)S(1)} %get-tuple-element.25), channel_id=1, source_target_pairs={{0,30},{1,31},{2,0},{3,1},{4,2},{5,3},{6,4},{7,5},{8,6},{9,7},{10,... | collective-permute-start | bytes 319496 | tf_op jit(solution)/shard_map/ppermute | solution.py:312
  51.5 0.0 copy-start.1
  51.6 0.0 copy-start.2
  51.6 0.0 copy-start.5
  51.6 2.8 %collective-permute-done.2.ahead_ref = bf16[104,512]{1,0:T(8,128)(2,1)S(1)} collective-permute-done((bf16[104,512]{1,0:T(8,128)(2,1)S(1)}, bf16[104,512]{1,0:T(8,128)(2,1)S(1)}, u32[]{:S(2)}, u32[]{:S(2)}) %collective-permute-start.2) | collective-permute-done | bytes 106528 | tf_op jit(solution)/shard_map/ppermute | solution.py:312
  54.4 0.0 collective-permute-done.3.behind_ref
  54.4 0.0 collective-permute-done.after_ref
  54.4 0.0 collective-permute-done.1.before_ref
  54.4 0.8 near.1
  55.3 15.3 %all-to-all-start.1 = ((bf16[8,104,128]{2,1,0:T(8,128)(2,1)}), bf16[8,104,128]{2,1,0:T(8,128)(2,1)}, u32[]{:S(2)}, u32[]{:S(2)}) async-start(bf16[8,104,128]{2,1,0:T(8,128)(2,1)} %near.1), calls=%async_computation.1 | async-start | bytes 425984 | tf_op jit(solution)/shard_map/all_to_all | solution.py:339
  70.6 3.3 %collective-permute-start.4 = (bf16[32,16,224]{2,1,0:T(8,128)(2,1)S(1)}, bf16[32,16,224]{2,1,0:T(8,128)(2,1)}, u32[]{:S(2)}, u32[]{:S(2)}) collective-permute-start(bf16[32,16,224]{2,1,0:T(8,128)(2,1)S(1)} %slice.49.first_hbm), channel_id=1, source_target_pairs={{0,32},{32,0},{64,96},{96,64},{128,160},{160,128},{192,224},{224,1... | collective-permute-start | bytes 688136 | tf_op jit(solution)/shard_map/ppermute | solution.py:338
  73.9 2.5 %collective-permute-start.5 = (bf16[32,16,224]{2,1,0:T(8,128)(2,1)S(1)}, bf16[32,16,224]{2,1,0:T(8,128)(2,1)}, u32[]{:S(2)}, u32[]{:S(2)}) collective-permute-start(bf16[32,16,224]{2,1,0:T(8,128)(2,1)S(1)} %slice.49.first_hbm), channel_id=1, source_target_pairs={{0,64},{32,96},{64,0},{96,32},{128,192},{160,224},{192,128},{224,1... | collective-permute-start | bytes 688136 | tf_op jit(solution)/shard_map/ppermute | solution.py:338
  76.3 3.0 %collective-permute-start.6 = (bf16[32,16,224]{2,1,0:T(8,128)(2,1)S(1)}, bf16[32,16,224]{2,1,0:T(8,128)(2,1)}, u32[]{:S(2)}, u32[]{:S(2)}) collective-permute-start(bf16[32,16,224]{2,1,0:T(8,128)(2,1)S(1)} %slice.49.first_hbm), channel_id=1, source_target_pairs={{0,96},{32,64},{64,32},{96,0},{128,224},{160,192},{192,160},{224,1... | collective-permute-start | bytes 688136 | tf_op jit(solution)/shard_map/ppermute | solution.py:338
  79.4 20.5 %all-to-all-done.1 = bf16[8,104,128]{2,1,0:T(8,128)(2,1)} async-done(((bf16[8,104,128]{2,1,0:T(8,128)(2,1)}), bf16[8,104,128]{2,1,0:T(8,128)(2,1)}, u32[]{:S(2)}, u32[]{:S(2)}) %all-to-all-start.1) | async-done | bytes 213024 | tf_op jit(solution)/shard_map/all_to_all | solution.py:339
  99.8 0.9 add_convert_fusion
  100.7 30.3 %all-gather = bf16[1,104,1024]{2,1,0:T(8,128)(2,1)S(1)} all-gather(bf16[1,104,128]{2,1,0:T(8,128)(2,1)S(1)} %add_convert_fusion), channel_id=2, replica_groups={{0,4,8,12,16,20,24,28},{1,5,9,13,17,21,25,29},{2,6,10,14,18,22,26,30},{..., dimensions={2}, use_global_device_ids=true | all-gather | bytes 239616 | tf_op jit(solution)/shard_map/all_gather | solution.py:348
  131.0 21.3 %all-gather.1 = bf16[1,416,1024]{2,1,0:T(8,128)(2,1)S(1)} all-gather(bf16[1,104,1024]{2,1,0:T(8,128)(2,1)S(1)} %all-gather), channel_id=3, replica_groups={{0,1,2,3},{4,5,6,7},{8,9,10,11},{12,13,14,15},{16,17,18,19},{20,21,22,2..., dimensions={1}, use_global_device_ids=true | all-gather | bytes 1064960 | tf_op jit(solution)/shard_map/all_gather | solution.py:349
  152.3 3.3 %middle.1 = (bf16[384,2048]{1,0:T(8,128)(2,1)}, bf16[32,64,128]{2,1,0:T(8,128)(2,1)}, f32[32,224]{1,0:T(8,128)S(1)}) custom-call(bf16[416,1024]{1,0:T(8,128)(2,1)S(1)} %bitcast.23, bf16[384,2048]{1,0:T(8,128)(2,1)S(1)} %bitcast.24, bf16[32,2048]{1,0:T(8,128)(2,1)S(1)} %copy-done.5, bf16[224,2048]{1,0:T(8,128)(2,1)S(1)} %bitcast.26, bf16[224,2048]{1,0:T(8,128)(2,1)} %refs_4_.1), custom_call_target="tpu_custom_call" | custom-call | tf_op jit(solution)/shard_map/middle/pallas_call | solution.py:351
  155.7 13.3 %all-to-all-start.2 = ((bf16[32,64,128]{2,1,0:T(8,128)(2,1)}), bf16[32,64,128]{2,1,0:T(8,128)(2,1)S(1)}, u32[]{:S(2)}, u32[]{:S(2)}) async-start(bf16[32,64,128]{2,1,0:T(8,128)(2,1)} %get-tuple-element.27), calls=%async_computation.2 | async-start | bytes 1048576 | tf_op jit(solution)/shard_map/all_to_all | solution.py:368
  169.0 1.5 fusion.6
  170.5 1.6 fusion
  172.1 8.6 %all-to-all-done.2.back_ref = bf16[32,64,128]{2,1,0:T(8,128)(2,1)S(1)} async-done(((bf16[32,64,128]{2,1,0:T(8,128)(2,1)}), bf16[32,64,128]{2,1,0:T(8,128)(2,1)S(1)}, u32[]{:S(2)}, u32[]{:S(2)}) %all-to-all-start.2) | async-done | bytes 524320 | tf_op jit(solution)/shard_map/all_to_all | solution.py:368
  180.7 2.2 %last.1 = (bf16[32,224]{1,0:T(8,128)(2,1)}, bf16[64,224]{1,0:T(8,128)(2,1)}, bf16[32,224]{1,0:T(8,128)(2,1)}) custom-call(s32[1]{0:T(128)} %bitcast.turn_ref, bf16[32,64,128]{2,1,0:T(8,128)(2,1)S(1)} %all-to-all-done.2.back_ref, bf16[512,32]{1,0:T(8,128)(2,1)S(1)} %get-tuple-element.28.sel_ref, f32[32,224]{1,0:T(8,128)S(1)} %get-tuple-element.29.shared_back_ref, ...), custom_call_target="tpu_custom_call" | custom-call | tf_op jit(solution)/shard_map/last/pallas_call | solution.py:378
  (19 shorter events, 0.1 us)
Async XLA Ops:
  0.6 169.9 %copy-start = (bf16[1,384,224]{1,2,0:T(8,128)(2,1)S(1)}, bf16[1,384,224]{1,2,0:T(8,128)(2,1)}, u32[]{:S(2)}) copy-start(bf16[1,384,224]{1,2,0:T(8,128)(2,1)} %param.16) | copy-start | bytes 516100
  0.6 31.8 %copy-start.6 = (bf16[32,224]{1,0:T(8,128)(2,1)S(1)}, bf16[32,224]{1,0:T(8,128)(2,1)}, u32[]{:S(2)}) copy-start(bf16[32,224]{1,0:T(8,128)(2,1)} %grad_ref.1) | copy-start | bytes 43012
  0.7 31.8 %copy-start.3 = (bf16[1,1024,224]{1,2,0:T(8,128)(2,1)S(1)}, bf16[1,1024,224]{1,2,0:T(8,128)(2,1)}, u32[]{:S(2)}) copy-start(bf16[1,1024,224]{1,2,0:T(8,128)(2,1)} %param.19) | copy-start | bytes 1376260
  0.7 31.8 %copy-start.4 = (bf16[1024,224]{0,1:T(8,128)(2,1)S(1)}, bf16[1024,224]{0,1:T(8,128)(2,1)}, u32[]{:S(2)}) copy-start(bf16[1024,224]{0,1:T(8,128)(2,1)} %param.21) | copy-start | bytes 1376260
  3.0 29.4 %all-to-all-start = ((bf16[32,28,224]{2,1,0:T(8,128)(2,1)}), bf16[32,28,224]{2,1,0:T(8,128)(2,1)S(1)}, u32[]{:S(2)}, u32[]{:S(2)}) async-start(bf16[32,28,224]{2,1,0:T(8,128)(2,1)} %get-tuple-element.20), calls=%async_computation | async-start | bytes 1048576 | tf_op jit(solution)/shard_map/all_to_all | solution.py:303
  33.0 21.4 %collective-permute-start = (bf16[104,1024]{1,0:T(8,128)(2,1)S(1)}, bf16[104,1024]{1,0:T(8,128)(2,1)S(1)}, u32[]{:S(2)}, u32[]{:S(2)}) collective-permute-start(bf16[104,1024]{1,0:T(8,128)(2,1)S(1)} %get-tuple-element.22), channel_id=1, source_target_pairs={{0,1},{1,2},{2,3},{3,4},{4,5},{5,6},{6,7},{7,8},{8,9},{9,10},{10,1... | collective-permute-start | bytes 638984 | tf_op jit(solution)/shard_map/ppermute | solution.py:312
  34.9 19.5 %collective-permute-start.1 = (bf16[104,1024]{1,0:T(8,128)(2,1)S(1)}, bf16[104,1024]{1,0:T(8,128)(2,1)S(1)}, u32[]{:S(2)}, u32[]{:S(2)}) collective-permute-start(bf16[104,1024]{1,0:T(8,128)(2,1)S(1)} %get-tuple-element.23), channel_id=1, source_target_pairs={{0,31},{1,0},{2,1},{3,2},{4,3},{5,4},{6,5},{7,6},{8,7},{9,8},{10,9... | collective-permute-start | bytes 638984 | tf_op jit(solution)/shard_map/ppermute | solution.py:312
  44.1 10.3 %collective-permute-start.2 = (bf16[104,512]{1,0:T(8,128)(2,1)S(1)}, bf16[104,512]{1,0:T(8,128)(2,1)S(1)}, u32[]{:S(2)}, u32[]{:S(2)}) collective-permute-start(bf16[104,512]{1,0:T(8,128)(2,1)S(1)} %get-tuple-element.24), channel_id=1, source_target_pairs={{0,2},{1,3},{2,4},{3,5},{4,6},{5,7},{6,8},{7,9},{8,10},{9,11},{10,... | collective-permute-start | bytes 319496 | tf_op jit(solution)/shard_map/ppermute | solution.py:312
  46.0 8.4 %collective-permute-start.3 = (bf16[104,512]{1,0:T(8,128)(2,1)S(1)}, bf16[104,512]{1,0:T(8,128)(2,1)S(1)}, u32[]{:S(2)}, u32[]{:S(2)}) collective-permute-start(bf16[104,512]{1,0:T(8,128)(2,1)S(1)} %get-tuple-element.25), channel_id=1, source_target_pairs={{0,30},{1,31},{2,0},{3,1},{4,2},{5,3},{6,4},{7,5},{8,6},{9,7},{10,... | collective-permute-start | bytes 319496 | tf_op jit(solution)/shard_map/ppermute | solution.py:312
  51.5 104.1 %copy-start.8 = (bf16[32,16,224]{2,1,0:T(8,128)(2,1)}, bf16[32,16,224]{2,1,0:T(8,128)(2,1)S(1)}, u32[]{:S(2)}) copy-start(bf16[32,16,224]{2,1,0:T(8,128)(2,1)S(1)} %slice.49.first_hbm) | copy-start | bytes 688132
  51.5 100.8 %copy-start.1 = (bf16[1,384,2048]{2,1,0:T(8,128)(2,1)S(1)}, bf16[1,384,2048]{2,1,0:T(8,128)(2,1)}, u32[]{:S(2)}) copy-start(bf16[1,384,2048]{2,1,0:T(8,128)(2,1)} %param.17) | copy-start | bytes 4718596
  51.6 100.8 %copy-start.2 = (bf16[1,224,2048]{2,1,0:T(8,128)(2,1)S(1)}, bf16[1,224,2048]{2,1,0:T(8,128)(2,1)}, u32[]{:S(2)}) copy-start(bf16[1,224,2048]{2,1,0:T(8,128)(2,1)} %param.18) | copy-start | bytes 2752516
  51.6 100.8 %copy-start.5 = (bf16[32,2048]{1,0:T(8,128)(2,1)S(1)}, bf16[32,2048]{1,0:T(8,128)(2,1)}, u32[]{:S(2)}) copy-start(bf16[32,2048]{1,0:T(8,128)(2,1)} %refs_2_.3) | copy-start | bytes 393220
  55.3 44.6 %all-to-all-start.1 = ((bf16[8,104,128]{2,1,0:T(8,128)(2,1)}), bf16[8,104,128]{2,1,0:T(8,128)(2,1)}, u32[]{:S(2)}, u32[]{:S(2)}) async-start(bf16[8,104,128]{2,1,0:T(8,128)(2,1)} %near.1), calls=%async_computation.1 | async-start | bytes 425984 | tf_op jit(solution)/shard_map/all_to_all | solution.py:339
  70.6 101.5 %collective-permute-start.4 = (bf16[32,16,224]{2,1,0:T(8,128)(2,1)S(1)}, bf16[32,16,224]{2,1,0:T(8,128)(2,1)}, u32[]{:S(2)}, u32[]{:S(2)}) collective-permute-start(bf16[32,16,224]{2,1,0:T(8,128)(2,1)S(1)} %slice.49.first_hbm), channel_id=1, source_target_pairs={{0,32},{32,0},{64,96},{96,64},{128,160},{160,128},{192,224},{224,1... | collective-permute-start | bytes 688136 | tf_op jit(solution)/shard_map/ppermute | solution.py:338
  73.9 98.2 %collective-permute-start.5 = (bf16[32,16,224]{2,1,0:T(8,128)(2,1)S(1)}, bf16[32,16,224]{2,1,0:T(8,128)(2,1)}, u32[]{:S(2)}, u32[]{:S(2)}) collective-permute-start(bf16[32,16,224]{2,1,0:T(8,128)(2,1)S(1)} %slice.49.first_hbm), channel_id=1, source_target_pairs={{0,64},{32,96},{64,0},{96,32},{128,192},{160,224},{192,128},{224,1... | collective-permute-start | bytes 688136 | tf_op jit(solution)/shard_map/ppermute | solution.py:338
  76.3 95.8 %collective-permute-start.6 = (bf16[32,16,224]{2,1,0:T(8,128)(2,1)S(1)}, bf16[32,16,224]{2,1,0:T(8,128)(2,1)}, u32[]{:S(2)}, u32[]{:S(2)}) collective-permute-start(bf16[32,16,224]{2,1,0:T(8,128)(2,1)S(1)} %slice.49.first_hbm), channel_id=1, source_target_pairs={{0,96},{32,64},{64,32},{96,0},{128,224},{160,192},{192,160},{224,1... | collective-permute-start | bytes 688136 | tf_op jit(solution)/shard_map/ppermute | solution.py:338
  155.7 25.0 %all-to-all-start.2 = ((bf16[32,64,128]{2,1,0:T(8,128)(2,1)}), bf16[32,64,128]{2,1,0:T(8,128)(2,1)S(1)}, u32[]{:S(2)}, u32[]{:S(2)}) async-start(bf16[32,64,128]{2,1,0:T(8,128)(2,1)} %get-tuple-element.27), calls=%async_computation.2 | async-start | bytes 1048576 | tf_op jit(solution)/shard_map/all_to_all | solution.py:368
  169.0 1.5 copy-start.7

commit v9 on v8

--- a/solution.py
+++ b/solution.py
@@ -131,11 +131,11 @@
 
 
 def middle_kernel(
-    capacity,
     full_ref,
     routed_pre_ref,
     shared_pre_ref,
     w_ref,
+    spread_ref,
     shared_w_hbm,
     grad_pre_hbm,
     payload_ref,
@@ -186,13 +186,7 @@
     used = gu_cols + down_cols
     payload_ref[:, :tokens, used:] = jnp.zeros((groups, tokens, LANES - used), jnp.bfloat16)
     returned = dot(grad_pre_ref[...], w_ref[...], 1, 1).astype(jnp.bfloat16)
-    row = lax.broadcasted_iota(jnp.int32, (groups * SLOT_ROWS, slots), 0)
-    col = lax.broadcasted_iota(jnp.int32, (groups * SLOT_ROWS, slots), 1)
-    expert = row // SLOT_ROWS
-    place = row - expert * SLOT_ROWS
-    wanted = jnp.where(place < capacity, expert * capacity + place, -1)
-    spread = jnp.where(wanted == col, 1.0, 0.0).astype(jnp.bfloat16)
-    spaced = dot(spread, returned, 1, 0).astype(jnp.bfloat16)
+    spaced = dot(spread_ref[...], returned, 1, 0).astype(jnp.bfloat16)
     spaced = spaced.reshape(groups, SLOT_ROWS, width)
     payload_ref[:, tokens : tokens + SLOT_ROWS, :] = spaced[:, :, :LANES]
     payload_ref[:, tokens + SLOT_ROWS :, : width - LANES] = spaced[:, :, LANES:]
@@ -332,7 +326,12 @@
         compiler_params=limit,
         name="near",
     )(own, shift(to_next, 1), shift(to_last, -1), shift(to_right, 2), shift(to_left, -2))
-    near, piece = lax.optimization_barrier((near, incoming[:, : tokens // 2]))
+    place = jnp.arange(groups * SLOT_ROWS, dtype=jnp.int32)
+    place = jnp.where(
+        place % SLOT_ROWS < capacity, place // SLOT_ROWS * capacity + place % SLOT_ROWS, -1
+    )
+    near, piece, place = lax.optimization_barrier((near, incoming[:, : tokens // 2], place))
+    spread = (place[:, None] == jnp.arange(slots, dtype=jnp.int32)[None]).astype(jnp.bfloat16)
     pieces = [piece]
     for turn in (1, 2, 3):
         pieces.append(lax.ppermute(piece, "expert", [(i, i ^ turn) for i in range(groups)]))
@@ -349,14 +348,14 @@
     full = lax.all_gather(full, "dp", axis=0, tiled=True, axis_index_groups=near_groups)
 
     grad_pre, payload, shared_back = pl.pallas_call(
-        lambda *refs: middle_kernel(capacity, *refs),
+        middle_kernel,
         out_shape=(
             pltpu.HBM((slots, 2 * hidden_width), jnp.bfloat16),
-            jax.ShapeDtypeStruct((groups, tokens + 2 * SLOT_ROWS, LANES), jnp.bfloat16),
+            pltpu.HBM((groups, tokens + 2 * SLOT_ROWS, LANES), jnp.bfloat16),
             jax.ShapeDtypeStruct((tokens, width), jnp.float32),
         ),
-        in_specs=vmem(4) + [pl.BlockSpec(memory_space=pltpu.HBM)],
-        out_specs=[pl.BlockSpec(memory_space=pltpu.HBM)] + vmem(2),
+        in_specs=vmem(5) + [pl.BlockSpec(memory_space=pltpu.HBM)],
+        out_specs=[pl.BlockSpec(memory_space=pltpu.HBM), pl.BlockSpec(), *vmem(1)],
         scratch_shapes=[
             pltpu.VMEM(shared_gate_up.shape, jnp.bfloat16),
             pltpu.VMEM((slots, 2 * hidden_width), jnp.bfloat16),
@@ -364,7 +363,7 @@
         ],
         compiler_params=limit,
         name="middle",
-    )(full, routed_pre, shared_pre, w_gate_up, in_hbm(shared_gate_up))
+    )(full, routed_pre, shared_pre, w_gate_up, spread, in_hbm(shared_gate_up))
     back = lax.all_to_all(payload, "expert", split_axis=0, concat_axis=0, tiled=True)
 
     gate = routed_pre[:, :hidden_width].astype(jnp.float32)

time: 184 us -> 184 us (level)
  transfers between devices with their start and end apart: 10 -> 10, of which waited for: 4 -> 4; matrix products, arithmetic and copies ran while one was open for 2% -> 3% of each run, Pallas kernels for 2% -> 2%
where the time goes in v9:
time: 184 us; the launch traced here: 183 us
  starting transfers between devices  73.8 us (40%)
  blocking collectives  51.6 us (28%)
  waiting for transfers between devices  42.7 us (23%)
  Pallas kernels  9.12 us (5%)
  matrix products  3.07 us (2%)
    all_gather x1, blocking collectives, on_device(): lax.all_gather(own, 'dp', axis=1, tiled=True, axis_index_groups=far_groups)  30.3 us
    all_gather x1, blocking collectives, on_device(): lax.all_gather(full, 'dp', axis=0, tiled=True, axis_index_groups=near_gro...  21.3 us
    all_to_all x1, waiting for transfers between devices, on_device(): lax.all_to_all(near, 'dp', split_axis=0, concat_axis=0, tiled=True, axis_...  20.3 us
    ppermute x4, starting transfers between devices, shift(): return lax.ppermute(x, 'dp', [(i, (i + by) % ring) for i in range(ring)])  18.5 us
    all_to_all x1, starting transfers between devices, on_device(): lax.all_to_all(outgoing, 'expert', split_axis=0, concat_axis=0, tiled=True)  17.7 us
    all_to_all x1, starting transfers between devices, on_device(): lax.all_to_all(near, 'dp', split_axis=0, concat_axis=0, tiled=True, axis_...  15.4 us
    all_to_all x1, starting transfers between devices, on_device(): lax.all_to_all(payload, 'expert', split_axis=0, concat_axis=0, tiled=True)  13.4 us
    all_to_all x1, waiting for transfers between devices, on_device(): lax.all_to_all(outgoing, 'expert', split_axis=0, concat_axis=0, tiled=True)  11.6 us
  transfers between devices with their start and end apart: 10, of which 4 were waited for; matrix products, arithmetic and copies ran while one was open for 3% of the time, Pallas kernels for 2%

profile of v9, /device:TPU:1, one launch (start us, length us, event | category | flops | bytes accessed | tf_op | source)
XLA Modules:
  0.0 183.0 jit_solution(6079040343953241372)
XLA Ops:
  0.6 0.0 copy-start
  0.7 2.3 %route.1 = (bf16[512,32]{1,0:T(8,128)(2,1)S(1)}, bf16[32,28,224]{2,1,0:T(8,128)(2,1)}) custom-call(s32[8,32]{1,0:T(8,128)} %bitcast.29, f32[8,32]{1,0:T(8,128)} %bitcast.30, bf16[32,224]{1,0:T(8,128)(2,1)} %grad_ref.1, bf16[32,224]{1,0:T(8,128)(2,1)} %refs_3_.1), custom_call_target="tpu_custom_call" | custom-call | tf_op jit(solution)/shard_map/route/pallas_call | solution.py:280
  3.0 17.7 %all-to-all-start = ((bf16[32,28,224]{2,1,0:T(8,128)(2,1)}), bf16[32,28,224]{2,1,0:T(8,128)(2,1)S(1)}, u32[]{:S(2)}, u32[]{:S(2)}) async-start(bf16[32,28,224]{2,1,0:T(8,128)(2,1)} %get-tuple-element.21), calls=%async_computation | async-start | bytes 1048576 | tf_op jit(solution)/shard_map/all_to_all | solution.py:297
  20.7 11.6 %all-to-all-done = bf16[32,28,224]{2,1,0:T(8,128)(2,1)S(1)} async-done(((bf16[32,28,224]{2,1,0:T(8,128)(2,1)}), bf16[32,28,224]{2,1,0:T(8,128)(2,1)S(1)}, u32[]{:S(2)}, u32[]{:S(2)}) %all-to-all-start) | async-done | bytes 401440 | tf_op jit(solution)/shard_map/all_to_all | solution.py:297
  32.4 0.1 reshape.37.arrived_ref
  32.5 0.5 part.1
  33.0 1.9 %collective-permute-start = (bf16[104,1024]{1,0:T(8,128)(2,1)S(1)}, bf16[104,1024]{1,0:T(8,128)(2,1)S(1)}, u32[]{:S(2)}, u32[]{:S(2)}) collective-permute-start(bf16[104,1024]{1,0:T(8,128)(2,1)S(1)} %get-tuple-element.23), channel_id=1, source_target_pairs={{0,1},{1,2},{2,3},{3,4},{4,5},{5,6},{6,7},{7,8},{8,9},{9,10},{10,1... | collective-permute-start | bytes 638984 | tf_op jit(solution)/shard_map/ppermute | solution.py:306
  34.9 9.2 %collective-permute-start.1 = (bf16[104,1024]{1,0:T(8,128)(2,1)S(1)}, bf16[104,1024]{1,0:T(8,128)(2,1)S(1)}, u32[]{:S(2)}, u32[]{:S(2)}) collective-permute-start(bf16[104,1024]{1,0:T(8,128)(2,1)S(1)} %get-tuple-element.24), channel_id=1, source_target_pairs={{0,31},{1,0},{2,1},{3,2},{4,3},{5,4},{6,5},{7,6},{8,7},{9,8},{10,9... | collective-permute-start | bytes 638984 | tf_op jit(solution)/shard_map/ppermute | solution.py:306
  44.1 1.9 %collective-permute-start.2 = (bf16[104,512]{1,0:T(8,128)(2,1)S(1)}, bf16[104,512]{1,0:T(8,128)(2,1)S(1)}, u32[]{:S(2)}, u32[]{:S(2)}) collective-permute-start(bf16[104,512]{1,0:T(8,128)(2,1)S(1)} %get-tuple-element.25), channel_id=1, source_target_pairs={{0,2},{1,3},{2,4},{3,5},{4,6},{5,7},{6,8},{7,9},{8,10},{9,11},{10,... | collective-permute-start | bytes 319496 | tf_op jit(solution)/shard_map/ppermute | solution.py:306
  46.0 5.5 %collective-permute-start.3 = (bf16[104,512]{1,0:T(8,128)(2,1)S(1)}, bf16[104,512]{1,0:T(8,128)(2,1)S(1)}, u32[]{:S(2)}, u32[]{:S(2)}) collective-permute-start(bf16[104,512]{1,0:T(8,128)(2,1)S(1)} %get-tuple-element.26), channel_id=1, source_target_pairs={{0,30},{1,31},{2,0},{3,1},{4,2},{5,3},{6,4},{7,5},{8,6},{9,7},{10,... | collective-permute-start | bytes 319496 | tf_op jit(solution)/shard_map/ppermute | solution.py:306
  51.5 0.7 slice.49.first_hbm
  52.2 2.2 %collective-permute-done.2.ahead_ref = bf16[104,512]{1,0:T(8,128)(2,1)S(1)} collective-permute-done((bf16[104,512]{1,0:T(8,128)(2,1)S(1)}, bf16[104,512]{1,0:T(8,128)(2,1)S(1)}, u32[]{:S(2)}, u32[]{:S(2)}) %collective-permute-start.2) | collective-permute-done | bytes 106528 | tf_op jit(solution)/shard_map/ppermute | solution.py:306
  54.4 0.0 collective-permute-done.after_ref
  54.4 0.0 copy-start.1
  54.5 0.0 copy-start.2
  54.5 0.0 copy-start.5
  54.5 0.8 near.1
  55.3 15.4 %all-to-all-start.1 = ((bf16[8,104,128]{2,1,0:T(8,128)(2,1)}), bf16[8,104,128]{2,1,0:T(8,128)(2,1)}, u32[]{:S(2)}, u32[]{:S(2)}) async-start(bf16[8,104,128]{2,1,0:T(8,128)(2,1)} %near.1), calls=%async_computation.1 | async-start | bytes 425984 | tf_op jit(solution)/shard_map/all_to_all | solution.py:338
  70.7 3.3 %collective-permute-start.4 = (bf16[32,16,224]{2,1,0:T(8,128)(2,1)}, bf16[32,16,224]{2,1,0:T(8,128)(2,1)}, u32[]{:S(2)}, u32[]{:S(2)}) collective-permute-start(bf16[32,16,224]{2,1,0:T(8,128)(2,1)} %slice.49.first_hbm), channel_id=1, source_target_pairs={{0,32},{32,0},{64,96},{96,64},{128,160},{160,128},{192,224},{224,1... | collective-permute-start | bytes 688136 | tf_op jit(solution)/shard_map/ppermute | solution.py:337
  74.0 2.5 %collective-permute-start.5 = (bf16[32,16,224]{2,1,0:T(8,128)(2,1)}, bf16[32,16,224]{2,1,0:T(8,128)(2,1)}, u32[]{:S(2)}, u32[]{:S(2)}) collective-permute-start(bf16[32,16,224]{2,1,0:T(8,128)(2,1)} %slice.49.first_hbm), channel_id=1, source_target_pairs={{0,64},{32,96},{64,0},{96,32},{128,192},{160,224},{192,128},{224,1... | collective-permute-start | bytes 688136 | tf_op jit(solution)/shard_map/ppermute | solution.py:337
  76.5 3.0 %collective-permute-start.6 = (bf16[32,16,224]{2,1,0:T(8,128)(2,1)}, bf16[32,16,224]{2,1,0:T(8,128)(2,1)}, u32[]{:S(2)}, u32[]{:S(2)}) collective-permute-start(bf16[32,16,224]{2,1,0:T(8,128)(2,1)} %slice.49.first_hbm), channel_id=1, source_target_pairs={{0,96},{32,64},{64,32},{96,0},{128,224},{160,192},{192,160},{224,1... | collective-permute-start | bytes 688136 | tf_op jit(solution)/shard_map/ppermute | solution.py:337
  79.5 0.1 fusion.8.spread_ref
  79.7 20.3 %all-to-all-done.1 = bf16[8,104,128]{2,1,0:T(8,128)(2,1)} async-done(((bf16[8,104,128]{2,1,0:T(8,128)(2,1)}), bf16[8,104,128]{2,1,0:T(8,128)(2,1)}, u32[]{:S(2)}, u32[]{:S(2)}) %all-to-all-start.1) | async-done | bytes 213024 | tf_op jit(solution)/shard_map/all_to_all | solution.py:338
  100.0 0.9 add_convert_fusion
  100.9 30.3 %all-gather = bf16[1,104,1024]{2,1,0:T(8,128)(2,1)S(1)} all-gather(bf16[1,104,128]{2,1,0:T(8,128)(2,1)S(1)} %add_convert_fusion), channel_id=2, replica_groups={{0,4,8,12,16,20,24,28},{1,5,9,13,17,21,25,29},{2,6,10,14,18,22,26,30},{..., dimensions={2}, use_global_device_ids=true | all-gather | bytes 239616 | tf_op jit(solution)/shard_map/all_gather | solution.py:347
  131.2 21.3 %all-gather.1 = bf16[1,416,1024]{2,1,0:T(8,128)(2,1)S(1)} all-gather(bf16[1,104,1024]{2,1,0:T(8,128)(2,1)S(1)} %all-gather), channel_id=3, replica_groups={{0,1,2,3},{4,5,6,7},{8,9,10,11},{12,13,14,15},{16,17,18,19},{20,21,22,2..., dimensions={1}, use_global_device_ids=true | all-gather | bytes 1064960 | tf_op jit(solution)/shard_map/all_gather | solution.py:348
  152.5 3.3 %middle.1 = (bf16[384,2048]{1,0:T(8,128)(2,1)}, bf16[32,64,128]{2,1,0:T(8,128)(2,1)}, f32[32,224]{1,0:T(8,128)S(1)}) custom-call(bf16[416,1024]{1,0:T(8,128)(2,1)S(1)} %bitcast.23, bf16[384,2048]{1,0:T(8,128)(2,1)S(1)} %bitcast.24, bf16[32,2048]{1,0:T(8,128)(2,1)S(1)} %copy-done.5, bf16[224,2048]{1,0:T(8,128)(2,1)S(1)} %bitcast.26, ...), custom_call_target="tpu_custom_call" | custom-call | tf_op jit(solution)/shard_map/middle/pallas_call | solution.py:350
  155.8 13.4 %all-to-all-start.2 = ((bf16[32,64,128]{2,1,0:T(8,128)(2,1)}), bf16[32,64,128]{2,1,0:T(8,128)(2,1)S(1)}, u32[]{:S(2)}, u32[]{:S(2)}) async-start(bf16[32,64,128]{2,1,0:T(8,128)(2,1)} %get-tuple-element.29), calls=%async_computation.2 | async-start | bytes 1048576 | tf_op jit(solution)/shard_map/all_to_all | solution.py:367
  169.3 1.5 fusion.6
  170.8 1.6 fusion
  172.3 8.5 %all-to-all-done.2.back_ref = bf16[32,64,128]{2,1,0:T(8,128)(2,1)S(1)} async-done(((bf16[32,64,128]{2,1,0:T(8,128)(2,1)}), bf16[32,64,128]{2,1,0:T(8,128)(2,1)S(1)}, u32[]{:S(2)}, u32[]{:S(2)}) %all-to-all-start.2) | async-done | bytes 524320 | tf_op jit(solution)/shard_map/all_to_all | solution.py:367
  180.8 2.2 %last.1 = (bf16[32,224]{1,0:T(8,128)(2,1)}, bf16[64,224]{1,0:T(8,128)(2,1)}, bf16[32,224]{1,0:T(8,128)(2,1)}) custom-call(s32[1]{0:T(128)} %bitcast.turn_ref, bf16[32,64,128]{2,1,0:T(8,128)(2,1)S(1)} %all-to-all-done.2.back_ref, bf16[512,32]{1,0:T(8,128)(2,1)S(1)} %get-tuple-element.30.sel_ref, f32[32,224]{1,0:T(8,128)S(1)} %get-tuple-element.31.shared_back_ref, ...), custom_call_target="tpu_custom_call" | custom-call | tf_op jit(solution)/shard_map/last/pallas_call | solution.py:377
  (19 shorter events, 0.1 us)
Async XLA Ops:
  0.6 170.1 %copy-start = (bf16[1,384,224]{1,2,0:T(8,128)(2,1)S(1)}, bf16[1,384,224]{1,2,0:T(8,128)(2,1)}, u32[]{:S(2)}) copy-start(bf16[1,384,224]{1,2,0:T(8,128)(2,1)} %param.16) | copy-start | bytes 516100
  0.6 31.8 %copy-start.6 = (bf16[32,224]{1,0:T(8,128)(2,1)S(1)}, bf16[32,224]{1,0:T(8,128)(2,1)}, u32[]{:S(2)}) copy-start(bf16[32,224]{1,0:T(8,128)(2,1)} %grad_ref.1) | copy-start | bytes 43012
  0.7 31.8 %copy-start.3 = (bf16[1,1024,224]{1,2,0:T(8,128)(2,1)S(1)}, bf16[1,1024,224]{1,2,0:T(8,128)(2,1)}, u32[]{:S(2)}) copy-start(bf16[1,1024,224]{1,2,0:T(8,128)(2,1)} %param.19) | copy-start | bytes 1376260
  0.7 31.8 %copy-start.4 = (bf16[1024,224]{0,1:T(8,128)(2,1)S(1)}, bf16[1024,224]{0,1:T(8,128)(2,1)}, u32[]{:S(2)}) copy-start(bf16[1024,224]{0,1:T(8,128)(2,1)} %param.21) | copy-start | bytes 1376260
  3.0 29.4 %all-to-all-start = ((bf16[32,28,224]{2,1,0:T(8,128)(2,1)}), bf16[32,28,224]{2,1,0:T(8,128)(2,1)S(1)}, u32[]{:S(2)}, u32[]{:S(2)}) async-start(bf16[32,28,224]{2,1,0:T(8,128)(2,1)} %get-tuple-element.21), calls=%async_computation | async-start | bytes 1048576 | tf_op jit(solution)/shard_map/all_to_all | solution.py:297
  33.0 21.4 %collective-permute-start = (bf16[104,1024]{1,0:T(8,128)(2,1)S(1)}, bf16[104,1024]{1,0:T(8,128)(2,1)S(1)}, u32[]{:S(2)}, u32[]{:S(2)}) collective-permute-start(bf16[104,1024]{1,0:T(8,128)(2,1)S(1)} %get-tuple-element.23), channel_id=1, source_target_pairs={{0,1},{1,2},{2,3},{3,4},{4,5},{5,6},{6,7},{7,8},{8,9},{9,10},{10,1... | collective-permute-start | bytes 638984 | tf_op jit(solution)/shard_map/ppermute | solution.py:306
  34.9 19.5 %collective-permute-start.1 = (bf16[104,1024]{1,0:T(8,128)(2,1)S(1)}, bf16[104,1024]{1,0:T(8,128)(2,1)S(1)}, u32[]{:S(2)}, u32[]{:S(2)}) collective-permute-start(bf16[104,1024]{1,0:T(8,128)(2,1)S(1)} %get-tuple-element.24), channel_id=1, source_target_pairs={{0,31},{1,0},{2,1},{3,2},{4,3},{5,4},{6,5},{7,6},{8,7},{9,8},{10,9... | collective-permute-start | bytes 638984 | tf_op jit(solution)/shard_map/ppermute | solution.py:306
  44.1 10.3 %collective-permute-start.2 = (bf16[104,512]{1,0:T(8,128)(2,1)S(1)}, bf16[104,512]{1,0:T(8,128)(2,1)S(1)}, u32[]{:S(2)}, u32[]{:S(2)}) collective-permute-start(bf16[104,512]{1,0:T(8,128)(2,1)S(1)} %get-tuple-element.25), channel_id=1, source_target_pairs={{0,2},{1,3},{2,4},{3,5},{4,6},{5,7},{6,8},{7,9},{8,10},{9,11},{10,... | collective-permute-start | bytes 319496 | tf_op jit(solution)/shard_map/ppermute | solution.py:306
  46.0 8.4 %collective-permute-start.3 = (bf16[104,512]{1,0:T(8,128)(2,1)S(1)}, bf16[104,512]{1,0:T(8,128)(2,1)S(1)}, u32[]{:S(2)}, u32[]{:S(2)}) collective-permute-start(bf16[104,512]{1,0:T(8,128)(2,1)S(1)} %get-tuple-element.26), channel_id=1, source_target_pairs={{0,30},{1,31},{2,0},{3,1},{4,2},{5,3},{6,4},{7,5},{8,6},{9,7},{10,... | collective-permute-start | bytes 319496 | tf_op jit(solution)/shard_map/ppermute | solution.py:306
  54.4 98.1 %copy-start.1 = (bf16[1,384,2048]{2,1,0:T(8,128)(2,1)S(1)}, bf16[1,384,2048]{2,1,0:T(8,128)(2,1)}, u32[]{:S(2)}) copy-start(bf16[1,384,2048]{2,1,0:T(8,128)(2,1)} %param.17) | copy-start | bytes 4718596
  54.5 98.0 %copy-start.2 = (bf16[1,224,2048]{2,1,0:T(8,128)(2,1)S(1)}, bf16[1,224,2048]{2,1,0:T(8,128)(2,1)}, u32[]{:S(2)}) copy-start(bf16[1,224,2048]{2,1,0:T(8,128)(2,1)} %param.18) | copy-start | bytes 2752516
  54.5 98.0 %copy-start.5 = (bf16[32,2048]{1,0:T(8,128)(2,1)S(1)}, bf16[32,2048]{1,0:T(8,128)(2,1)}, u32[]{:S(2)}) copy-start(bf16[32,2048]{1,0:T(8,128)(2,1)} %shared_pre_ref.1) | copy-start | bytes 393220
  55.3 44.7 %all-to-all-start.1 = ((bf16[8,104,128]{2,1,0:T(8,128)(2,1)}), bf16[8,104,128]{2,1,0:T(8,128)(2,1)}, u32[]{:S(2)}, u32[]{:S(2)}) async-start(bf16[8,104,128]{2,1,0:T(8,128)(2,1)} %near.1), calls=%async_computation.1 | async-start | bytes 425984 | tf_op jit(solution)/shard_map/all_to_all | solution.py:338
  70.7 101.6 %collective-permute-start.4 = (bf16[32,16,224]{2,1,0:T(8,128)(2,1)}, bf16[32,16,224]{2,1,0:T(8,128)(2,1)}, u32[]{:S(2)}, u32[]{:S(2)}) collective-permute-start(bf16[32,16,224]{2,1,0:T(8,128)(2,1)} %slice.49.first_hbm), channel_id=1, source_target_pairs={{0,32},{32,0},{64,96},{96,64},{128,160},{160,128},{192,224},{224,1... | collective-permute-start | bytes 688136 | tf_op jit(solution)/shard_map/ppermute | solution.py:337
  74.0 98.3 %collective-permute-start.5 = (bf16[32,16,224]{2,1,0:T(8,128)(2,1)}, bf16[32,16,224]{2,1,0:T(8,128)(2,1)}, u32[]{:S(2)}, u32[]{:S(2)}) collective-permute-start(bf16[32,16,224]{2,1,0:T(8,128)(2,1)} %slice.49.first_hbm), channel_id=1, source_target_pairs={{0,64},{32,96},{64,0},{96,32},{128,192},{160,224},{192,128},{224,1... | collective-permute-start | bytes 688136 | tf_op jit(solution)/shard_map/ppermute | solution.py:337
  76.5 95.8 %collective-permute-start.6 = (bf16[32,16,224]{2,1,0:T(8,128)(2,1)}, bf16[32,16,224]{2,1,0:T(8,128)(2,1)}, u32[]{:S(2)}, u32[]{:S(2)}) collective-permute-start(bf16[32,16,224]{2,1,0:T(8,128)(2,1)} %slice.49.first_hbm), channel_id=1, source_target_pairs={{0,96},{32,64},{64,32},{96,0},{128,224},{160,192},{192,160},{224,1... | collective-permute-start | bytes 688136 | tf_op jit(solution)/shard_map/ppermute | solution.py:337
  155.8 25.0 %all-to-all-start.2 = ((bf16[32,64,128]{2,1,0:T(8,128)(2,1)}), bf16[32,64,128]{2,1,0:T(8,128)(2,1)S(1)}, u32[]{:S(2)}, u32[]{:S(2)}) async-start(bf16[32,64,128]{2,1,0:T(8,128)(2,1)} %get-tuple-element.29), calls=%async_computation.2 | async-start | bytes 1048576 | tf_op jit(solution)/shard_map/all_to_all | solution.py:367
  169.2 1.5 copy-start.7
